TPU v7x, 32 devices: a whole 2x2x4 slice. The times are simulated.
32 devices in a mesh: sens: 4 (over y, x), par: 8 (over z, core).
Axes of the slice: x: 2, y: 2, z: 4, core: 2. Of those that a mesh axis runs over, the one named last changes fastest.
Arguments:
- records: float32 [16, 600, 224], P(None, 'sens'), may hold values from -6 to 6
- spec_real: float32 [225, 600, 1024], P(None, 'sens', 'par'), may hold values from -0.125 to 0.125
- spec_imag: float32 [225, 600, 1024], P(None, 'sens', 'par'), may hold values from -0.125 to 0.125
- prior_cov: float32 [224, 224], replicated, as said below
- sensor_map: int32 [600], replicated, may hold values from 0 to 599, each once
- inverse_rows: float32 [384, 224, 600], P('sens', 'par'), may hold values from -0.015625 to 0.015625
Outputs:
- update: float32 [16, 384], P('par', 'sens')
Inputs may be any that keep to these rules, and one draw needn't show every extreme that they name: prior_cov is symmetric. sensor_map names every sensor once.
All inputs are finite; a program needn't handle non-finite values.
Results may differ from a plain program's by a relative error of at most 0.00013.
Values sent between devices are 32-bit elements; how exact they have to be, the bound alone decides.
No kernel may reach another device: no remote copies, remote signals or barrier semaphores. Data moves between devices by JAX's collectives and lax.ppermute only.
A program may use at most 128 MiB of HBM per device.

v0:
```python
import math

import jax
import jax.numpy as jnp
from jax import lax
from jax.sharding import PartitionSpec as P

highest = lax.Precision.HIGHEST


def spectrum_tables(num_steps, length):
    sample = jnp.arange(num_steps, dtype=jnp.int32)[:, None]
    frequency = jnp.arange(num_steps + 1, dtype=jnp.int32)[None, :]
    phases = (sample * frequency % length).astype(jnp.float32) * (2.0 * math.pi / length)
    return (jnp.cos(phases), -jnp.sin(phases))


def inverse_tables(sample_index, num_steps, length):
    frequency = jnp.arange(num_steps + 1, dtype=jnp.int32)[:, None]
    phases = (frequency * sample_index[None, :] % length).astype(jnp.float32) * (
        2.0 * math.pi / length
    )
    edge_bins = (frequency == 0) | (frequency == num_steps)
    weights = jnp.where(edge_bins, 1.0, 2.0).astype(jnp.float32) / length
    return (weights * jnp.cos(phases), -weights * jnp.sin(phases))


def to_spectrum(signal, cosine, minus_sine):
    part_real = jnp.dot(signal, cosine, precision=highest, preferred_element_type=jnp.float32)
    part_imag = jnp.dot(signal, minus_sine, precision=highest, preferred_element_type=jnp.float32)
    return (part_real, part_imag)


def to_times(part_real, part_imag, cosine, minus_sine):
    first_term = jnp.dot(part_real, cosine, precision=highest, preferred_element_type=jnp.float32)
    return first_term + jnp.dot(
        part_imag, minus_sine, precision=highest, preferred_element_type=jnp.float32
    )


def shards(records, spec_real, spec_imag, prior_cov, sensor_map, inverse_rows):
    num_steps = records.shape[2]
    length = 2 * num_steps
    cols_all = records.shape[0]
    sens_dev = spec_real.shape[1]
    block_steps = num_steps // lax.axis_size("par")
    fwd_cos, fwd_sin = spectrum_tables(num_steps, length)
    inv_cos, inv_sin = inverse_tables(jnp.arange(num_steps, dtype=jnp.int32), num_steps, length)
    prior_cos = jnp.dot(prior_cov, fwd_cos, precision=highest, preferred_element_type=jnp.float32)
    prior_sin = jnp.dot(prior_cov, fwd_sin, precision=highest, preferred_element_type=jnp.float32)
    rec_real, rec_imag = to_spectrum(records, fwd_cos, fwd_sin)
    adj_real = jnp.einsum(
        "csw,wsp->cpw", rec_real, spec_real, precision=highest, preferred_element_type=jnp.float32
    )
    adj_real = adj_real + jnp.einsum(
        "csw,wsp->cpw", rec_imag, spec_imag, precision=highest, preferred_element_type=jnp.float32
    )
    adj_imag = jnp.einsum(
        "csw,wsp->cpw", rec_imag, spec_real, precision=highest, preferred_element_type=jnp.float32
    )
    adj_imag = adj_imag - jnp.einsum(
        "csw,wsp->cpw", rec_real, spec_imag, precision=highest, preferred_element_type=jnp.float32
    )
    partial_adj = to_times(adj_real, adj_imag, inv_cos, inv_sin)
    adjoint = lax.psum(partial_adj, "sens")
    field_real, field_imag = to_spectrum(adjoint, prior_cos, prior_sin)
    pred_real = jnp.einsum(
        "cpw,wsp->csw", field_real, spec_real, precision=highest, preferred_element_type=jnp.float32
    )
    pred_real = pred_real - jnp.einsum(
        "cpw,wsp->csw", field_imag, spec_imag, precision=highest, preferred_element_type=jnp.float32
    )
    pred_imag = jnp.einsum(
        "cpw,wsp->csw", field_imag, spec_real, precision=highest, preferred_element_type=jnp.float32
    )
    pred_imag = pred_imag + jnp.einsum(
        "cpw,wsp->csw", field_real, spec_imag, precision=highest, preferred_element_type=jnp.float32
    )
    partial_pred = jnp.einsum(
        "csw,wt->cts", pred_real, inv_cos, precision=highest, preferred_element_type=jnp.float32
    )
    partial_pred = partial_pred + jnp.einsum(
        "csw,wt->cts", pred_imag, inv_sin, precision=highest, preferred_element_type=jnp.float32
    )
    partial_flat = partial_pred.reshape(cols_all, num_steps * sens_dev)
    predicted = lax.psum_scatter(partial_flat, "par", scatter_dimension=1, tiled=True)
    gathered = lax.all_gather(predicted, "sens", axis=1, tiled=True)
    step_index = jnp.arange(block_steps, dtype=jnp.int32)[:, None]
    pick_index = (
        (sensor_map // sens_dev)[None, :] * (block_steps * sens_dev)
        + step_index * sens_dev
        + (sensor_map % sens_dev)[None, :]
    )
    permuted = jnp.take(gathered, pick_index, axis=1)
    flat_data = permuted.reshape(cols_all, -1)
    flat_rows = inverse_rows.reshape(inverse_rows.shape[0], -1)
    partial_update = jnp.einsum(
        "ck,rk->cr", flat_data, flat_rows, precision=highest, preferred_element_type=jnp.float32
    )
    return lax.psum_scatter(partial_update, "par", scatter_dimension=0, tiled=True)


def solution(mesh):
    return jax.shard_map(
        shards,
        mesh=mesh,
        in_specs=(
            P(None, "sens", None),
            P(None, "sens", "par"),
            P(None, "sens", "par"),
            P(),
            P(),
            P("sens", "par", None),
        ),
        out_specs=P("par", "sens"),
        check_vma=False,
    )
```

profile of v0, /device:TPU:0, one launch (start us, length us, event | category | flops | bytes accessed | tf_op | source)
XLA Modules:
  0.0 497.6 jit_solution(14384187256340989680)
XLA Ops:
  6.5 0.0 copy-start
  6.5 0.0 all-reduce.5.cloned.1.call-start
  6.5 1.7 copy-done
  8.2 5.6 %fusion.15 = f32[16,150,225]{2,1,0:T(8,128)} fusion(f32[16,150,224]{2,0,1:T(8,128)S(1)} %copy-done), kind=kOutput, calls=%fused_computation.19 | convolution fusion | flops 1452024064 | bytes 4310400 | tf_op jit(solution)/shard_map/dot_general | solution.py:30
  13.8 5.6 %fusion.12 = f32[16,150,225]{2,1,0:T(8,128)} fusion(f32[16,150,224]{2,0,1:T(8,128)S(1)} %copy-done), kind=kOutput, calls=%fused_computation.18 | convolution fusion | flops 1451973632 | bytes 4310400 | tf_op jit(solution)/shard_map/dot_general | solution.py:29
  19.5 4.3 copy.18
  23.8 4.1 copy.16
  27.9 18.4 %fusion.117 = f32[225,16,128]{2,1,0:T(8,128)S(1)} fusion(f32[16,150,225]{1,0,2:T(8,128)} %copy.18, f32[225,150,128]{2,1,0:T(8,128)} %param.7), kind=kOutput, calls=%fused_computation.123 | convolution fusion | flops 829440000 | bytes 21283200 | tf_op jit(solution)/shard_map/csw,wsp->cpw/dot_general | solution.py:58
  46.3 0.0 copy-done.3
  46.4 0.0 slice-start.3
  46.4 0.0 slice-start.4
  46.4 18.1 %fusion.116 = f32[225,16,128]{2,1,0:T(8,128)S(1)} fusion(f32[16,150,225]{1,0,2:T(8,128)S(1)} %copy-done.3, f32[225,150,128]{2,1,0:T(8,128)} %param.7), kind=kOutput, calls=%fused_computation.122 | convolution fusion | flops 829440000 | bytes 21283200 | tf_op jit(solution)/shard_map/csw,wsp->cpw/dot_general | solution.py:52
  64.5 0.0 slice-done
  64.5 0.0 slice-done.1
  64.5 0.0 slice-done.2
  64.6 0.0 slice-done.3
  64.6 0.0 slice-done.4
  64.6 0.0 copy-start.2
  64.6 15.9 %subtract_bitcast_fusion.1 = f32[16,128,225]{1,0,2:T(8,128)S(1)} fusion(f32[225,16,128]{2,1,0:T(8,128)S(1)} %fusion.117, f32[16,150,225]{1,0,2:T(8,128)S(1)} %copy-done.3, f32[225,150,128]{2,1,0:T(8,128)S(1)} %bitcast.74), kind=kOutput, calls=%fused_computation.16 | convolution fusion | flops 829900800 | bytes 23126400 | tf_op jit(solution)/shard_map/csw,wsp->cpw/dot_general | solution.py:61
  80.5 0.0 copy-done.2
  80.5 15.7 %add_bitcast_fusion.2 = f32[16,128,225]{1,0,2:T(8,128)S(1)} fusion(f32[225,16,128]{2,1,0:T(8,128)S(1)} %fusion.116, f32[16,150,225]{1,0,2:T(8,128)S(1)} %copy-done.2, f32[225,150,128]{2,1,0:T(8,128)S(1)} %bitcast.74), kind=kOutput, calls=%fused_computation.17 | convolution fusion | flops 829900800 | bytes 23126400 | tf_op jit(solution)/shard_map/csw,wsp->cpw/dot_general | solution.py:55
  96.2 3.0 fusion.8
  99.3 0.0 copy-start.6
  99.3 4.3 fusion.26
  103.6 0.0 all-reduce.5.cloned.1.call-update
  103.6 0.0 all-reduce.7.cloned.1.call-start
  103.7 0.0 copy-done.6
  103.7 1.3 convolution_bitcast_fusion.1
  105.0 1.3 convolution_bitcast_fusion
  106.3 65.5 %all-reduce.5.cloned.1.call-done = f32[16,128,224]{1,2,0:T(8,128)} async-done(((f32[16,128,224]{1,2,0:T(8,128)}), f32[16,128,224]{1,2,0:T(8,128)}) %all-reduce.5.cloned.1.call-update) | async-done | bytes 1835024 | tf_op jit(solution)/shard_map/psum | solution.py:65
  171.8 3.3 fusion.119
  175.1 0.0 copy-start.4
  175.1 0.0 slice-start.5
  175.1 0.0 slice-start.6
  175.1 0.0 slice-start.7
  175.1 31.7 %fusion.20 = f32[225,16,150]{2,1,0:T(8,128)} fusion(f32[225,150,128]{2,1,0:T(8,128)} %param.7, f32[16,128,225]{1,2,0:T(8,128)S(1)} %fusion.119), kind=kOutput, calls=%fused_computation.20 | convolution fusion | flops 829440000 | bytes 21283200 | tf_op jit(solution)/shard_map/cpw,wsp->csw/dot_general | solution.py:73
  206.9 0.0 copy-done.4
  206.9 1.9 fusion.118
  208.8 0.0 slice-start.8
  208.8 0.0 slice-start.9
  208.8 30.4 %fusion.24 = f32[225,16,150]{2,1,0:T(8,128)S(1)} fusion(f32[225,150,128]{2,1,0:T(8,128)} %param.7, f32[16,128,225]{1,2,0:T(8,128)S(1)} %fusion.118), kind=kOutput, calls=%fused_computation.24 | convolution fusion | flops 829440000 | bytes 21283200 | tf_op jit(solution)/shard_map/cpw,wsp->csw/dot_general | solution.py:67
  239.2 0.0 slice-done.5
  239.2 29.7 %add_bitcast_fusion = f32[16,150,225]{1,0,2:T(8,128)S(1)} fusion(f32[225,16,150]{2,1,0:T(8,128)} %fusion.20, f32[225,150,128]{2,1,0:T(8,128)S(1)} %bitcast.76, f32[16,128,225]{1,2,0:T(8,128)S(1)} %fusion.118), kind=kOutput, calls=%fused_computation.5 | convolution fusion | flops 829980032 | bytes 23443200 | tf_op jit(solution)/shard_map/cpw,wsp->csw/dot_general | solution.py:76
  268.9 9.1 %fusion = f32[224,16,150]{0,2,1:T(8,128)S(1)} fusion(f32[16,150,225]{1,0,2:T(8,128)S(1)} %add_bitcast_fusion, f32[225]{0:T(256)S(1)} %fusion.90), kind=kOutput, calls=%fused_computation.1 | convolution fusion | flops 1452024064 | bytes 4311300 | tf_op jit(solution)/shard_map/csw,wt->cts/dot_general | solution.py:82
  278.1 27.8 %subtract_bitcast_fusion = f32[16,150,225]{1,0,2:T(8,128)S(1)} fusion(f32[225,16,150]{2,1,0:T(8,128)S(1)} %fusion.24, f32[225,150,128]{2,1,0:T(8,128)S(1)} %bitcast.76, f32[16,128,225]{1,2,0:T(8,128)S(1)} %fusion.119), kind=kOutput, calls=%fused_computation.6 | convolution fusion | flops 829980032 | bytes 23443200 | tf_op jit(solution)/shard_map/cpw,wsp->csw/dot_general | solution.py:70
  305.8 10.0 %add_bitcast_fusion.1 = f32[16,224,150]{1,2,0:T(8,128)} fusion(f32[224,16,150]{0,2,1:T(8,128)S(1)} %fusion, f32[16,150,225]{1,0,2:T(8,128)S(1)} %subtract_bitcast_fusion, f32[225]{0:T(256)S(1)} %fusion.89), kind=kOutput, calls=%fused_computation.7 | convolution fusion | flops 1452561664 | bytes 6461700 | tf_op jit(solution)/shard_map/csw,wt->cts/dot_general | solution.py:79
  315.9 3.9 copy.29
  319.8 4.2 reshape.125
  324.1 0.0 all-reduce.7.cloned.1.call-update
  324.1 0.0 all-gather.3.cloned.1.call-start
  324.1 0.6 dynamic-slice
  325.4 64.0 %all-reduce.7.cloned.1.call-done = f32[16,33600]{1,0:T(8,128)} async-done(((f32[16,33600]{1,0:T(8,128)}), f32[16,33600]{1,0:T(8,128)}) %all-reduce.7.cloned.1.call-update) | async-done | bytes 2150416
  389.4 1.8 dynamic-slice_bitcast_fusion
  391.2 0.0 all-gather.3.cloned.1.call-update
  391.3 0.1 compare_select_fusion
  391.4 0.1 reshape.128
  392.1 0.1 fusion.86
  392.2 25.7 %all-gather.3.cloned.1.call-done = f32[4,4200,16]{1,2,0:T(8,128)} async-done(((f32[1,4200,16]{1,2,0:T(8,128)}), f32[4,4200,16]{1,2,0:T(8,128)}) %all-gather.3.cloned.1.call-update) | async-done | bytes 1075216 | tf_op jit(solution)/shard_map/all_gather | solution.py:87
  417.9 6.1 %copy.30 = f32[4,4200,16]{2,1,0:T(8,128)} copy(f32[4,4200,16]{1,2,0:T(8,128)} %all-gather.3.cloned.1.call-done) | data formatting | bytes 2150400 | tf_op jit(solution)/shard_map/all_gather | solution.py:87
  424.1 35.3 %gather_fusion = f32[16800,16]{1,0:T(8,128)} fusion(f32[16,16800]{0,1:T(8,128)} %bitcast.77, s32[17408]{0:T(1024)S(1)} %pad_clamp_fusion), kind=kCustom, calls=%fused_computation | custom fusion | bytes 2217600 | tf_op jit(solution)/shard_map/jit(_take)/gather | solution.py:94
  459.4 6.4 %copy.31 = f32[28,600,16]{1,2,0:T(8,128)} copy(f32[28,600,16]{2,1,0:T(8,128)} %bitcast.78) | data formatting | bytes 2150400 | tf_op jit(solution)/shard_map/jit(_take)/gather | solution.py:94
  465.7 7.7 %fusion.32 = f32[16,96]{1,0:T(8,128)S(1)} fusion(f32[96,28,600]{2,0,1:T(8,128)} %param.11, f32[28,600,16]{1,2,0:T(8,128)} %copy.31, pred[28,600]{1,0:T(8,128)(4,1)S(1)} %fusion.86), kind=kOutput, calls=%fused_computation.32 | convolution fusion | flops 309926400 | bytes 7549344 | tf_op jit(solution)/shard_map/ck,rk->cr/dot_general | solution.py:97
  473.4 16.6 %all-reduce.1 = f32[16,96]{1,0:T(8,128)S(1)} all-reduce(f32[16,96]{1,0:T(8,128)S(1)} %fusion.32), channel_id=3, replica_groups=mesh['sens'=4,'par'=8] {'par'}, use_global_device_ids=true, to_apply=%region_2.3.clone | all-reduce | flops 1536 | bytes 12288
  490.1 0.6 constant_dynamic-slice_fusion
  (21 shorter events, 0.1 us)
Async XLA Ops:
  6.5 1.7 copy-start
  6.5 165.2 %all-reduce.5.cloned.1.call-start = ((), (), s32[]{:S(2)}) async-start(), calls=%async_computation | async-start | bytes 3670016 | tf_op jit(solution)/shard_map/psum | solution.py:65
  27.9 18.4 %copy-start.3 = (f32[16,150,225]{1,0,2:T(8,128)S(1)}, f32[16,150,225]{1,0,2:T(8,128)}, u32[]{:S(2)}) copy-start(f32[16,150,225]{1,0,2:T(8,128)} %copy.16) | copy-start | bytes 6480004
  27.9 36.6 %slice-start = ((s8[17510400]{0:T(1024)(128)(4,1)}), s8[4194304]{0:T(1024)(128)(4,1)S(1)}, s32[]{:S(2)}) async-start(s8[17510400]{0:T(1024)(128)(4,1)} %bitcast.73), calls=%async_computation.3 | async-start | bytes 8388608
  27.9 36.6 %slice-start.1 = ((s8[17510400]{0:T(1024)(128)(4,1)}), s8[4194304]{0:T(1024)(128)(4,1)S(1)}, s32[]{:S(2)}) async-start(s8[17510400]{0:T(1024)(128)(4,1)} %bitcast.73), calls=%async_computation.4 | async-start | bytes 8388608
  27.9 36.6 %slice-start.2 = ((s8[17510400]{0:T(1024)(128)(4,1)}), s8[4194304]{0:T(1024)(128)(4,1)S(1)}, s32[]{:S(2)}) async-start(s8[17510400]{0:T(1024)(128)(4,1)} %bitcast.73), calls=%async_computation.5 | async-start | bytes 8388608
  46.4 18.2 %slice-start.3 = ((s8[17510400]{0:T(1024)(128)(4,1)}), s8[4194304]{0:T(1024)(128)(4,1)S(1)}, s32[]{:S(2)}) async-start(s8[17510400]{0:T(1024)(128)(4,1)} %bitcast.73), calls=%async_computation.6 | async-start | bytes 8388608
  46.4 18.2 %slice-start.4 = ((s8[17510400]{0:T(1024)(128)(4,1)}), s8[733184]{0:T(1024)(128)(4,1)S(1)}, s32[]{:S(2)}) async-start(s8[17510400]{0:T(1024)(128)(4,1)} %bitcast.73), calls=%async_computation.7 | async-start | bytes 1466368
  64.6 15.9 %copy-start.2 = (f32[16,150,225]{1,0,2:T(8,128)S(1)}, f32[16,150,225]{1,0,2:T(8,128)}, u32[]{:S(2)}) copy-start(f32[16,150,225]{1,0,2:T(8,128)} %copy.18) | copy-start | bytes 6480004
  99.3 4.4 copy-start.6
  103.6 285.8 %all-reduce.7.cloned.1.call-start = ((), (), s32[]{:S(2)}) async-start(), calls=%async_computation.2 | async-start | bytes 4308992
  175.1 31.8 %copy-start.4 = (f32[16,128,224]{1,2,0:T(8,128)S(1)}, f32[16,128,224]{1,2,0:T(8,128)}, u32[]{:S(2)}) copy-start(f32[16,128,224]{1,2,0:T(8,128)} %all-reduce.5.cloned.1.call-done) | copy-start | bytes 5505028
  175.1 64.1 %slice-start.5 = ((s8[17510400]{0:T(1024)(128)(4,1)}), s8[4194304]{0:T(1024)(128)(4,1)S(1)}, s32[]{:S(2)}) async-start(s8[17510400]{0:T(1024)(128)(4,1)} %bitcast.75), calls=%async_computation.8 | async-start | bytes 8388608
  175.1 64.1 %slice-start.6 = ((s8[17510400]{0:T(1024)(128)(4,1)}), s8[4194304]{0:T(1024)(128)(4,1)S(1)}, s32[]{:S(2)}) async-start(s8[17510400]{0:T(1024)(128)(4,1)} %bitcast.75), calls=%async_computation.9 | async-start | bytes 8388608
  175.1 64.1 %slice-start.7 = ((s8[17510400]{0:T(1024)(128)(4,1)}), s8[4194304]{0:T(1024)(128)(4,1)S(1)}, s32[]{:S(2)}) async-start(s8[17510400]{0:T(1024)(128)(4,1)} %bitcast.75), calls=%async_computation.10 | async-start | bytes 8388608
  208.8 30.5 %slice-start.8 = ((s8[17510400]{0:T(1024)(128)(4,1)}), s8[4194304]{0:T(1024)(128)(4,1)S(1)}, s32[]{:S(2)}) async-start(s8[17510400]{0:T(1024)(128)(4,1)} %bitcast.75), calls=%async_computation.11 | async-start | bytes 8388608
  208.8 30.5 %slice-start.9 = ((s8[17510400]{0:T(1024)(128)(4,1)}), s8[733184]{0:T(1024)(128)(4,1)S(1)}, s32[]{:S(2)}) async-start(s8[17510400]{0:T(1024)(128)(4,1)} %bitcast.75), calls=%async_computation.12 | async-start | bytes 1466368
  319.8 4.3 copy-start.7
  324.1 67.2 %copy-start.5 = (s32[600]{0:T(1024)S(1)}, s32[600]{0:T(1024)}, u32[]{:S(2)}) copy-start(s32[600]{0:T(1024)} %param.10) | copy-start | bytes 7204
  324.1 93.8 %all-gather.3.cloned.1.call-start = ((), (), s32[]{:S(2)}) async-start(), calls=%async_computation.1 | async-start | bytes 1351680 | tf_op jit(solution)/shard_map/all_gather | solution.py:87
  459.4 31.3 %copy-start.1 = (f32[16,150,224]{2,0,1:T(8,128)S(1)}, f32[16,150,224]{2,0,1:T(8,128)}, u32[]{:S(2)}) copy-start(f32[16,150,224]{2,0,1:T(8,128)} %param.6) | copy-start | bytes 6451204
Sparse Core Ops, SparseCore 0:
  103.7 67.9 all-reduce.4
  324.2 65.1 all-reduce.6
  391.4 26.4 all-gather.2
where the time goes:
time: 504 us; the launch traced here: 498 us
  matrix products  241 us (48%)
  waiting for transfers between devices  155 us (31%)
  local copies, waits for them, and re-layouts  69.3 us (14%)
  blocking collectives  16.6 us (3%)
  between operations  15.2 us (3%)
    psum x1, waiting for transfers between devices, shards(): adjoint = lax.psum(partial_adj, 'sens')  65.5 us
    unnamed x4, waiting for transfers between devices  64.1 us
    gather x2, local copies, waits for them, and re-layouts, shards(): permuted = jnp.take(gathered, pick_index, axis=1)  41.7 us
    dot_general x1, matrix products, shards(): jnp.einsum('cpw,wsp->csw', field_imag, spec_real, precision=highest, pref...  31.7 us
    dot_general x1, matrix products, shards(): jnp.einsum('cpw,wsp->csw', field_real, spec_real, precision=highest, pref...  30.4 us
    dot_general x1, matrix products, shards(): jnp.einsum('cpw,wsp->csw', field_real, spec_imag, precision=highest, pref...  29.7 us
    dot_general x1, matrix products, shards(): jnp.einsum('cpw,wsp->csw', field_imag, spec_imag, precision=highest, pref...  27.8 us
    all_gather x1, waiting for transfers between devices, shards(): gathered = lax.all_gather(predicted, 'sens', axis=1, tiled=True)  25.7 us
  transfers between devices with their start and end apart: 3, of which 3 were waited for; matrix products, arithmetic and copies ran while one was open for 1% of the time, Pallas kernels for 0%

commit v1 on v0

v1 whole, which is shorter than its diff:
```python
import functools

import jax
import jax.numpy as jnp
import numpy as np
from jax import lax
from jax.experimental import pallas as pl
from jax.experimental.pallas import tpu as pltpu
from jax.sharding import PartitionSpec as P

F32 = jnp.float32
BF16 = jnp.bfloat16
LANES = 128


def round_up(value, step):
    return (value + step - 1) // step * step


def split(value):
    high = value.astype(BF16)
    low = (value - high.astype(F32)).astype(BF16)
    return high, low


def dot(left, right):
    return lax.dot_general(left, right, (((1,), (0,)), ((), ())), preferred_element_type=F32)


def dot_nt(left, right):
    return lax.dot_general(left, right, (((1,), (1,)), ((), ())), preferred_element_type=F32)


def split_host(table):
    high = table.astype(np.float32).astype(jnp.bfloat16)
    low = (table - high.astype(np.float64)).astype(jnp.bfloat16)
    return high, low


def forward_table(steps, bins, padded):
    length = 2 * steps
    phase = 2.0 * np.pi * ((np.arange(bins)[:, None] * np.arange(steps)[None, :]) % length) / length
    table = np.zeros((2 * padded, steps))
    table[:bins] = np.cos(phase)
    table[padded : padded + bins] = -np.sin(phase)
    return table


def inverse_table(steps, bins, padded):
    length = 2 * steps
    phase = 2.0 * np.pi * ((np.arange(steps)[:, None] * np.arange(bins)[None, :]) % length) / length
    weight = np.full((bins,), 2.0)
    weight[0] = 1.0
    weight[-1] = 1.0
    weight = weight / length
    table = np.zeros((steps, 2 * padded))
    table[:, :bins] = np.cos(phase) * weight
    table[:, padded : padded + bins] = -np.sin(phase) * weight
    return table


def block_of(bins, most):
    return max(size for size in range(1, most + 1) if bins % size == 0)


class Packing:
    def __init__(self, cols, sens_dev):
        self.cols = cols
        self.sens_dev = sens_dev
        self.full = sens_dev // LANES
        self.rest = sens_dev % LANES
        self.share = LANES // self.rest if self.rest else 1
        self.rest_rows = -(-cols // self.share) if self.rest else 0
        self.rows = self.full * cols + self.rest_rows
        self.width = LANES * (self.full + (1 if self.rest else 0))


def adjoint_kernel(mask_ref, rec_ref, fh_ref, fl_ref, ih_ref, il_ref, sr_ref, si_ref, *rest):
    outs, (rec_spec, adj) = rest[:-2], rest[-2:]
    step = pl.program_id(0)
    cols = rec_ref.shape[0]
    block, sens_dev, par_dev = sr_ref.shape
    bins = rec_spec.shape[0]
    padded = adj.shape[1] // 2
    half = cols // 2

    @pl.when(step == 0)
    def _():
        fh, fl = fh_ref[...], fl_ref[...]
        for k in range(cols):
            rh, rl = split(rec_ref[jnp.bitwise_xor(k, mask_ref[k // half])])
            value = dot_nt(fh, rh) + (dot_nt(fl, rh) + dot_nt(fh, rl))
            rec_spec[:, k, :] = value[:bins]
            rec_spec[:, cols + k, :] = value[padded : padded + bins]
        zeros = jnp.zeros((cols, padded - bins, par_dev), F32)
        adj[:, bins:padded, :] = zeros
        adj[:, padded + bins :, :] = zeros

    for i in range(block):
        w = step * block + i
        xh, xl = split(rec_spec[w])
        sh, sl = split(jnp.concatenate([sr_ref[i], si_ref[i]], axis=1))
        both = dot(jnp.concatenate([xh, xl], axis=0), sh)
        value = both[: 2 * cols] + both[2 * cols :] + dot(xh, sl)
        adj[:, pl.ds(w, 1), :] = (value[:cols, :par_dev] + value[cols:, par_dev:])[:, None, :]
        adj[:, pl.ds(padded + w, 1), :] = (value[cols:, :par_dev] - value[:cols, par_dev:])[:, None, :]

    @pl.when(step == pl.num_programs(0) - 1)
    def _():
        ih, il = ih_ref[...], il_ref[...]
        per = cols // len(outs)
        for k in range(0, cols, 2):
            ah, al = split(jnp.concatenate([adj[k], adj[k + 1]], axis=1))
            value = dot(ih, ah) + (dot(il, ah) + dot(ih, al))
            outs[k // per][k % per] = value[:, :par_dev]
            outs[(k + 1) // per][(k + 1) % per] = value[:, par_dev:]


def forward_kernel(packing, mask_ref, th_ref, tl_ref, ih_ref, il_ref, *rest):
    (keep_ref, send_ref, field, pred, left) = rest[-5:]
    sr_ref, si_ref = rest[-7:-5]
    pieces = rest[:-7]
    step = pl.program_id(0)
    cols = packing.cols
    block, sens_dev, par_dev = sr_ref.shape
    bins = field.shape[0]
    padded = pred.shape[1] // 2
    half = cols // 2
    full, width = packing.full, packing.full * LANES

    @pl.when(step == 0)
    def _():
        th, tl = th_ref[...], tl_ref[...]
        per = cols // len(pieces)
        for k in range(0, cols, 2):
            first, second = pieces[k // per][k % per], pieces[(k + 1) // per][(k + 1) % per]
            ah, al = split(jnp.concatenate([first, second], axis=1))
            value = dot(th, ah) + (dot(tl, ah) + dot(th, al))
            for j in range(2):
                c = jnp.bitwise_xor(k + j, mask_ref[k // half])
                part = value[:, j * par_dev : (j + 1) * par_dev]
                field[:, pl.ds(c, 1), :] = part[:bins][:, None, :]
                field[:, pl.ds(cols + c, 1), :] = part[padded : padded + bins][:, None, :]
        zeros = jnp.zeros((cols, padded - bins, sens_dev), F32)
        pred[:, bins:padded, :] = zeros
        pred[:, padded + bins :, :] = zeros

    for i in range(block):
        w = step * block + i
        x = field[w]
        turned = jnp.concatenate([-x[cols:], x[:cols]], axis=0)
        xh, xl = split(jnp.concatenate([x, turned], axis=1))
        sh, sl = split(jnp.concatenate([sr_ref[i], si_ref[i]], axis=1))
        both = dot_nt(jnp.concatenate([xh, xl], axis=0), sh)
        value = both[: 2 * cols] + both[2 * cols :] + dot_nt(xh, sl)
        pred[:, pl.ds(w, 1), :] = value[:cols][:, None, :]
        pred[:, pl.ds(padded + w, 1), :] = value[cols:][:, None, :]

    @pl.when(step == pl.num_programs(0) - 1)
    def _():
        ih, il = ih_ref[...], il_ref[...]
        rows = packing.rows
        count = ih.shape[0] // 2
        for c in range(cols):
            ph, pl_low = split(pred[c])
            value = dot(ih, ph) + (dot(il, ph) + dot(ih, pl_low))
            for f in range(full):
                part = value[:, f * LANES : (f + 1) * LANES]
                keep_ref[pl.ds(c * full + f, count, stride=rows), :] = part[:count]
                send_ref[pl.ds(c * full + f, count, stride=rows), :] = part[count:]
            if packing.rest:
                place = c % packing.share
                pieces_of = [value[:, width:]]
                if place:
                    pieces_of = [jnp.zeros((2 * count, place * packing.rest), F32)] + pieces_of
                after = LANES - (place + 1) * packing.rest
                if after:
                    pieces_of = pieces_of + [jnp.zeros((2 * count, after), F32)]
                part = jnp.concatenate(pieces_of, axis=1)
                if place == 0:
                    left[...] = part
                else:
                    left[...] += part
                if place == packing.share - 1 or c == cols - 1:
                    row = cols * full + c // packing.share
                    keep_ref[pl.ds(row, count, stride=rows), :] = left[:count]
                    send_ref[pl.ds(row, count, stride=rows), :] = left[count:]


def prepare_kernel(packing, index_ref, map_ref, prior_ref, fh_ref, fl_ref, inv_ref, rows_ref,
                   oh_ref, ol_ref, th_ref, tl_ref, ih_ref, il_ref, select, table):
    step = pl.program_id(0)
    blocks = oh_ref.shape[2] // packing.width
    times = rows_ref.shape[1]
    count = rows_ref.shape[0]

    @pl.when(step == 0)
    def _():
        lane = lax.broadcasted_iota(jnp.int32, (1, packing.width), 1)
        width = packing.full * LANES
        if packing.rest:
            beyond = lane - width
            folded = width + lax.rem(jnp.maximum(beyond, 0), packing.rest)
            local = jnp.where(beyond >= 0, folded, lane)
            valid = beyond < packing.share * packing.rest
        else:
            local = lane
            valid = lane >= 0
        for m in range(blocks):
            owner = jnp.bitwise_xor(index_ref[0], m)
            wanted = jnp.where(valid, owner * packing.sens_dev + local, -1)
            hit = map_ref[...] == wanted
            select[:, m * packing.width : (m + 1) * packing.width] = jnp.where(hit, 1.0, 0.0).astype(BF16)
        ph, pl_low = split(prior_ref[...])
        folded_table = dot_nt(fh_ref[...], ph) + (dot_nt(fl_ref[...], ph) + dot_nt(fh_ref[...], pl_low))
        th, tl = split(folded_table)
        th_ref[...] = th
        tl_ref[...] = tl
        par = inv_ref.shape[0]
        pairs = par // 2
        for r in range(2):
            for d in range(pairs):
                z = lax.rem(index_ref[1] // 2 + d, pairs)
                core = jnp.bitwise_xor(lax.rem(index_ref[1], 2), r)
                j = r * pairs + d
                table[j * times : (j + 1) * times, :] = inv_ref[2 * z + core]
        ih, il = split(table[...])
        ih_ref[...] = ih
        il_ref[...] = il

    group = block_of(times, 7)
    for t in range(0, times, group):
        parts = []
        for g in range(group):
            parts.extend(split(rows_ref[:, t + g, :]))
        moved = dot(jnp.concatenate(parts, axis=0), select[...]).astype(BF16)
        for g in range(group):
            oh_ref[t + g] = moved[2 * g * count : (2 * g + 1) * count]
            ol_ref[t + g] = moved[(2 * g + 1) * count : (2 * g + 2) * count]


def update_kernel(packing, oh_ref, ol_ref, *rest):
    gathered, out_ref = rest[:-1], rest[-1]
    times = oh_ref.shape[0]
    cols, rows, full = packing.cols, packing.rows, packing.full
    total = jnp.zeros(out_ref.shape, F32)
    if packing.rest:
        row = lax.broadcasted_iota(jnp.int32, (cols, LANES), 0)
        lane = lax.broadcasted_iota(jnp.int32, (cols, LANES), 1)
        own = lax.rem(row, packing.share) == lane // packing.rest
        shared = row // packing.share
    for t in range(times):
        for m, ref in enumerate(gathered):
            held = ref[t * rows : (t + 1) * rows, :]
            parts = []
            if full == 1:
                parts.append(held[:cols])
            elif full > 1:
                wide = held[: cols * full].reshape(cols, full, LANES)
                parts.extend(wide[:, f, :] for f in range(full))
            if packing.rest:
                spread = jnp.zeros((cols, LANES), F32)
                for j in range(packing.rest_rows):
                    line = held[cols * full + j : cols * full + j + 1]
                    spread = jnp.where(own & (shared == j), line, spread)
                parts.append(spread)
            xh, xl = split(jnp.concatenate(parts, axis=1))
            place = slice(m * packing.width, (m + 1) * packing.width)
            both = dot_nt(jnp.concatenate([xh, xl], axis=0), oh_ref[t, :, place])
            total = total + (both[:cols] + both[cols:] + dot_nt(xh, ol_ref[t, :, place]))
    out_ref[...] = total


def whole(array):
    return pl.BlockSpec(array.shape, lambda *_: (0,) * array.ndim)


def swap(size, mask):
    return [(k, k ^ mask) for k in range(size)]


def reduce_quarters(keep, send, first, second, size):
    per = keep.shape[0] // 2
    near = keep + lax.ppermute(send, "sens", swap(size, first))
    here = near[:per] + lax.ppermute(near[per:], "sens", swap(size, second))
    over = lax.ppermute(here, "sens", swap(size, second))
    back = lax.ppermute(here, "sens", swap(size, first))
    return [here, over, back, lax.ppermute(over, "sens", swap(size, first))]


def shards(records, spec_real, spec_imag, prior_cov, sensor_map, inverse_rows):
    cols, sens_dev, steps = records.shape
    bins, _, par_dev = spec_real.shape
    padded = round_up(bins, 8)
    sens, par = lax.axis_size("sens"), lax.axis_size("par")
    sens_index, par_index = lax.axis_index("sens"), lax.axis_index("par")
    packing = Packing(cols, sens_dev)
    rows_dev, times, sensors = inverse_rows.shape
    quarters = sens == 4 and cols % 8 == 0
    limit = 56 * 2**20

    fwd = forward_table(steps, bins, padded)
    inv = inverse_table(steps, bins, padded)
    fh, fl = (jnp.asarray(part) for part in split_host(fwd))
    ih, il = (jnp.asarray(part) for part in split_host(inv))
    inv_blocks = jnp.asarray(inv.reshape(par, times, 2 * padded).astype(np.float32))

    if quarters:
        bit0, bit1 = sens_index & 1, sens_index >> 1
        unit = cols // 8
        mask = jnp.stack([(2 * bit0 + bit1) * unit, (2 * bit1 + bit0) * unit]).astype(jnp.int32)
        n_out = 4
    else:
        mask = jnp.zeros((2,), jnp.int32)
        n_out = 1

    block = block_of(bins, 15)
    grid = (bins // block,)
    spec_block = pl.BlockSpec((block, sens_dev, par_dev), lambda i: (i, 0, 0))
    smem = pl.BlockSpec(memory_space=pltpu.SMEM)
    phase_cost = pl.CostEstimate(
        flops=24 * cols * bins * sens_dev * par_dev, bytes_accessed=8 * bins * sens_dev * par_dev, transcendentals=0
    )
    out_a = [jax.ShapeDtypeStruct((cols // n_out, steps, par_dev), F32)] * n_out
    parts = pl.pallas_call(
        adjoint_kernel,
        grid=grid,
        in_specs=[smem, whole(records), whole(fh), whole(fl), whole(ih), whole(il), spec_block, spec_block],
        out_specs=[whole(shape) for shape in out_a],
        out_shape=out_a,
        scratch_shapes=[
            pltpu.VMEM((bins, 2 * cols, sens_dev), F32),
            pltpu.VMEM((cols, 2 * padded, par_dev), F32),
        ],
        compiler_params=pltpu.CompilerParams(vmem_limit_bytes=limit),
        cost_estimate=phase_cost,
        name="adjoint",
    )(mask, records, fh, fl, ih, il, spec_real, spec_imag)

    index = jnp.stack([sens_index, par_index]).astype(jnp.int32)
    row_block = block_of(rows_dev, 32)
    width = sens * packing.width
    moved = jax.ShapeDtypeStruct((times, rows_dev, width), BF16)
    folded = jax.ShapeDtypeStruct((2 * padded, steps), BF16)
    turned = jax.ShapeDtypeStruct((steps, 2 * padded), BF16)
    map_column = sensor_map.reshape(sensors, 1)
    oh, ol, th, tl, ih2, il2 = pl.pallas_call(
        functools.partial(prepare_kernel, packing),
        grid=(rows_dev // row_block,),
        in_specs=[
            smem,
            whole(map_column),
            whole(prior_cov),
            whole(fh),
            whole(fl),
            whole(inv_blocks),
            pl.BlockSpec((row_block, times, sensors), lambda i: (i, 0, 0)),
        ],
        out_specs=[pl.BlockSpec((times, row_block, width), lambda i: (0, i, 0))] * 2
        + [whole(folded)] * 2
        + [whole(turned)] * 2,
        out_shape=[moved, moved, folded, folded, turned, turned],
        scratch_shapes=[pltpu.VMEM((sensors, width), BF16), pltpu.VMEM((steps, 2 * padded), F32)],
        compiler_params=pltpu.CompilerParams(vmem_limit_bytes=limit),
        cost_estimate=pl.CostEstimate(
            flops=4 * rows_dev * times * sensors * width, bytes_accessed=8 * rows_dev * times * sensors, transcendentals=0
        ),
        name="prepare",
    )(index, map_column, prior_cov, fh, fl, inv_blocks, inverse_rows)

    if quarters:
        pieces = reduce_quarters(parts[0], parts[1], 1, 2, sens) + reduce_quarters(parts[2], parts[3], 2, 1, sens)
    else:
        pieces = [lax.psum(parts[0], "sens")]

    shard_rows = times * packing.rows
    half = jax.ShapeDtypeStruct((par // 2 * shard_rows, LANES), F32)
    keep, send = pl.pallas_call(
        functools.partial(forward_kernel, packing),
        grid=grid,
        in_specs=[smem, whole(th), whole(tl), whole(ih2), whole(il2)]
        + [whole(piece) for piece in pieces]
        + [spec_block, spec_block],
        out_specs=[whole(half)] * 2,
        out_shape=[half, half],
        scratch_shapes=[
            pltpu.VMEM((bins, 2 * cols, par_dev), F32),
            pltpu.VMEM((cols, 2 * padded, sens_dev), F32),
            pltpu.VMEM((steps, LANES), F32),
        ],
        compiler_params=pltpu.CompilerParams(vmem_limit_bytes=limit),
        cost_estimate=phase_cost,
        name="forward",
    )(mask, th, tl, ih2, il2, *pieces, spec_real, spec_imag)

    pair = keep + lax.ppermute(send, "par", swap(par, 1))
    mine = pair[:shard_rows]
    for d in range(1, par // 2):
        there = pair[d * shard_rows : (d + 1) * shard_rows]
        mine = mine + lax.ppermute(there, "par", [(k, (k + 2 * d) % par) for k in range(par)])
    gathered = [mine] + [lax.ppermute(mine, "sens", swap(sens, m)) for m in range(1, sens)]

    result = jax.ShapeDtypeStruct((cols, rows_dev), F32)
    partial = pl.pallas_call(
        functools.partial(update_kernel, packing),
        out_shape=result,
        compiler_params=pltpu.CompilerParams(vmem_limit_bytes=limit),
        cost_estimate=pl.CostEstimate(
            flops=6 * rows_dev * times * cols * width, bytes_accessed=4 * rows_dev * times * width, transcendentals=0
        ),
        name="update",
    )(oh, ol, *gathered)
    per_dev = cols // par
    spread = lax.all_to_all(partial.reshape(par, per_dev, rows_dev), "par", 0, 0)
    return jnp.sum(spread, axis=0)


def solution(mesh):
    return jax.shard_map(
        shards,
        mesh=mesh,
        in_specs=(
            P(None, "sens", None),
            P(None, "sens", "par"),
            P(None, "sens", "par"),
            P(),
            P(),
            P("sens", "par", None),
        ),
        out_specs=P("par", "sens"),
        check_vma=False,
    )
```

time: 504 us -> 210 us (0.42); the launches traced: 498 us -> 209 us
  matrix products: 241 us -> 0 us
  waiting for transfers between devices: 155 us -> 50 us
  Pallas kernels: 0 us -> 103 us
  local copies, waits for them, and re-layouts: 69.3 us -> 17.3 us
  starting transfers between devices: 0.09 us -> 23.2 us
  between operations: 15.2 us -> 0.19 us
  blocking collectives: 16.6 us -> 9.62 us
  other arithmetic: 0.23 us -> 5.56 us
    dot_general x19 -> x0, matrix products: 241 us -> none  [the longest x1 31.7 us: shards(): jnp.einsum('cpw,wsp->csw', field_imag, spec_real, precision=highest, pref...]
    pallas_call x0 -> x4, Pallas kernels: none -> 103 us  [the longest x1 35.7 us: shards(): pl.pallas_call(functools.partial(prepare_kernel, packing), grid=(rows_dev...]
    psum x1 -> x0, waiting for transfers between devices: 65.5 us -> none  [shards(): adjoint = lax.psum(partial_adj, 'sens')]
    unnamed x4 -> x0, waiting for transfers between devices: 64.1 us -> none
    ppermute x0 -> x17, waiting for transfers between devices: none -> 50 us  [the longest x3 23.7 us: shards(): lax.ppermute(there, 'par', [(k, (k + 2 * d) % par) for k in range(par)])]
    gather x2 -> x0, local copies, waits for them, and re-layouts: 41.7 us -> none  [shards(): permuted = jnp.take(gathered, pick_index, axis=1)]
    all_gather x1 -> x0, waiting for transfers between devices: 25.7 us -> none  [shards(): gathered = lax.all_gather(predicted, 'sens', axis=1, tiled=True)]
    ppermute x0 -> x17, starting transfers between devices: none -> 23.2 us  [the longest x3 4.66 us: shards(): lax.ppermute(there, 'par', [(k, (k + 2 * d) % par) for k in range(par)])]
  transfers between devices with their start and end apart: 3 -> 17, of which waited for: 3 -> 8; matrix products, arithmetic and copies ran while one was open for 1% -> 7% of each run, Pallas kernels for 0% -> 17%
where the time goes in v1:
time: 210 us; the launch traced here: 209 us
  Pallas kernels  103 us (49%)
  waiting for transfers between devices  50 us (24%)
  starting transfers between devices  23.2 us (11%)
  local copies, waits for them, and re-layouts  17.3 us (8%)
  blocking collectives  9.62 us (5%)
  other arithmetic  5.56 us (3%)
    pallas_call x1, Pallas kernels, shards(): pl.pallas_call(functools.partial(prepare_kernel, packing), grid=(rows_dev...  35.7 us
    pallas_call x1, Pallas kernels, shards(): pl.pallas_call(functools.partial(forward_kernel, packing), grid=grid, in_...  32.6 us
    pallas_call x1, Pallas kernels, shards(): pl.pallas_call(adjoint_kernel, grid=grid, in_specs=[smem, whole(records),...  26.9 us
    ppermute x3, waiting for transfers between devices, shards(): lax.ppermute(there, 'par', [(k, (k + 2 * d) % par) for k in range(par)])  23.7 us
    unnamed x28, local copies, waits for them, and re-layouts  16.4 us
    ppermute x3, waiting for transfers between devices, shards(): lax.ppermute(mine, 'sens', swap(sens, m))  11 us
    all_to_all x1, blocking collectives, shards(): lax.all_to_all(partial.reshape(par, per_dev, rows_dev), 'par', 0, 0)  9.62 us
    ppermute x2, waiting for transfers between devices, reduce_quarters(): near = keep + lax.ppermute(send, 'sens', swap(size, first))  9.21 us
  transfers between devices with their start and end apart: 17, of which 8 were waited for; matrix products, arithmetic and copies ran while one was open for 7% of the time, Pallas kernels for 17%

profile of v1, /device:TPU:0, one launch (start us, length us, event | category | flops | bytes accessed | tf_op | source)
XLA Modules:
  0.0 209.4 jit_solution(1029771669722974080)
XLA Ops:
  0.0 4.6 %copy.16.rec_ref = f32[16,150,224]{2,1,0:T(8,128)} copy(f32[16,150,224]{2,0,1:T(8,128)} %param.11) | data formatting | bytes 4300800 | tf_op args[0]
  4.6 0.6 pad_add_fusion.1.mask_ref
  5.2 26.9 %adjoint.1 = (f32[4,224,128]{2,1,0:T(8,128)}, f32[4,224,128]{2,1,0:T(8,128)}, f32[4,224,128]{2,1,0:T(8,128)}, f32[4,224,128]{2,1,0:T(8,128)}) custom-call(s32[2]{0:T(128)} %pad_add_fusion.1.mask_ref, f32[16,150,224]{2,1,0:T(8,128)} %copy.16.rec_ref, bf16[464,224]{1,0:T(8,128)(2,1)} %constant.24.clone.fh_ref, bf16[464,224]{1,0:T(8,128)(2,1)} %constant.25.clone.fl_ref, ...), custom_call_target="tpu_custom_call" | custom-call | flops 1658880000 | bytes 34560000 | tf_op jit(solution)/shard_map/adjoint/pallas_call | solution.py:325
  32.1 2.9 %collective-permute-start = (f32[4,224,128]{2,1,0:T(8,128)}, f32[4,224,128]{2,1,0:T(8,128)S(1)}, u32[]{:S(2)}, u32[]{:S(2)}) collective-permute-start(f32[4,224,128]{2,1,0:T(8,128)} %get-tuple-element.24), channel_id=1, source_target_pairs={{0,8},{8,0},{16,24},{24,16},{1,9},{9,1},{17,25},{25,17},{2,10},{10... | collective-permute-start | bytes 1376264 | tf_op jit(solution)/shard_map/ppermute | solution.py:284
  35.1 1.5 collective-permute-start.5
  36.6 9.2 %collective-permute-done = f32[4,224,128]{2,1,0:T(8,128)S(1)} collective-permute-done((f32[4,224,128]{2,1,0:T(8,128)}, f32[4,224,128]{2,1,0:T(8,128)S(1)}, u32[]{:S(2)}, u32[]{:S(2)}) %collective-permute-start) | collective-permute-done | bytes 458784 | tf_op jit(solution)/shard_map/ppermute | solution.py:284
  45.8 1.1 add.32
  46.9 1.8 collective-permute-start.1
  48.8 0.0 collective-permute-done.5
  48.8 1.1 add.34
  49.9 1.6 collective-permute-start.6
  51.4 2.3 %collective-permute-done.1 = f32[2,224,128]{2,1,0:T(8,128)S(1)} collective-permute-done((f32[2,224,128]{2,1,0:T(8,128)S(1)}, f32[2,224,128]{2,1,0:T(8,128)S(1)}, u32[]{:S(2)}, u32[]{:S(2)}) %collective-permute-start.1) | collective-permute-done | bytes 229408 | tf_op jit(solution)/shard_map/ppermute | solution.py:285
  53.8 0.0 copy-start.1
  53.8 1.5 collective-permute-start.2
  55.3 0.8 collective-permute-done.6
  56.2 0.0 copy-start.2
  56.2 1.6 collective-permute-start.7
  57.7 0.0 copy-done.12
  57.7 0.9 reshape.8.map_ref
  58.6 10.1 %copy.15.rows_ref = f32[96,28,600]{2,1,0:T(8,128)} copy(f32[96,28,600]{2,0,1:T(8,128)} %param.16) | data formatting | bytes 12902400 | tf_op args[5]
  68.7 0.6 pad_add_fusion.index_ref
  69.3 0.0 copy-done.1
  69.3 0.5 collective-permute-start.3
  69.9 0.0 copy-done.2
  69.9 0.6 collective-permute-start.8
  70.4 0.0 collective-permute-done.2.rest_1_
  70.4 1.4 collective-permute-start.4
  71.9 0.0 collective-permute-done.7.rest_5_
  71.9 1.5 collective-permute-start.9
  73.4 35.7 %prepare.1 = (bf16[28,96,1024]{2,1,0:T(8,128)(2,1)}, bf16[28,96,1024]{2,1,0:T(8,128)(2,1)}, bf16[464,224]{1,0:T(8,128)(2,1)}, bf16[464,224]{1,0:T(8,128)(2,1)}, ...) custom-call(s32[2]{0:T(128)} %pad_add_fusion.index_ref, s32[600,1]{1,0:T(8,128)} %reshape.8.map_ref, ...), custom_call_target="tpu_custom_call" | custom-call | flops 6606028800 | bytes 12902400 | tf_op jit(solution)/shard_map/prepare/pallas_call | solution.py:347
  109.1 0.0 copy-done.6
  109.1 0.0 collective-permute-done.3.rest_2_
  109.2 0.0 collective-permute-done.8.rest_6_
  109.2 0.0 copy-start.9
  109.2 0.0 collective-permute-done.4.rest_3_
  109.2 0.0 collective-permute-done.9.rest_7_
  109.2 0.6 copy-done.8
  109.8 0.1 copy-done.9
  109.9 0.1 copy-done.10
  110.0 0.1 copy-done.11
  110.1 32.6 %forward.1 = (f32[2240,128]{1,0:T(8,128)}, f32[2240,128]{1,0:T(8,128)}) custom-call(s32[2]{0:T(128)} %pad_add_fusion.1.mask_ref, bf16[464,224]{1,0:T(8,128)(2,1)} %get-tuple-element.19.th_ref, bf16[464,224]{1,0:T(8,128)(2,1)} %get-tuple-element.20.tl_ref, bf16[224,464]{1,0:T(8,128)(2,1)} %get-tuple-element.21.ih_ref, ...), custom_call_target="tpu_custom_call" | custom-call | flops 1658880000 | bytes 34560000 | tf_op jit(solution)/shard_map/forward/pallas_call | solution.py:378
  142.7 0.0 collective-permute-start.10
  142.7 3.0 %collective-permute-done.10 = f32[2240,128]{1,0:T(8,128)S(1)} collective-permute-done((f32[2240,128]{1,0:T(8,128)}, f32[2240,128]{1,0:T(8,128)S(1)}, u32[]{:S(2)}, u32[]{:S(2)}) %collective-permute-start.10) | collective-permute-done | bytes 1146912 | tf_op jit(solution)/shard_map/ppermute | solution.py:396
  145.7 1.4 add.36
  147.1 0.1 fusion.2
  147.2 3.7 %collective-permute-start.13 = (f32[560,128]{1,0:T(8,128)S(1)}, f32[560,128]{1,0:T(8,128)S(1)}, u32[]{:S(2)}, u32[]{:S(2)}) collective-permute-start(f32[560,128]{1,0:T(8,128)S(1)} %get-tuple-element.30), channel_id=1, source_target_pairs={{0,6},{1,7},{2,0},{3,1},{4,2},{5,3},{6,4},{7,5},{8,14},{9,15},{10,... | collective-permute-start | bytes 860168 | tf_op jit(solution)/shard_map/ppermute | solution.py:400
  150.8 0.0 collective-permute-start.12
  150.8 1.0 collective-permute-start.11
  151.8 6.3 %collective-permute-done.13 = f32[560,128]{1,0:T(8,128)S(1)} collective-permute-done((f32[560,128]{1,0:T(8,128)S(1)}, f32[560,128]{1,0:T(8,128)S(1)}, u32[]{:S(2)}, u32[]{:S(2)}) %collective-permute-start.13) | collective-permute-done | bytes 286752 | tf_op jit(solution)/shard_map/ppermute | solution.py:400
  158.1 17.4 %collective-permute-done.12 = f32[560,128]{1,0:T(8,128)S(1)} collective-permute-done((f32[560,128]{1,0:T(8,128)S(1)}, f32[560,128]{1,0:T(8,128)S(1)}, u32[]{:S(2)}, u32[]{:S(2)}) %collective-permute-start.12) | collective-permute-done | bytes 286752 | tf_op jit(solution)/shard_map/ppermute | solution.py:400
  175.5 0.0 collective-permute-done.11
  175.5 0.1 fusion.1.rest_0_
  175.6 0.6 collective-permute-start.14
  176.2 0.5 collective-permute-start.15
  176.7 2.5 %collective-permute-start.16 = (f32[560,128]{1,0:T(8,128)S(1)}, f32[560,128]{1,0:T(8,128)S(1)}, u32[]{:S(2)}, u32[]{:S(2)}) collective-permute-start(f32[560,128]{1,0:T(8,128)S(1)} %fusion.1.rest_0_), channel_id=1, source_target_pairs={{0,24},{8,16},{16,8},{24,0},{1,25},{9,17},{17,9},{25,1},{2,26},{10... | collective-permute-start | bytes 860168 | tf_op jit(solution)/shard_map/ppermute | solution.py:401
  179.2 6.3 %collective-permute-done.14.rest_1_ = f32[560,128]{1,0:T(8,128)S(1)} collective-permute-done((f32[560,128]{1,0:T(8,128)S(1)}, f32[560,128]{1,0:T(8,128)S(1)}, u32[]{:S(2)}, u32[]{:S(2)}) %collective-permute-start.14) | collective-permute-done | bytes 286752 | tf_op jit(solution)/shard_map/ppermute | solution.py:401
  185.5 4.7 %collective-permute-done.15.rest_2_ = f32[560,128]{1,0:T(8,128)S(1)} collective-permute-done((f32[560,128]{1,0:T(8,128)S(1)}, f32[560,128]{1,0:T(8,128)S(1)}, u32[]{:S(2)}, u32[]{:S(2)}) %collective-permute-start.15) | collective-permute-done | bytes 286752 | tf_op jit(solution)/shard_map/ppermute | solution.py:401
  190.1 0.0 collective-permute-done.16.rest_3_
  190.1 0.0 copy-done.3
  190.2 0.7 copy-done.4
  190.8 0.1 copy-done.5
  190.9 8.3 %update.1 = f32[16,96]{1,0:T(8,128)} custom-call(bf16[28,96,1024]{2,1,0:T(8,128)(2,1)} %get-tuple-element.17.oh_ref, bf16[28,96,1024]{2,1,0:T(8,128)(2,1)} %get-tuple-element.18.ol_ref, f32[560,128]{1,0:T(8,128)} %copy-done, f32[560,128]{1,0:T(8,128)} %copy-done.3, f32[560,128]{1,0:T(8,128)} %copy-done.4, f32[560,128]{1,0:T(8,128)} %copy-done.5), custom_call_target="tpu_custom_call" | custom-call | flops 264241152 | bytes 11010048 | tf_op jit(solution)/shard_map/update/pallas_call | solution.py:404
  199.2 9.6 %all_to_all.5 = f32[8,2,96]{2,1,0:T(2,128)S(1)} all-to-all(f32[8,2,96]{2,1,0:T(2,128)} %bitcast.5), channel_id=1, replica_groups=mesh['sens'=4,'par'=8] {'par'}, dimensions={0} | all-to-all | bytes 12288 | tf_op jit(solution)/shard_map/all_to_all | solution.py:414
  208.8 0.6 reduce_sum.9
  (16 shorter events, 0.1 us)
Async XLA Ops:
  32.1 13.7 %collective-permute-start = (f32[4,224,128]{2,1,0:T(8,128)}, f32[4,224,128]{2,1,0:T(8,128)S(1)}, u32[]{:S(2)}, u32[]{:S(2)}) collective-permute-start(f32[4,224,128]{2,1,0:T(8,128)} %get-tuple-element.24), channel_id=1, source_target_pairs={{0,8},{8,0},{16,24},{24,16},{1,9},{9,1},{17,25},{25,17},{2,10},{10... | collective-permute-start | bytes 1376264 | tf_op jit(solution)/shard_map/ppermute | solution.py:284
  35.1 13.7 %collective-permute-start.5 = (f32[4,224,128]{2,1,0:T(8,128)}, f32[4,224,128]{2,1,0:T(8,128)S(1)}, u32[]{:S(2)}, u32[]{:S(2)}) collective-permute-start(f32[4,224,128]{2,1,0:T(8,128)} %get-tuple-element.26), channel_id=1, source_target_pairs={{0,16},{8,24},{16,0},{24,8},{1,17},{9,25},{17,1},{25,9},{2,18},{10... | collective-permute-start | bytes 1376264 | tf_op jit(solution)/shard_map/ppermute | solution.py:284
  45.8 11.9 %copy-start.12 = (s32[600]{0:T(1024)S(1)}, s32[600]{0:T(1024)}, u32[]{:S(2)}) copy-start(s32[600]{0:T(1024)} %param.15) | copy-start | bytes 7204
  46.9 6.9 %collective-permute-start.1 = (f32[2,224,128]{2,1,0:T(8,128)S(1)}, f32[2,224,128]{2,1,0:T(8,128)S(1)}, u32[]{:S(2)}, u32[]{:S(2)}) collective-permute-start(f32[2,224,128]{2,1,0:T(8,128)S(1)} %slice.33), channel_id=1, source_target_pairs={{0,16},{8,24},{16,0},{24,8},{1,17},{9,25},{17,1},{25,9},{2,18},{10... | collective-permute-start | bytes 688136 | tf_op jit(solution)/shard_map/ppermute | solution.py:285
  49.9 6.3 %collective-permute-start.6 = (f32[2,224,128]{2,1,0:T(8,128)S(1)}, f32[2,224,128]{2,1,0:T(8,128)S(1)}, u32[]{:S(2)}, u32[]{:S(2)}) collective-permute-start(f32[2,224,128]{2,1,0:T(8,128)S(1)} %slice.35), channel_id=1, source_target_pairs={{0,8},{8,0},{16,24},{24,16},{1,9},{9,1},{17,25},{25,17},{2,10},{10... | collective-permute-start | bytes 688136 | tf_op jit(solution)/shard_map/ppermute | solution.py:285
  53.8 15.5 %copy-start.1 = (f32[2,224,128]{2,1,0:T(8,128)}, f32[2,224,128]{2,1,0:T(8,128)S(1)}, u32[]{:S(2)}) copy-start(f32[2,224,128]{2,1,0:T(8,128)S(1)} %slice_add_fusion.2.rest_0_) | copy-start | bytes 688132
  53.8 16.6 %collective-permute-start.2 = (f32[2,224,128]{2,1,0:T(8,128)S(1)}, f32[2,224,128]{2,1,0:T(8,128)S(1)}, u32[]{:S(2)}, u32[]{:S(2)}) collective-permute-start(f32[2,224,128]{2,1,0:T(8,128)S(1)} %slice_add_fusion.2.rest_0_), channel_id=1, source_target_pairs={{0,16},{8,24},{16,0},{24,8},{1,17},{9,25},{17,1},{25,9},{2,18},{10... | collective-permute-start | bytes 688136 | tf_op jit(solution)/shard_map/ppermute | solution.py:286
  56.2 13.7 %copy-start.2 = (f32[2,224,128]{2,1,0:T(8,128)}, f32[2,224,128]{2,1,0:T(8,128)S(1)}, u32[]{:S(2)}) copy-start(f32[2,224,128]{2,1,0:T(8,128)S(1)} %slice_add_fusion.1.rest_4_) | copy-start | bytes 688132
  56.2 15.7 %collective-permute-start.7 = (f32[2,224,128]{2,1,0:T(8,128)S(1)}, f32[2,224,128]{2,1,0:T(8,128)S(1)}, u32[]{:S(2)}, u32[]{:S(2)}) collective-permute-start(f32[2,224,128]{2,1,0:T(8,128)S(1)} %slice_add_fusion.1.rest_4_), channel_id=1, source_target_pairs={{0,8},{8,0},{16,24},{24,16},{1,9},{9,1},{17,25},{25,17},{2,10},{10... | collective-permute-start | bytes 688136 | tf_op jit(solution)/shard_map/ppermute | solution.py:286
  69.3 39.8 %collective-permute-start.3 = (f32[2,224,128]{2,1,0:T(8,128)S(1)}, f32[2,224,128]{2,1,0:T(8,128)S(1)}, u32[]{:S(2)}, u32[]{:S(2)}) collective-permute-start(f32[2,224,128]{2,1,0:T(8,128)S(1)} %slice_add_fusion.2.rest_0_), channel_id=1, source_target_pairs={{0,8},{8,0},{16,24},{24,16},{1,9},{9,1},{17,25},{25,17},{2,10},{10... | collective-permute-start | bytes 688136 | tf_op jit(solution)/shard_map/ppermute | solution.py:287
  69.9 39.3 %collective-permute-start.8 = (f32[2,224,128]{2,1,0:T(8,128)S(1)}, f32[2,224,128]{2,1,0:T(8,128)S(1)}, u32[]{:S(2)}, u32[]{:S(2)}) collective-permute-start(f32[2,224,128]{2,1,0:T(8,128)S(1)} %slice_add_fusion.1.rest_4_), channel_id=1, source_target_pairs={{0,16},{8,24},{16,0},{24,8},{1,17},{9,25},{17,1},{25,9},{2,18},{10... | collective-permute-start | bytes 688136 | tf_op jit(solution)/shard_map/ppermute | solution.py:287
  70.4 38.7 %copy-start.6 = (f32[2,224,128]{2,1,0:T(8,128)}, f32[2,224,128]{2,1,0:T(8,128)S(1)}, u32[]{:S(2)}) copy-start(f32[2,224,128]{2,1,0:T(8,128)S(1)} %collective-permute-done.2.rest_1_) | copy-start | bytes 688132
  70.4 38.7 %collective-permute-start.4 = (f32[2,224,128]{2,1,0:T(8,128)S(1)}, f32[2,224,128]{2,1,0:T(8,128)S(1)}, u32[]{:S(2)}, u32[]{:S(2)}) collective-permute-start(f32[2,224,128]{2,1,0:T(8,128)S(1)} %collective-permute-done.2.rest_1_), channel_id=1, source_target_pairs={{0,8},{8,0},{16,24},{24,16},{1,9},{9,1},{17,25},{25,17},{2,10},{10... | collective-permute-start | bytes 688136 | tf_op jit(solution)/shard_map/ppermute | solution.py:288
  71.9 37.3 %copy-start.7 = (f32[2,224,128]{2,1,0:T(8,128)}, f32[2,224,128]{2,1,0:T(8,128)S(1)}, u32[]{:S(2)}) copy-start(f32[2,224,128]{2,1,0:T(8,128)S(1)} %collective-permute-done.7.rest_5_) | copy-start | bytes 688132
  71.9 37.3 %collective-permute-start.9 = (f32[2,224,128]{2,1,0:T(8,128)S(1)}, f32[2,224,128]{2,1,0:T(8,128)S(1)}, u32[]{:S(2)}, u32[]{:S(2)}) collective-permute-start(f32[2,224,128]{2,1,0:T(8,128)S(1)} %collective-permute-done.7.rest_5_), channel_id=1, source_target_pairs={{0,16},{8,24},{16,0},{24,8},{1,17},{9,25},{17,1},{25,9},{2,18},{10... | collective-permute-start | bytes 688136 | tf_op jit(solution)/shard_map/ppermute | solution.py:288
  109.2 0.7 copy-start.8
  109.2 0.8 copy-start.9
  109.2 0.8 copy-start.10
  109.2 0.9 copy-start.11
  142.7 3.0 %collective-permute-start.10 = (f32[2240,128]{1,0:T(8,128)}, f32[2240,128]{1,0:T(8,128)S(1)}, u32[]{:S(2)}, u32[]{:S(2)}) collective-permute-start(f32[2240,128]{1,0:T(8,128)} %get-tuple-element.28), channel_id=1, source_target_pairs={{0,1},{1,0},{2,3},{3,2},{4,5},{5,4},{6,7},{7,6},{8,9},{9,8},{10,11... | collective-permute-start | bytes 3440648 | tf_op jit(solution)/shard_map/ppermute | solution.py:396
  147.2 11.0 %collective-permute-start.13 = (f32[560,128]{1,0:T(8,128)S(1)}, f32[560,128]{1,0:T(8,128)S(1)}, u32[]{:S(2)}, u32[]{:S(2)}) collective-permute-start(f32[560,128]{1,0:T(8,128)S(1)} %get-tuple-element.30), channel_id=1, source_target_pairs={{0,6},{1,7},{2,0},{3,1},{4,2},{5,3},{6,4},{7,5},{8,14},{9,15},{10,... | collective-permute-start | bytes 860168 | tf_op jit(solution)/shard_map/ppermute | solution.py:400
  150.8 24.7 %collective-permute-start.12 = (f32[560,128]{1,0:T(8,128)S(1)}, f32[560,128]{1,0:T(8,128)S(1)}, u32[]{:S(2)}, u32[]{:S(2)}) collective-permute-start(f32[560,128]{1,0:T(8,128)S(1)} %get-tuple-element.31), channel_id=1, source_target_pairs={{0,4},{1,5},{2,6},{3,7},{4,0},{5,1},{6,2},{7,3},{8,12},{9,13},{10,... | collective-permute-start | bytes 860168 | tf_op jit(solution)/shard_map/ppermute | solution.py:400
  150.8 24.7 %collective-permute-start.11 = (f32[560,128]{1,0:T(8,128)S(1)}, f32[560,128]{1,0:T(8,128)S(1)}, u32[]{:S(2)}, u32[]{:S(2)}) collective-permute-start(f32[560,128]{1,0:T(8,128)S(1)} %get-tuple-element.29), channel_id=1, source_target_pairs={{0,2},{1,3},{2,4},{3,5},{4,6},{5,7},{6,0},{7,1},{8,10},{9,11},{10,... | collective-permute-start | bytes 860168 | tf_op jit(solution)/shard_map/ppermute | solution.py:400
  175.6 14.5 %copy-start = (f32[560,128]{1,0:T(8,128)}, f32[560,128]{1,0:T(8,128)S(1)}, u32[]{:S(2)}) copy-start(f32[560,128]{1,0:T(8,128)S(1)} %fusion.1.rest_0_) | copy-start | bytes 860164
  175.6 9.8 %collective-permute-start.14 = (f32[560,128]{1,0:T(8,128)S(1)}, f32[560,128]{1,0:T(8,128)S(1)}, u32[]{:S(2)}, u32[]{:S(2)}) collective-permute-start(f32[560,128]{1,0:T(8,128)S(1)} %fusion.1.rest_0_), channel_id=1, source_target_pairs={{0,8},{8,0},{16,24},{24,16},{1,9},{9,1},{17,25},{25,17},{2,10},{10... | collective-permute-start | bytes 860168 | tf_op jit(solution)/shard_map/ppermute | solution.py:401
  176.2 13.9 %collective-permute-start.15 = (f32[560,128]{1,0:T(8,128)S(1)}, f32[560,128]{1,0:T(8,128)S(1)}, u32[]{:S(2)}, u32[]{:S(2)}) collective-permute-start(f32[560,128]{1,0:T(8,128)S(1)} %fusion.1.rest_0_), channel_id=1, source_target_pairs={{0,16},{8,24},{16,0},{24,8},{1,17},{9,25},{17,1},{25,9},{2,18},{10... | collective-permute-start | bytes 860168 | tf_op jit(solution)/shard_map/ppermute | solution.py:401
  176.7 13.4 %collective-permute-start.16 = (f32[560,128]{1,0:T(8,128)S(1)}, f32[560,128]{1,0:T(8,128)S(1)}, u32[]{:S(2)}, u32[]{:S(2)}) collective-permute-start(f32[560,128]{1,0:T(8,128)S(1)} %fusion.1.rest_0_), channel_id=1, source_target_pairs={{0,24},{8,16},{16,8},{24,0},{1,25},{9,17},{17,9},{25,1},{2,26},{10... | collective-permute-start | bytes 860168 | tf_op jit(solution)/shard_map/ppermute | solution.py:401
  185.5 4.7 %copy-start.3 = (f32[560,128]{1,0:T(8,128)}, f32[560,128]{1,0:T(8,128)S(1)}, u32[]{:S(2)}) copy-start(f32[560,128]{1,0:T(8,128)S(1)} %collective-permute-done.14.rest_1_) | copy-start | bytes 860164
  190.1 0.7 copy-start.4
  190.1 0.8 copy-start.5

commit v2 on v1

v2 whole, which is shorter than its diff:
```python
import functools

import jax
import jax.numpy as jnp
import numpy as np
from jax import lax
from jax.experimental import pallas as pl
from jax.experimental.pallas import tpu as pltpu
from jax.sharding import PartitionSpec as P

F32 = jnp.float32
BF16 = jnp.bfloat16
LANES = 128


def round_up(value, step):
    return (value + step - 1) // step * step


def split(value):
    high = value.astype(BF16)
    low = (value - high.astype(F32)).astype(BF16)
    return high, low


def dot(left, right):
    return lax.dot_general(left, right, (((1,), (0,)), ((), ())), preferred_element_type=F32)


def dot_nt(left, right):
    return lax.dot_general(left, right, (((1,), (1,)), ((), ())), preferred_element_type=F32)


def split_host(table):
    high = table.astype(np.float32).astype(jnp.bfloat16)
    low = (table - high.astype(np.float64)).astype(jnp.bfloat16)
    return high, low


def forward_table(steps, bins, padded):
    length = 2 * steps
    phase = 2.0 * np.pi * ((np.arange(bins)[:, None] * np.arange(steps)[None, :]) % length) / length
    table = np.zeros((2 * padded, steps))
    table[:bins] = np.cos(phase)
    table[padded : padded + bins] = -np.sin(phase)
    return table


def inverse_table(steps, bins, padded):
    length = 2 * steps
    phase = 2.0 * np.pi * ((np.arange(steps)[:, None] * np.arange(bins)[None, :]) % length) / length
    weight = np.full((bins,), 2.0)
    weight[0] = 1.0
    weight[-1] = 1.0
    weight = weight / length
    table = np.zeros((steps, 2 * padded))
    table[:, :bins] = np.cos(phase) * weight
    table[:, padded : padded + bins] = -np.sin(phase) * weight
    return table


def block_of(bins, most):
    return max(size for size in range(1, most + 1) if bins % size == 0)


class Packing:
    def __init__(self, cols, sens_dev):
        self.cols = cols
        self.sens_dev = sens_dev
        self.full = sens_dev // LANES
        self.rest = sens_dev % LANES
        self.share = LANES // self.rest if self.rest else 1
        self.rest_rows = -(-cols // self.share) if self.rest else 0
        self.rows = self.full * cols + self.rest_rows
        self.width = LANES * (self.full + (1 if self.rest else 0))


def lane_tiles(value):
    rows, columns = value.shape
    tiles = []
    for start in range(0, columns, LANES):
        tile = value[:, start : start + LANES]
        short = LANES - tile.shape[1]
        if short:
            tile = jnp.concatenate([tile, jnp.zeros((rows, short), value.dtype)], axis=1)
        tiles.append(tile)
    return tiles


def spec_copies(hbm_refs, vmem_refs, sems, chunk, block):
    part = pl.ds(chunk * block, block)
    return [
        pltpu.make_async_copy(hbm.at[part], vmem.at[part], sems.at[j, chunk])
        for j, (hbm, vmem) in enumerate(zip(hbm_refs, vmem_refs))
    ]


def start_all(hbm_refs, vmem_refs, sems, chunks, block):
    for chunk in range(chunks):
        for copy in spec_copies(hbm_refs, vmem_refs, sems, chunk, block):
            copy.start()


def adjoint_kernel(mask_ref, rec_ref, fh_ref, fl_ref, ih_ref, il_ref, sr_hbm, si_hbm, *rest):
    outs, (sr_ref, si_ref, sems, spread, rec_spec, adj) = rest[:-6], rest[-6:]
    sens_dev, cols, steps = rec_ref.shape
    bins, _, par_dev = sr_ref.shape
    chunks = sems.shape[1]
    block = bins // chunks
    padded = adj.shape[0] // cols // 2
    tall = 2 * padded
    half = cols // 2
    start_all((sr_hbm, si_hbm), (sr_ref, si_ref), sems, chunks, block)

    every = rec_ref[...].reshape(sens_dev * cols, steps)
    for f, tile in enumerate(lane_tiles(every)):
        spread[f] = tile
    for row in list(range(bins, padded)) + list(range(padded + bins, tall)):
        adj[pl.ds(row, cols, stride=tall), :] = jnp.zeros((cols, par_dev), F32)

    def column(c, _):
        own = [spread[f, pl.ds(c, sens_dev, stride=cols), :] for f in range(spread.shape[0])]
        rh, rl = split(jnp.concatenate(own, axis=1)[:, :steps])
        fh, fl = fh_ref[...], fl_ref[...]
        value = dot_nt(fh, rh) + (dot_nt(fl, rh) + dot_nt(fh, rl))
        for f, tile in enumerate(lane_tiles(value)):
            rec_spec[f, pl.ds(c, bins, stride=2 * cols), :] = tile[:bins]
            rec_spec[f, pl.ds(cols + c, bins, stride=2 * cols), :] = tile[padded : padded + bins]
        return 0

    lax.fori_loop(0, cols, column, 0)

    def chunk_body(chunk, _):
        for copy in spec_copies((sr_hbm, si_hbm), (sr_ref, si_ref), sems, chunk, block):
            copy.wait()
        for i in range(block):
            w = chunk * block + i
            at = pl.ds(pl.multiple_of(w * 2 * cols, 8), 2 * cols)
            x = jnp.concatenate([rec_spec[f, at, :] for f in range(rec_spec.shape[0])], axis=1)[:, :sens_dev]
            xh, xl = split(x)
            sh, sl = split(jnp.concatenate([sr_ref[w], si_ref[w]], axis=1))
            both = dot(jnp.concatenate([xh, xl], axis=0), sh)
            value = both[: 2 * cols] + both[2 * cols :] + dot(xh, sl)
            adj[pl.ds(w, cols, stride=tall), :] = value[:cols, :par_dev] + value[cols:, par_dev:]
            adj[pl.ds(padded + w, cols, stride=tall), :] = value[cols:, :par_dev] - value[:cols, par_dev:]
        return 0

    lax.fori_loop(0, chunks, chunk_body, 0)

    per = cols // len(outs)
    for o, out in enumerate(outs):
        def pair(j, _):
            wide = []
            for e in range(2):
                k = o * per + 2 * j + e
                c = jnp.bitwise_xor(k, mask_ref[o * per // half])
                wide.append(adj[pl.ds(pl.multiple_of(c * tall, 8), tall), :])
            ah, al = split(jnp.concatenate(wide, axis=1))
            ih, il = ih_ref[...], il_ref[...]
            value = dot(ih, ah) + (dot(il, ah) + dot(ih, al))
            out[2 * j] = value[:, :par_dev]
            out[2 * j + 1] = value[:, par_dev:]
            return 0

        lax.fori_loop(0, per // 2, pair, 0)


def forward_kernel(packing, mask_ref, th_ref, tl_ref, ih_ref, il_ref, *rest):
    (keep_ref, send_ref, sr_ref, si_ref, sems, whole_ref, field, pred, left) = rest[-9:]
    sr_hbm, si_hbm = rest[-11:-9]
    pieces = rest[:-11]
    cols = packing.cols
    bins, sens_dev, par_dev = sr_ref.shape
    chunks = sems.shape[1]
    block = bins // chunks
    padded = pred.shape[1] // cols // 2
    tall = 2 * padded
    half = cols // 2
    full, width = packing.full, packing.full * LANES
    start_all((sr_hbm, si_hbm), (sr_ref, si_ref), sems, chunks, block)

    per = cols // len(pieces)
    for p, piece in enumerate(pieces):
        for e in range(per):
            k = p * per + e
            whole_ref[jnp.bitwise_xor(k, mask_ref[k // half])] = piece[e]
    for row in list(range(bins, padded)) + list(range(padded + bins, tall)):
        for f in range(pred.shape[0]):
            pred[f, pl.ds(row, cols, stride=tall), :] = jnp.zeros((cols, LANES), F32)

    def transform(j, _):
        ah, al = split(jnp.concatenate([whole_ref[2 * j], whole_ref[2 * j + 1]], axis=1))
        th, tl = th_ref[...], tl_ref[...]
        value = dot(th, ah) + (dot(tl, ah) + dot(th, al))
        for e in range(2):
            c = 2 * j + e
            part = value[:, e * par_dev : (e + 1) * par_dev]
            field[pl.ds(c, bins, stride=2 * cols), :] = part[:bins]
            field[pl.ds(cols + c, bins, stride=2 * cols), :] = part[padded : padded + bins]
        return 0

    lax.fori_loop(0, cols // 2, transform, 0)

    def chunk_body(chunk, _):
        for copy in spec_copies((sr_hbm, si_hbm), (sr_ref, si_ref), sems, chunk, block):
            copy.wait()
        for i in range(block):
            w = chunk * block + i
            x = field[pl.ds(pl.multiple_of(w * 2 * cols, 8), 2 * cols), :]
            turned = jnp.concatenate([-x[cols:], x[:cols]], axis=0)
            xh, xl = split(jnp.concatenate([x, turned], axis=1))
            sh, sl = split(jnp.concatenate([sr_ref[w], si_ref[w]], axis=1))
            both = dot_nt(jnp.concatenate([xh, xl], axis=0), sh)
            value = both[: 2 * cols] + both[2 * cols :] + dot_nt(xh, sl)
            for f, tile in enumerate(lane_tiles(value)):
                pred[f, pl.ds(w, cols, stride=tall), :] = tile[:cols]
                pred[f, pl.ds(padded + w, cols, stride=tall), :] = tile[cols:]
        return 0

    lax.fori_loop(0, chunks, chunk_body, 0)

    rows = packing.rows
    count = ih_ref.shape[0] // 2
    for c in range(cols):
        wide = [pred[f, c * tall : (c + 1) * tall, :] for f in range(pred.shape[0])]
        ph, pl_low = split(jnp.concatenate(wide, axis=1))
        ih, il = ih_ref[...], il_ref[...]
        value = dot(ih, ph) + (dot(il, ph) + dot(ih, pl_low))
        for f in range(full):
            part = value[:, f * LANES : (f + 1) * LANES]
            keep_ref[pl.ds(c * full + f, count, stride=rows), :] = part[:count]
            send_ref[pl.ds(c * full + f, count, stride=rows), :] = part[count:]
        if packing.rest:
            place = c % packing.share
            part = value[:, width:]
            if place:
                part = pltpu.roll(part, place * packing.rest, 1)
                left[...] += part
            else:
                left[...] = part
            if place == packing.share - 1 or c == cols - 1:
                row = cols * full + c // packing.share
                keep_ref[pl.ds(row, count, stride=rows), :] = left[:count]
                send_ref[pl.ds(row, count, stride=rows), :] = left[count:]


def prepare_kernel(packing, index_ref, map_ref, prior_ref, fh_ref, fl_ref, inv_ref, rows_ref,
                   oh_ref, ol_ref, th_ref, tl_ref, ih_ref, il_ref, select, table):
    step = pl.program_id(0)
    blocks = oh_ref.shape[2] // packing.width
    times = inv_ref.shape[1]

    @pl.when(step == 0)
    def _():
        lane = lax.broadcasted_iota(jnp.int32, (1, packing.width), 1)
        width = packing.full * LANES
        if packing.rest:
            beyond = lane - width
            folded = width + lax.rem(jnp.maximum(beyond, 0), packing.rest)
            local = jnp.where(beyond >= 0, folded, lane)
            valid = beyond < packing.share * packing.rest
        else:
            local = lane
            valid = lane >= 0
        for m in range(blocks):
            owner = jnp.bitwise_xor(index_ref[0], m)
            wanted = jnp.where(valid, owner * packing.sens_dev + local, -1)
            hit = map_ref[...] == wanted
            select[:, m * packing.width : (m + 1) * packing.width] = jnp.where(hit, 1.0, 0.0).astype(BF16)
        ph, pl_low = split(prior_ref[...])
        folded_table = dot_nt(fh_ref[...], ph) + (dot_nt(fl_ref[...], ph) + dot_nt(fh_ref[...], pl_low))
        th, tl = split(folded_table)
        th_ref[...] = th
        tl_ref[...] = tl
        par = inv_ref.shape[0]
        pairs = par // 2
        for r in range(2):
            for d in range(pairs):
                z = lax.rem(index_ref[1] // 2 + d, pairs)
                core = jnp.bitwise_xor(lax.rem(index_ref[1], 2), r)
                j = r * pairs + d
                table[j * times : (j + 1) * times, :] = inv_ref[2 * z + core]
        ih, il = split(table[...])
        ih_ref[...] = ih
        il_ref[...] = il

    group, count, sensors = rows_ref.shape
    high, low = split(rows_ref[...].reshape(group * count, sensors))
    moved = dot(jnp.concatenate([high, low], axis=0), select[...]).astype(BF16)
    oh_ref[...] = moved[: group * count].reshape(oh_ref.shape)
    ol_ref[...] = moved[group * count :].reshape(ol_ref.shape)


def update_kernel(packing, oh_hbm, ol_hbm, *rest):
    gathered, (out_ref, oh_ref, ol_ref, sems) = rest[:-4], rest[-4:]
    times = oh_ref.shape[0]
    chunks = sems.shape[1]
    start_all((oh_hbm, ol_hbm), (oh_ref, ol_ref), sems, chunks, times // chunks)
    cols, rows, full = packing.cols, packing.rows, packing.full
    total = jnp.zeros(out_ref.shape, F32)
    if packing.rest:
        row = lax.broadcasted_iota(jnp.int32, (cols, LANES), 0)
        lane = lax.broadcasted_iota(jnp.int32, (cols, LANES), 1)
        own = lax.rem(row, packing.share) == lane // packing.rest
        shared = row // packing.share

    group = times // chunks

    def body(i, total):
        for copy in spec_copies((oh_hbm, ol_hbm), (oh_ref, ol_ref), sems, i, group):
            copy.wait()
        base = i * (group * rows)
        if group * rows % 8 == 0:
            base = pl.multiple_of(base, 8)
        for m, ref in enumerate(gathered):
            block = ref[pl.ds(base, group * rows), :]
            place = slice(m * packing.width, (m + 1) * packing.width)
            for g in range(group):
                held = block[g * rows : (g + 1) * rows]
                parts = []
                if full == 1:
                    parts.append(held[:cols])
                elif full > 1:
                    wide = held[: cols * full].reshape(cols, full, LANES)
                    parts.extend(wide[:, f, :] for f in range(full))
                if packing.rest:
                    spread = jnp.zeros((cols, LANES), F32)
                    for j in range(packing.rest_rows):
                        line = held[cols * full + j : cols * full + j + 1]
                        spread = jnp.where(own & (shared == j), line, spread)
                    parts.append(spread)
                xh, xl = split(jnp.concatenate(parts, axis=1))
                t = i * group + g
                both = dot_nt(jnp.concatenate([xh, xl], axis=0), oh_ref[t, :, place])
                total = total + (both[:cols] + both[cols:] + dot_nt(xh, ol_ref[t, :, place]))
        return total

    out_ref[...] = lax.fori_loop(0, chunks, body, total)


def whole(array):
    return pl.BlockSpec(array.shape, lambda *_: (0,) * array.ndim)


def swap(size, mask):
    return [(k, k ^ mask) for k in range(size)]


def reduce_quarters(keep, send, first, second, size):
    near = keep + lax.ppermute(send, "sens", swap(size, first))
    return near


def reduce_rest(near, first, second, size):
    per = near.shape[0] // 2
    here = near[:per] + lax.ppermute(near[per:], "sens", swap(size, second))
    over = lax.ppermute(here, "sens", swap(size, second))
    back = lax.ppermute(here, "sens", swap(size, first))
    return [here, over, back, lax.ppermute(over, "sens", swap(size, first))]


def shards(records, spec_real, spec_imag, prior_cov, sensor_map, inverse_rows):
    cols, sens_dev, steps = records.shape
    bins, _, par_dev = spec_real.shape
    padded = round_up(bins, 8)
    sens, par = lax.axis_size("sens"), lax.axis_size("par")
    sens_index, par_index = lax.axis_index("sens"), lax.axis_index("par")
    packing = Packing(cols, sens_dev)
    rows_dev, times, sensors = inverse_rows.shape
    quarters = sens == 4 and cols % 8 == 0
    limit = 58 * 2**20

    fwd = forward_table(steps, bins, padded)
    inv = inverse_table(steps, bins, padded)
    fh, fl = (jnp.asarray(part) for part in split_host(fwd))
    ih, il = (jnp.asarray(part) for part in split_host(inv))
    inv_blocks = jnp.asarray(inv.reshape(par, times, 2 * padded).astype(np.float32))

    if quarters:
        bit0, bit1 = sens_index & 1, sens_index >> 1
        unit = cols // 8
        mask = jnp.stack([(2 * bit0 + bit1) * unit, (2 * bit1 + bit0) * unit]).astype(jnp.int32)
        n_out = 4
    else:
        mask = jnp.zeros((2,), jnp.int32)
        n_out = 1

    by_sensor = jnp.transpose(records, (1, 0, 2))
    by_time = jnp.transpose(inverse_rows, (1, 0, 2))
    block = block_of(bins, 15)
    outside = pl.BlockSpec(memory_space=pltpu.HBM)
    spec_scratch = [
        pltpu.VMEM(spec_real.shape, F32),
        pltpu.VMEM(spec_real.shape, F32),
        pltpu.SemaphoreType.DMA((2, bins // block)),
    ]
    sens_tiles = -(-sens_dev // LANES)
    smem = pl.BlockSpec(memory_space=pltpu.SMEM)
    phase_cost = pl.CostEstimate(
        flops=24 * cols * bins * sens_dev * par_dev, bytes_accessed=8 * bins * sens_dev * par_dev, transcendentals=0
    )
    out_a = [jax.ShapeDtypeStruct((cols // n_out, steps, par_dev), F32)] * n_out
    parts = pl.pallas_call(
        adjoint_kernel,
        in_specs=[smem, whole(by_sensor), whole(fh), whole(fl), whole(ih), whole(il), outside, outside],
        out_specs=[whole(shape) for shape in out_a],
        out_shape=out_a,
        scratch_shapes=spec_scratch
        + [
            pltpu.VMEM((-(-steps // LANES), sens_dev * cols, LANES), F32),
            pltpu.VMEM((sens_tiles, bins * 2 * cols, LANES), F32),
            pltpu.VMEM((cols * 2 * padded, par_dev), F32),
        ],
        compiler_params=pltpu.CompilerParams(vmem_limit_bytes=limit),
        cost_estimate=phase_cost,
        name="adjoint",
    )(mask, by_sensor, fh, fl, ih, il, spec_real, spec_imag)

    index = jnp.stack([sens_index, par_index]).astype(jnp.int32)
    *parts, index = lax.optimization_barrier((*parts, index))
    time_block = block_of(times, 4)
    width = sens * packing.width
    moved = jax.ShapeDtypeStruct((times, rows_dev, width), BF16)
    folded = jax.ShapeDtypeStruct((2 * padded, steps), BF16)
    turned = jax.ShapeDtypeStruct((steps, 2 * padded), BF16)
    map_column = sensor_map.reshape(sensors, 1)
    oh, ol, th, tl, ih2, il2 = pl.pallas_call(
        functools.partial(prepare_kernel, packing),
        grid=(times // time_block,),
        in_specs=[
            smem,
            whole(map_column),
            whole(prior_cov),
            whole(fh),
            whole(fl),
            whole(inv_blocks),
            pl.BlockSpec((time_block, rows_dev, sensors), lambda i: (i, 0, 0)),
        ],
        out_specs=[pl.BlockSpec((time_block, rows_dev, width), lambda i: (i, 0, 0))] * 2
        + [whole(folded)] * 2
        + [whole(turned)] * 2,
        out_shape=[moved, moved, folded, folded, turned, turned],
        scratch_shapes=[pltpu.VMEM((sensors, width), BF16), pltpu.VMEM((steps, 2 * padded), F32)],
        compiler_params=pltpu.CompilerParams(vmem_limit_bytes=limit),
        cost_estimate=pl.CostEstimate(
            flops=4 * rows_dev * times * sensors * width, bytes_accessed=8 * rows_dev * times * sensors, transcendentals=0
        ),
        name="prepare",
    )(index, map_column, prior_cov, fh, fl, inv_blocks, by_time)

    if quarters:
        near0 = reduce_quarters(parts[0], parts[1], 1, 2, sens)
        near1 = reduce_quarters(parts[2], parts[3], 2, 1, sens)
        near0, near1, th = lax.optimization_barrier((near0, near1, th))
        pieces = reduce_rest(near0, 1, 2, sens) + reduce_rest(near1, 2, 1, sens)
    else:
        pieces = [lax.psum(parts[0], "sens")]

    shard_rows = times * packing.rows
    half = jax.ShapeDtypeStruct((par // 2 * shard_rows, LANES), F32)
    keep, send = pl.pallas_call(
        functools.partial(forward_kernel, packing),
        in_specs=[smem, whole(th), whole(tl), whole(ih2), whole(il2)]
        + [whole(piece) for piece in pieces]
        + [outside, outside],
        out_specs=[whole(half)] * 2,
        out_shape=[half, half],
        scratch_shapes=spec_scratch
        + [
            pltpu.VMEM((cols, steps, par_dev), F32),
            pltpu.VMEM((bins * 2 * cols, par_dev), F32),
            pltpu.VMEM((sens_tiles, cols * 2 * padded, LANES), F32),
            pltpu.VMEM((steps, LANES), F32),
        ],
        compiler_params=pltpu.CompilerParams(vmem_limit_bytes=limit),
        cost_estimate=phase_cost,
        name="forward",
    )(mask, th, tl, ih2, il2, *pieces, spec_real, spec_imag)

    pair = keep + lax.ppermute(send, "par", swap(par, 1))
    mine = pair[:shard_rows]
    for d in range(1, par // 2):
        there = pair[d * shard_rows : (d + 1) * shard_rows]
        mine = mine + lax.ppermute(there, "par", [(k, (k + 2 * d) % par) for k in range(par)])
    gathered = [mine] + [lax.ppermute(mine, "sens", swap(sens, m)) for m in range(1, sens)]

    result = jax.ShapeDtypeStruct((cols, rows_dev), F32)
    partial = pl.pallas_call(
        functools.partial(update_kernel, packing),
        in_specs=[outside, outside] + [whole(part) for part in gathered],
        out_shape=result,
        scratch_shapes=[
            pltpu.VMEM(oh.shape, BF16),
            pltpu.VMEM(ol.shape, BF16),
            pltpu.SemaphoreType.DMA((2, times // block_of(times, 2))),
        ],
        compiler_params=pltpu.CompilerParams(vmem_limit_bytes=limit),
        cost_estimate=pl.CostEstimate(
            flops=6 * rows_dev * times * cols * width, bytes_accessed=4 * rows_dev * times * width, transcendentals=0
        ),
        name="update",
    )(oh, ol, *gathered)
    per_dev = cols // par
    spread = lax.all_to_all(partial.reshape(par, per_dev, rows_dev), "par", 0, 0)
    return jnp.sum(spread, axis=0)


def solution(mesh):
    return jax.shard_map(
        shards,
        mesh=mesh,
        in_specs=(
            P(None, "sens", None),
            P(None, "sens", "par"),
            P(None, "sens", "par"),
            P(),
            P(),
            P("sens", "par", None),
        ),
        out_specs=P("par", "sens"),
        check_vma=False,
    )
```

time: 210 us -> 170 us (0.81)
  Pallas kernels: 103 us -> 79 us
  local copies, waits for them, and re-layouts: 17.3 us -> 2.51 us
  waiting for transfers between devices: 50 us -> 55.9 us
  starting transfers between devices: 23.2 us -> 19.7 us
    pallas_call x4, Pallas kernels: 103 us -> 79 us  [the longest x1 29.4 us: shards(): pl.pallas_call(adjoint_kernel, in_specs=[smem, whole(by_sensor), whole(fh...]
    unnamed x28 -> x30, local copies, waits for them, and re-layouts: 16.4 us -> 1.54 us
    ppermute x8, waiting for transfers between devices: 3.16 us -> 16 us  [the longest x2 6.12 us: reduce_rest(): here = near[:per] + lax.ppermute(near[per:], 'sens', swap(size, second))]
    ppermute x2, waiting for transfers between devices: 9.21 us -> 0.01 us  [reduce_quarters(): near = keep + lax.ppermute(send, 'sens', swap(size, first))]
    ppermute x8, starting transfers between devices: 10.5 us -> 6.89 us  [the longest x2 3.19 us: reduce_rest(): back = lax.ppermute(here, 'sens', swap(size, first))]
  transfers between devices with their start and end apart: 17 -> 17, of which waited for: 8 -> 11; matrix products, arithmetic and copies ran while one was open for 7% -> 1% of each run, Pallas kernels for 17% -> 8%
where the time goes in v2:
time: 170 us
  Pallas kernels  79 us (46%)
  waiting for transfers between devices  55.9 us (33%)
  starting transfers between devices  19.7 us (12%)
  blocking collectives  8.8 us (5%)
  other arithmetic  3.49 us (2%)
  local copies, waits for them, and re-layouts  2.51 us (1%)
    pallas_call x1, Pallas kernels, shards(): pl.pallas_call(adjoint_kernel, in_specs=[smem, whole(by_sensor), whole(fh...  29.4 us
    pallas_call x1, Pallas kernels, shards(): pl.pallas_call(functools.partial(forward_kernel, packing), in_specs=[smem...  27.3 us
    ppermute x3, waiting for transfers between devices, shards(): lax.ppermute(there, 'par', [(k, (k + 2 * d) % par) for k in range(par)])  24.6 us
    pallas_call x1, Pallas kernels, shards(): pl.pallas_call(functools.partial(prepare_kernel, packing), grid=(times //...  14.2 us
    ppermute x3, waiting for transfers between devices, shards(): lax.ppermute(mine, 'sens', swap(sens, m))  12.3 us
    all_to_all x1, blocking collectives, shards(): lax.all_to_all(partial.reshape(par, per_dev, rows_dev), 'par', 0, 0)  8.8 us
    pallas_call x1, Pallas kernels, shards(): pl.pallas_call(functools.partial(update_kernel, packing), in_specs=[outsi...  8.12 us
    ppermute x2, waiting for transfers between devices, reduce_rest(): here = near[:per] + lax.ppermute(near[per:], 'sens', swap(size, second))  6.12 us
  transfers between devices with their start and end apart: 17, of which 11 were waited for; matrix products, arithmetic and copies ran while one was open for 1% of the time, Pallas kernels for 8%

profile of v2, /device:TPU:0, one launch (start us, length us, event | category | flops | bytes accessed | tf_op | source)
XLA Modules:
  0.0 169.6 jit_solution(3984210704305672025)
XLA Ops:
  0.0 0.7 pad_add_fusion.mask_ref
  0.7 0.6 pad_add_fusion.1.index_ref
  1.3 29.4 %adjoint.1 = (f32[4,224,128]{2,1,0:T(8,128)}, f32[4,224,128]{2,1,0:T(8,128)}, f32[4,224,128]{2,1,0:T(8,128)}, f32[4,224,128]{2,1,0:T(8,128)}) custom-call(s32[2]{0:T(128)} %pad_add_fusion.mask_ref, f32[150,16,224]{2,1,0:T(8,128)} %bitcast.7, bf16[464,224]{1,0:T(8,128)(2,1)} %constant.24.clone.fh_ref, bf16[464,224]{1,0:T(8,128)(2,1)} %constant.25.clone.fl_ref, ...), custom_call_target="tpu_custom_call" | custom-call | flops 1658880000 | bytes 34560000 | tf_op jit(solution)/shard_map/adjoint/pallas_call | solution.py:403
  30.7 3.0 %collective-permute-start = (f32[4,224,128]{2,1,0:T(8,128)}, f32[4,224,128]{2,1,0:T(8,128)S(1)}, u32[]{:S(2)}, u32[]{:S(2)}) collective-permute-start(f32[4,224,128]{2,1,0:T(8,128)} %get-tuple-element.33), channel_id=1, source_target_pairs={{0,8},{8,0},{16,24},{24,16},{1,9},{9,1},{17,25},{25,17},{2,10},{10... | collective-permute-start | bytes 1376264 | tf_op jit(solution)/shard_map/ppermute | solution.py:350
  33.7 1.5 collective-permute-start.1
  35.2 0.0 copy-done.14
  35.2 0.9 reshape.8.map_ref
  36.1 14.2 %prepare.1 = (bf16[28,96,1024]{2,1,0:T(8,128)(2,1)}, bf16[28,96,1024]{2,1,0:T(8,128)(2,1)}, bf16[464,224]{1,0:T(8,128)(2,1)}, bf16[464,224]{1,0:T(8,128)(2,1)}, ...) custom-call(s32[2]{0:T(128)} %pad_add_fusion.1.index_ref, s32[600,1]{1,0:T(8,128)} %reshape.8.map_ref, ...), custom_call_target="tpu_custom_call" | custom-call | flops 6606028800 | bytes 12902400 | tf_op jit(solution)/shard_map/prepare/pallas_call | solution.py:427
  50.3 0.0 collective-permute-done
  50.3 0.0 copy-done.4
  50.3 0.1 add.32
  50.4 0.0 collective-permute-done.1
  50.4 0.0 copy-done.3
  50.4 0.1 add.33
  50.5 0.6 collective-permute-start.6
  51.1 0.1 collective-permute-start.2
  51.2 6.1 %collective-permute-done.6 = f32[2,224,128]{2,1,0:T(8,128)S(1)} collective-permute-done((f32[2,224,128]{2,1,0:T(8,128)S(1)}, f32[2,224,128]{2,1,0:T(8,128)S(1)}, u32[]{:S(2)}, u32[]{:S(2)}) %collective-permute-start.6) | collective-permute-done | bytes 229408 | tf_op jit(solution)/shard_map/ppermute | solution.py:356
  57.3 0.0 copy-start.1
  57.3 0.6 collective-permute-start.7
  57.9 0.0 collective-permute-done.2
  58.0 0.0 copy-start.2
  58.0 0.4 collective-permute-start.3
  58.4 1.7 collective-permute-start.8
  60.1 1.5 collective-permute-start.4
  61.6 4.4 %collective-permute-done.7.rest_5_ = f32[2,224,128]{2,1,0:T(8,128)S(1)} collective-permute-done((f32[2,224,128]{2,1,0:T(8,128)S(1)}, f32[2,224,128]{2,1,0:T(8,128)S(1)}, u32[]{:S(2)}, u32[]{:S(2)}) %collective-permute-start.7) | collective-permute-done | bytes 229408 | tf_op jit(solution)/shard_map/ppermute | solution.py:357
  66.0 0.5 collective-permute-start.9
  66.5 0.1 collective-permute-done.3.rest_1_
  66.6 1.5 collective-permute-start.5
  68.1 2.9 %collective-permute-done.8.rest_6_ = f32[2,224,128]{2,1,0:T(8,128)S(1)} collective-permute-done((f32[2,224,128]{2,1,0:T(8,128)S(1)}, f32[2,224,128]{2,1,0:T(8,128)S(1)}, u32[]{:S(2)}, u32[]{:S(2)}) %collective-permute-start.8) | collective-permute-done | bytes 229408 | tf_op jit(solution)/shard_map/ppermute | solution.py:358
  71.0 0.0 collective-permute-done.4.rest_2_
  71.0 2.5 %collective-permute-done.9.rest_7_ = f32[2,224,128]{2,1,0:T(8,128)S(1)} collective-permute-done((f32[2,224,128]{2,1,0:T(8,128)S(1)}, f32[2,224,128]{2,1,0:T(8,128)S(1)}, u32[]{:S(2)}, u32[]{:S(2)}) %collective-permute-start.9) | collective-permute-done | bytes 229408 | tf_op jit(solution)/shard_map/ppermute | solution.py:359
  73.5 0.0 collective-permute-done.5.rest_3_
  73.5 0.0 copy-done.1
  73.5 0.0 copy-done.2
  73.5 0.0 copy-done.8
  73.5 0.0 copy-done.9
  73.5 0.0 copy-done.10
  73.5 0.0 copy-done.11
  73.5 0.6 copy-done.12
  74.1 0.1 copy-done.13
  74.2 27.3 %forward.1 = (f32[2240,128]{1,0:T(8,128)}, f32[2240,128]{1,0:T(8,128)}) custom-call(s32[2]{0:T(128)} %pad_add_fusion.mask_ref, bf16[464,224]{1,0:T(8,128)(2,1)} %get-tuple-element.37.th_ref, bf16[464,224]{1,0:T(8,128)(2,1)} %get-tuple-element.38.tl_ref, bf16[224,464]{1,0:T(8,128)(2,1)} %get-tuple-element.39.ih_ref, ...), custom_call_target="tpu_custom_call" | custom-call | flops 1658880000 | bytes 34560000 | tf_op jit(solution)/shard_map/forward/pallas_call | solution.py:461
  101.6 0.1 collective-permute-start.10
  101.7 3.0 %collective-permute-done.10 = f32[2240,128]{1,0:T(8,128)S(1)} collective-permute-done((f32[2240,128]{1,0:T(8,128)}, f32[2240,128]{1,0:T(8,128)S(1)}, u32[]{:S(2)}, u32[]{:S(2)}) %collective-permute-start.10) | collective-permute-done | bytes 1146912 | tf_op jit(solution)/shard_map/ppermute | solution.py:480
  104.7 1.4 add.36
  106.0 0.1 fusion.2
  106.1 1.6 collective-permute-start.11
  107.7 2.2 %collective-permute-start.13 = (f32[560,128]{1,0:T(8,128)S(1)}, f32[560,128]{1,0:T(8,128)S(1)}, u32[]{:S(2)}, u32[]{:S(2)}) collective-permute-start(f32[560,128]{1,0:T(8,128)S(1)} %get-tuple-element.46), channel_id=1, source_target_pairs={{0,6},{1,7},{2,0},{3,1},{4,2},{5,3},{6,4},{7,5},{8,14},{9,15},{10,... | collective-permute-start | bytes 860168 | tf_op jit(solution)/shard_map/ppermute | solution.py:484
  110.0 0.8 collective-permute-start.12
  110.8 6.9 %collective-permute-done.11 = f32[560,128]{1,0:T(8,128)S(1)} collective-permute-done((f32[560,128]{1,0:T(8,128)S(1)}, f32[560,128]{1,0:T(8,128)S(1)}, u32[]{:S(2)}, u32[]{:S(2)}) %collective-permute-start.11) | collective-permute-done | bytes 286752 | tf_op jit(solution)/shard_map/ppermute | solution.py:484
  117.7 4.8 %collective-permute-done.13 = f32[560,128]{1,0:T(8,128)S(1)} collective-permute-done((f32[560,128]{1,0:T(8,128)S(1)}, f32[560,128]{1,0:T(8,128)S(1)}, u32[]{:S(2)}, u32[]{:S(2)}) %collective-permute-start.13) | collective-permute-done | bytes 286752 | tf_op jit(solution)/shard_map/ppermute | solution.py:484
  122.5 12.9 %collective-permute-done.12 = f32[560,128]{1,0:T(8,128)S(1)} collective-permute-done((f32[560,128]{1,0:T(8,128)S(1)}, f32[560,128]{1,0:T(8,128)S(1)}, u32[]{:S(2)}, u32[]{:S(2)}) %collective-permute-start.12) | collective-permute-done | bytes 286752 | tf_op jit(solution)/shard_map/ppermute | solution.py:484
  135.3 0.1 fusion.1.rest_0_
  135.4 1.5 collective-permute-start.16
  136.9 1.5 collective-permute-start.15
  138.4 0.5 collective-permute-start.14
  139.0 7.1 %collective-permute-done.16.rest_3_ = f32[560,128]{1,0:T(8,128)S(1)} collective-permute-done((f32[560,128]{1,0:T(8,128)S(1)}, f32[560,128]{1,0:T(8,128)S(1)}, u32[]{:S(2)}, u32[]{:S(2)}) %collective-permute-start.16) | collective-permute-done | bytes 286752 | tf_op jit(solution)/shard_map/ppermute | solution.py:485
  146.1 5.2 %collective-permute-done.15.rest_2_ = f32[560,128]{1,0:T(8,128)S(1)} collective-permute-done((f32[560,128]{1,0:T(8,128)S(1)}, f32[560,128]{1,0:T(8,128)S(1)}, u32[]{:S(2)}, u32[]{:S(2)}) %collective-permute-start.15) | collective-permute-done | bytes 286752 | tf_op jit(solution)/shard_map/ppermute | solution.py:485
  151.3 0.0 collective-permute-done.14.rest_1_
  151.3 0.0 copy-done.5
  151.3 0.7 copy-done.6
  152.0 0.1 copy-done.7
  152.1 8.1 %update.1 = f32[16,96]{1,0:T(8,128)} custom-call(bf16[28,96,1024]{2,1,0:T(8,128)(2,1)} %get-tuple-element.30.oh_hbm, bf16[28,96,1024]{2,1,0:T(8,128)(2,1)} %get-tuple-element.31.ol_hbm, f32[560,128]{1,0:T(8,128)} %copy-done, f32[560,128]{1,0:T(8,128)} %copy-done.7, f32[560,128]{1,0:T(8,128)} %copy-done.6, f32[560,128]{1,0:T(8,128)} %copy-done.5), custom_call_target="tpu_custom_call" | custom-call | flops 264241152 | bytes 11010048 | tf_op jit(solution)/shard_map/update/pallas_call | solution.py:488
  160.2 8.8 %all_to_all.5 = f32[8,2,96]{2,1,0:T(2,128)S(1)} all-to-all(f32[8,2,96]{2,1,0:T(2,128)} %bitcast.8), channel_id=1, replica_groups=mesh['sens'=4,'par'=8] {'par'}, dimensions={0} | all-to-all | bytes 12288 | tf_op jit(solution)/shard_map/all_to_all | solution.py:504
  169.0 0.6 reduce_sum.9
  (18 shorter events, 0.1 us)
Async XLA Ops:
  1.3 33.9 %copy-start.14 = (s32[600]{0:T(1024)S(1)}, s32[600]{0:T(1024)}, u32[]{:S(2)}) copy-start(s32[600]{0:T(1024)} %param.15) | copy-start | bytes 7204
  30.7 19.6 %collective-permute-start = (f32[4,224,128]{2,1,0:T(8,128)}, f32[4,224,128]{2,1,0:T(8,128)S(1)}, u32[]{:S(2)}, u32[]{:S(2)}) collective-permute-start(f32[4,224,128]{2,1,0:T(8,128)} %get-tuple-element.33), channel_id=1, source_target_pairs={{0,8},{8,0},{16,24},{24,16},{1,9},{9,1},{17,25},{25,17},{2,10},{10... | collective-permute-start | bytes 1376264 | tf_op jit(solution)/shard_map/ppermute | solution.py:350
  33.7 16.7 %collective-permute-start.1 = (f32[4,224,128]{2,1,0:T(8,128)}, f32[4,224,128]{2,1,0:T(8,128)S(1)}, u32[]{:S(2)}, u32[]{:S(2)}) collective-permute-start(f32[4,224,128]{2,1,0:T(8,128)} %get-tuple-element.35), channel_id=1, source_target_pairs={{0,16},{8,24},{16,0},{24,8},{1,17},{9,25},{17,1},{25,9},{2,18},{10... | collective-permute-start | bytes 1376264 | tf_op jit(solution)/shard_map/ppermute | solution.py:350
  36.1 14.2 %copy-start.4 = (f32[4,224,128]{2,1,0:T(8,128)S(1)}, f32[4,224,128]{2,1,0:T(8,128)}, u32[]{:S(2)}) copy-start(f32[4,224,128]{2,1,0:T(8,128)} %get-tuple-element.32) | copy-start | bytes 1376260
  36.1 14.3 %copy-start.3 = (f32[4,224,128]{2,1,0:T(8,128)S(1)}, f32[4,224,128]{2,1,0:T(8,128)}, u32[]{:S(2)}) copy-start(f32[4,224,128]{2,1,0:T(8,128)} %get-tuple-element.34) | copy-start | bytes 1376260
  50.5 6.8 %collective-permute-start.6 = (f32[2,224,128]{2,1,0:T(8,128)S(1)}, f32[2,224,128]{2,1,0:T(8,128)S(1)}, u32[]{:S(2)}, u32[]{:S(2)}) collective-permute-start(f32[2,224,128]{2,1,0:T(8,128)S(1)} %slice.27), channel_id=1, source_target_pairs={{0,8},{8,0},{16,24},{24,16},{1,9},{9,1},{17,25},{25,17},{2,10},{10... | collective-permute-start | bytes 688136 | tf_op jit(solution)/shard_map/ppermute | solution.py:356
  51.1 6.9 %collective-permute-start.2 = (f32[2,224,128]{2,1,0:T(8,128)S(1)}, f32[2,224,128]{2,1,0:T(8,128)S(1)}, u32[]{:S(2)}, u32[]{:S(2)}) collective-permute-start(f32[2,224,128]{2,1,0:T(8,128)S(1)} %slice.25), channel_id=1, source_target_pairs={{0,16},{8,24},{16,0},{24,8},{1,17},{9,25},{17,1},{25,9},{2,18},{10... | collective-permute-start | bytes 688136 | tf_op jit(solution)/shard_map/ppermute | solution.py:356
  57.3 16.1 %copy-start.1 = (f32[2,224,128]{2,1,0:T(8,128)}, f32[2,224,128]{2,1,0:T(8,128)S(1)}, u32[]{:S(2)}) copy-start(f32[2,224,128]{2,1,0:T(8,128)S(1)} %slice_add_fusion.1.rest_4_) | copy-start | bytes 688132
  57.3 8.6 %collective-permute-start.7 = (f32[2,224,128]{2,1,0:T(8,128)S(1)}, f32[2,224,128]{2,1,0:T(8,128)S(1)}, u32[]{:S(2)}, u32[]{:S(2)}) collective-permute-start(f32[2,224,128]{2,1,0:T(8,128)S(1)} %slice_add_fusion.1.rest_4_), channel_id=1, source_target_pairs={{0,8},{8,0},{16,24},{24,16},{1,9},{9,1},{17,25},{25,17},{2,10},{10... | collective-permute-start | bytes 688136 | tf_op jit(solution)/shard_map/ppermute | solution.py:357
  58.0 15.5 %copy-start.2 = (f32[2,224,128]{2,1,0:T(8,128)}, f32[2,224,128]{2,1,0:T(8,128)S(1)}, u32[]{:S(2)}) copy-start(f32[2,224,128]{2,1,0:T(8,128)S(1)} %slice_add_fusion.2.rest_0_) | copy-start | bytes 688132
  58.0 8.6 %collective-permute-start.3 = (f32[2,224,128]{2,1,0:T(8,128)S(1)}, f32[2,224,128]{2,1,0:T(8,128)S(1)}, u32[]{:S(2)}, u32[]{:S(2)}) collective-permute-start(f32[2,224,128]{2,1,0:T(8,128)S(1)} %slice_add_fusion.2.rest_0_), channel_id=1, source_target_pairs={{0,16},{8,24},{16,0},{24,8},{1,17},{9,25},{17,1},{25,9},{2,18},{10... | collective-permute-start | bytes 688136 | tf_op jit(solution)/shard_map/ppermute | solution.py:357
  58.4 12.6 %collective-permute-start.8 = (f32[2,224,128]{2,1,0:T(8,128)S(1)}, f32[2,224,128]{2,1,0:T(8,128)S(1)}, u32[]{:S(2)}, u32[]{:S(2)}) collective-permute-start(f32[2,224,128]{2,1,0:T(8,128)S(1)} %slice_add_fusion.1.rest_4_), channel_id=1, source_target_pairs={{0,16},{8,24},{16,0},{24,8},{1,17},{9,25},{17,1},{25,9},{2,18},{10... | collective-permute-start | bytes 688136 | tf_op jit(solution)/shard_map/ppermute | solution.py:358
  60.1 10.9 %collective-permute-start.4 = (f32[2,224,128]{2,1,0:T(8,128)S(1)}, f32[2,224,128]{2,1,0:T(8,128)S(1)}, u32[]{:S(2)}, u32[]{:S(2)}) collective-permute-start(f32[2,224,128]{2,1,0:T(8,128)S(1)} %slice_add_fusion.2.rest_0_), channel_id=1, source_target_pairs={{0,8},{8,0},{16,24},{24,16},{1,9},{9,1},{17,25},{25,17},{2,10},{10... | collective-permute-start | bytes 688136 | tf_op jit(solution)/shard_map/ppermute | solution.py:358
  66.0 7.5 %copy-start.8 = (f32[2,224,128]{2,1,0:T(8,128)}, f32[2,224,128]{2,1,0:T(8,128)S(1)}, u32[]{:S(2)}) copy-start(f32[2,224,128]{2,1,0:T(8,128)S(1)} %collective-permute-done.7.rest_5_) | copy-start | bytes 688132
  66.0 7.5 %collective-permute-start.9 = (f32[2,224,128]{2,1,0:T(8,128)S(1)}, f32[2,224,128]{2,1,0:T(8,128)S(1)}, u32[]{:S(2)}, u32[]{:S(2)}) collective-permute-start(f32[2,224,128]{2,1,0:T(8,128)S(1)} %collective-permute-done.7.rest_5_), channel_id=1, source_target_pairs={{0,16},{8,24},{16,0},{24,8},{1,17},{9,25},{17,1},{25,9},{2,18},{10... | collective-permute-start | bytes 688136 | tf_op jit(solution)/shard_map/ppermute | solution.py:359
  66.6 6.9 %copy-start.9 = (f32[2,224,128]{2,1,0:T(8,128)}, f32[2,224,128]{2,1,0:T(8,128)S(1)}, u32[]{:S(2)}) copy-start(f32[2,224,128]{2,1,0:T(8,128)S(1)} %collective-permute-done.3.rest_1_) | copy-start | bytes 688132
  66.6 6.9 %collective-permute-start.5 = (f32[2,224,128]{2,1,0:T(8,128)S(1)}, f32[2,224,128]{2,1,0:T(8,128)S(1)}, u32[]{:S(2)}, u32[]{:S(2)}) collective-permute-start(f32[2,224,128]{2,1,0:T(8,128)S(1)} %collective-permute-done.3.rest_1_), channel_id=1, source_target_pairs={{0,8},{8,0},{16,24},{24,16},{1,9},{9,1},{17,25},{25,17},{2,10},{10... | collective-permute-start | bytes 688136 | tf_op jit(solution)/shard_map/ppermute | solution.py:359
  71.0 2.5 %copy-start.10 = (f32[2,224,128]{2,1,0:T(8,128)}, f32[2,224,128]{2,1,0:T(8,128)S(1)}, u32[]{:S(2)}) copy-start(f32[2,224,128]{2,1,0:T(8,128)S(1)} %collective-permute-done.8.rest_6_) | copy-start | bytes 688132
  71.0 2.5 %copy-start.11 = (f32[2,224,128]{2,1,0:T(8,128)}, f32[2,224,128]{2,1,0:T(8,128)S(1)}, u32[]{:S(2)}) copy-start(f32[2,224,128]{2,1,0:T(8,128)S(1)} %collective-permute-done.4.rest_2_) | copy-start | bytes 688132
  73.5 0.7 copy-start.12
  73.5 0.8 copy-start.13
  101.6 3.1 %collective-permute-start.10 = (f32[2240,128]{1,0:T(8,128)}, f32[2240,128]{1,0:T(8,128)S(1)}, u32[]{:S(2)}, u32[]{:S(2)}) collective-permute-start(f32[2240,128]{1,0:T(8,128)} %get-tuple-element.44), channel_id=1, source_target_pairs={{0,1},{1,0},{2,3},{3,2},{4,5},{5,4},{6,7},{7,6},{8,9},{9,8},{10,11... | collective-permute-start | bytes 3440648 | tf_op jit(solution)/shard_map/ppermute | solution.py:480
  106.1 11.6 %collective-permute-start.11 = (f32[560,128]{1,0:T(8,128)S(1)}, f32[560,128]{1,0:T(8,128)S(1)}, u32[]{:S(2)}, u32[]{:S(2)}) collective-permute-start(f32[560,128]{1,0:T(8,128)S(1)} %get-tuple-element.45), channel_id=1, source_target_pairs={{0,2},{1,3},{2,4},{3,5},{4,6},{5,7},{6,0},{7,1},{8,10},{9,11},{10,... | collective-permute-start | bytes 860168 | tf_op jit(solution)/shard_map/ppermute | solution.py:484
  107.7 14.7 %collective-permute-start.13 = (f32[560,128]{1,0:T(8,128)S(1)}, f32[560,128]{1,0:T(8,128)S(1)}, u32[]{:S(2)}, u32[]{:S(2)}) collective-permute-start(f32[560,128]{1,0:T(8,128)S(1)} %get-tuple-element.46), channel_id=1, source_target_pairs={{0,6},{1,7},{2,0},{3,1},{4,2},{5,3},{6,4},{7,5},{8,14},{9,15},{10,... | collective-permute-start | bytes 860168 | tf_op jit(solution)/shard_map/ppermute | solution.py:484
  110.0 25.3 %collective-permute-start.12 = (f32[560,128]{1,0:T(8,128)S(1)}, f32[560,128]{1,0:T(8,128)S(1)}, u32[]{:S(2)}, u32[]{:S(2)}) collective-permute-start(f32[560,128]{1,0:T(8,128)S(1)} %get-tuple-element.47), channel_id=1, source_target_pairs={{0,4},{1,5},{2,6},{3,7},{4,0},{5,1},{6,2},{7,3},{8,12},{9,13},{10,... | collective-permute-start | bytes 860168 | tf_op jit(solution)/shard_map/ppermute | solution.py:484
  135.4 15.9 %copy-start = (f32[560,128]{1,0:T(8,128)}, f32[560,128]{1,0:T(8,128)S(1)}, u32[]{:S(2)}) copy-start(f32[560,128]{1,0:T(8,128)S(1)} %fusion.1.rest_0_) | copy-start | bytes 860164
  135.4 10.7 %collective-permute-start.16 = (f32[560,128]{1,0:T(8,128)S(1)}, f32[560,128]{1,0:T(8,128)S(1)}, u32[]{:S(2)}, u32[]{:S(2)}) collective-permute-start(f32[560,128]{1,0:T(8,128)S(1)} %fusion.1.rest_0_), channel_id=1, source_target_pairs={{0,24},{8,16},{16,8},{24,0},{1,25},{9,17},{17,9},{25,1},{2,26},{10... | collective-permute-start | bytes 860168 | tf_op jit(solution)/shard_map/ppermute | solution.py:485
  136.9 14.4 %collective-permute-start.15 = (f32[560,128]{1,0:T(8,128)S(1)}, f32[560,128]{1,0:T(8,128)S(1)}, u32[]{:S(2)}, u32[]{:S(2)}) collective-permute-start(f32[560,128]{1,0:T(8,128)S(1)} %fusion.1.rest_0_), channel_id=1, source_target_pairs={{0,16},{8,24},{16,0},{24,8},{1,17},{9,25},{17,1},{25,9},{2,18},{10... | collective-permute-start | bytes 860168 | tf_op jit(solution)/shard_map/ppermute | solution.py:485
  138.4 12.8 %collective-permute-start.14 = (f32[560,128]{1,0:T(8,128)S(1)}, f32[560,128]{1,0:T(8,128)S(1)}, u32[]{:S(2)}, u32[]{:S(2)}) collective-permute-start(f32[560,128]{1,0:T(8,128)S(1)} %fusion.1.rest_0_), channel_id=1, source_target_pairs={{0,8},{8,0},{16,24},{24,16},{1,9},{9,1},{17,25},{25,17},{2,10},{10... | collective-permute-start | bytes 860168 | tf_op jit(solution)/shard_map/ppermute | solution.py:485
  146.1 5.2 %copy-start.5 = (f32[560,128]{1,0:T(8,128)}, f32[560,128]{1,0:T(8,128)S(1)}, u32[]{:S(2)}) copy-start(f32[560,128]{1,0:T(8,128)S(1)} %collective-permute-done.16.rest_3_) | copy-start | bytes 860164
  151.3 0.7 copy-start.6
  151.3 0.8 copy-start.7

commit v3 on v2

--- a/solution.py
+++ b/solution.py
@@ -128,7 +128,7 @@
             rec_spec[f, pl.ds(cols + c, bins, stride=2 * cols), :] = tile[padded : padded + bins]
         return 0
 
-    lax.fori_loop(0, cols, column, 0)
+    lax.fori_loop(0, cols, column, 0, unroll=4)
 
     def chunk_body(chunk, _):
         for copy in spec_copies((sr_hbm, si_hbm), (sr_ref, si_ref), sems, chunk, block):
@@ -162,14 +162,15 @@
             out[2 * j + 1] = value[:, par_dev:]
             return 0
 
-        lax.fori_loop(0, per // 2, pair, 0)
+        lax.fori_loop(0, per // 2, pair, 0, unroll=True)
 
 
 def forward_kernel(packing, mask_ref, th_ref, tl_ref, ih_ref, il_ref, *rest):
-    (keep_ref, send_ref, sr_ref, si_ref, sems, whole_ref, field, pred, left) = rest[-9:]
-    sr_hbm, si_hbm = rest[-11:-9]
-    pieces = rest[:-11]
-    cols = packing.cols
+    keep_refs, send_refs = rest[-11:-9], rest[-9:-7]
+    (sr_ref, si_ref, sems, whole_ref, field, pred, left) = rest[-7:]
+    sr_hbm, si_hbm = rest[-13:-11]
+    pieces = rest[:-13]
+    cols = 2 * packing.cols
     bins, sens_dev, par_dev = sr_ref.shape
     chunks = sems.shape[1]
     block = bins // chunks
@@ -199,7 +200,7 @@
             field[pl.ds(cols + c, bins, stride=2 * cols), :] = part[padded : padded + bins]
         return 0
 
-    lax.fori_loop(0, cols // 2, transform, 0)
+    lax.fori_loop(0, cols // 2, transform, 0, unroll=4)
 
     def chunk_body(chunk, _):
         for copy in spec_copies((sr_hbm, si_hbm), (sr_ref, si_ref), sems, chunk, block):
@@ -221,8 +222,10 @@
 
     rows = packing.rows
     count = ih_ref.shape[0] // 2
-    for c in range(cols):
-        wide = [pred[f, c * tall : (c + 1) * tall, :] for f in range(pred.shape[0])]
+    for column in range(cols):
+        keep_ref, send_ref = keep_refs[column // packing.cols], send_refs[column // packing.cols]
+        c = column % packing.cols
+        wide = [pred[f, column * tall : (column + 1) * tall, :] for f in range(pred.shape[0])]
         ph, pl_low = split(jnp.concatenate(wide, axis=1))
         ih, il = ih_ref[...], il_ref[...]
         value = dot(ih, ph) + (dot(il, ph) + dot(ih, pl_low))
@@ -238,52 +241,50 @@
                 left[...] += part
             else:
                 left[...] = part
-            if place == packing.share - 1 or c == cols - 1:
-                row = cols * full + c // packing.share
+            if place == packing.share - 1 or c == packing.cols - 1:
+                row = packing.cols * full + c // packing.share
                 keep_ref[pl.ds(row, count, stride=rows), :] = left[:count]
                 send_ref[pl.ds(row, count, stride=rows), :] = left[count:]
 
 
-def prepare_kernel(packing, index_ref, map_ref, prior_ref, fh_ref, fl_ref, inv_ref, rows_ref,
-                   oh_ref, ol_ref, th_ref, tl_ref, ih_ref, il_ref, select, table):
-    step = pl.program_id(0)
-    blocks = oh_ref.shape[2] // packing.width
+def tables_kernel(packing, index_ref, map_ref, prior_ref, fh_ref, fl_ref, inv_ref,
+                  select, th_ref, tl_ref, ih_ref, il_ref, table):
+    blocks = select.shape[1] // packing.width
     times = inv_ref.shape[1]
-
-    @pl.when(step == 0)
-    def _():
-        lane = lax.broadcasted_iota(jnp.int32, (1, packing.width), 1)
-        width = packing.full * LANES
-        if packing.rest:
-            beyond = lane - width
-            folded = width + lax.rem(jnp.maximum(beyond, 0), packing.rest)
-            local = jnp.where(beyond >= 0, folded, lane)
-            valid = beyond < packing.share * packing.rest
-        else:
-            local = lane
-            valid = lane >= 0
-        for m in range(blocks):
-            owner = jnp.bitwise_xor(index_ref[0], m)
-            wanted = jnp.where(valid, owner * packing.sens_dev + local, -1)
-            hit = map_ref[...] == wanted
-            select[:, m * packing.width : (m + 1) * packing.width] = jnp.where(hit, 1.0, 0.0).astype(BF16)
-        ph, pl_low = split(prior_ref[...])
-        folded_table = dot_nt(fh_ref[...], ph) + (dot_nt(fl_ref[...], ph) + dot_nt(fh_ref[...], pl_low))
-        th, tl = split(folded_table)
-        th_ref[...] = th
-        tl_ref[...] = tl
-        par = inv_ref.shape[0]
-        pairs = par // 2
-        for r in range(2):
-            for d in range(pairs):
-                z = lax.rem(index_ref[1] // 2 + d, pairs)
-                core = jnp.bitwise_xor(lax.rem(index_ref[1], 2), r)
-                j = r * pairs + d
-                table[j * times : (j + 1) * times, :] = inv_ref[2 * z + core]
-        ih, il = split(table[...])
-        ih_ref[...] = ih
-        il_ref[...] = il
-
+    lane = lax.broadcasted_iota(jnp.int32, (1, packing.width), 1)
+    width = packing.full * LANES
+    if packing.rest:
+        beyond = lane - width
+        folded = width + lax.rem(jnp.maximum(beyond, 0), packing.rest)
+        local = jnp.where(beyond >= 0, folded, lane)
+        valid = beyond < packing.share * packing.rest
+    else:
+        local = lane
+        valid = lane >= 0
+    for m in range(blocks):
+        owner = jnp.bitwise_xor(index_ref[0], m)
+        wanted = jnp.where(valid, owner * packing.sens_dev + local, -1)
+        hit = map_ref[...] == wanted
+        select[:, m * packing.width : (m + 1) * packing.width] = jnp.where(hit, 1.0, 0.0).astype(BF16)
+    ph, pl_low = split(prior_ref[...])
+    folded_table = dot_nt(fh_ref[...], ph) + (dot_nt(fl_ref[...], ph) + dot_nt(fh_ref[...], pl_low))
+    th, tl = split(folded_table)
+    th_ref[...] = th
+    tl_ref[...] = tl
+    par = inv_ref.shape[0]
+    pairs = par // 2
+    for r in range(2):
+        for d in range(pairs):
+            z = lax.rem(index_ref[1] // 2 + d, pairs)
+            core = jnp.bitwise_xor(lax.rem(index_ref[1], 2), r)
+            j = r * pairs + d
+            table[j * times : (j + 1) * times, :] = inv_ref[2 * z + core]
+    ih, il = split(table[...])
+    ih_ref[...] = ih
+    il_ref[...] = il
+
+
+def rows_kernel(select, rows_ref, oh_ref, ol_ref):
     group, count, sensors = rows_ref.shape
     high, low = split(rows_ref[...].reshape(group * count, sensors))
     moved = dot(jnp.concatenate([high, low], axis=0), select[...]).astype(BF16)
@@ -291,51 +292,65 @@
     ol_ref[...] = moved[group * count :].reshape(ol_ref.shape)
 
 
-def update_kernel(packing, oh_hbm, ol_hbm, *rest):
-    gathered, (out_ref, oh_ref, ol_ref, sems) = rest[:-4], rest[-4:]
+def update_kernel(packing, count, *rest):
+    high, low, gathered = rest[:count], rest[count : 2 * count], rest[2 * count : -4]
+    out_ref, oh_ref, ol_ref, sems = rest[-4:]
     times = oh_ref.shape[0]
     chunks = sems.shape[1]
-    start_all((oh_hbm, ol_hbm), (oh_ref, ol_ref), sems, chunks, times // chunks)
+    group = times // chunks
+    sources, first = [], 0
+    for hbm in zip(high, low):
+        part = pl.ds(first * group, hbm[0].shape[0])
+        own_chunks = hbm[0].shape[0] // group
+        held = (hbm, (oh_ref.at[part], ol_ref.at[part]), sems.at[:, pl.ds(first, own_chunks)])
+        start_all(*held, own_chunks, group)
+        sources.append((first, own_chunks, held))
+        first += own_chunks
     cols, rows, full = packing.cols, packing.rows, packing.full
-    total = jnp.zeros(out_ref.shape, F32)
+    sens = len(gathered) // 2
     if packing.rest:
         row = lax.broadcasted_iota(jnp.int32, (cols, LANES), 0)
         lane = lax.broadcasted_iota(jnp.int32, (cols, LANES), 1)
         own = lax.rem(row, packing.share) == lane // packing.rest
         shared = row // packing.share
 
-    group = times // chunks
-
-    def body(i, total):
-        for copy in spec_copies((oh_hbm, ol_hbm), (oh_ref, ol_ref), sems, i, group):
+    def unpack(held):
+        parts = []
+        if full == 1:
+            parts.append(held[:cols])
+        elif full > 1:
+            wide = held[: cols * full].reshape(cols, full, LANES)
+            parts.extend(wide[:, f, :] for f in range(full))
+        if packing.rest:
+            spread = jnp.zeros((cols, LANES), F32)
+            for j in range(packing.rest_rows):
+                line = held[cols * full + j : cols * full + j + 1]
+                spread = jnp.where(own & (shared == j), line, spread)
+            parts.append(spread)
+        return jnp.concatenate(parts, axis=1)
+
+    def body(first, held, step, total):
+        i = first + step
+        for copy in spec_copies(*held, step, group):
             copy.wait()
         base = i * (group * rows)
         if group * rows % 8 == 0:
             base = pl.multiple_of(base, 8)
-        for m, ref in enumerate(gathered):
-            block = ref[pl.ds(base, group * rows), :]
+        for m in range(sens):
+            blocks = [gathered[h * sens + m][pl.ds(base, group * rows), :] for h in range(2)]
             place = slice(m * packing.width, (m + 1) * packing.width)
             for g in range(group):
-                held = block[g * rows : (g + 1) * rows]
-                parts = []
-                if full == 1:
-                    parts.append(held[:cols])
-                elif full > 1:
-                    wide = held[: cols * full].reshape(cols, full, LANES)
-                    parts.extend(wide[:, f, :] for f in range(full))
-                if packing.rest:
-                    spread = jnp.zeros((cols, LANES), F32)
-                    for j in range(packing.rest_rows):
-                        line = held[cols * full + j : cols * full + j + 1]
-                        spread = jnp.where(own & (shared == j), line, spread)
-                    parts.append(spread)
-                xh, xl = split(jnp.concatenate(parts, axis=1))
+                x = jnp.concatenate([unpack(block[g * rows : (g + 1) * rows]) for block in blocks], axis=0)
+                xh, xl = split(x)
                 t = i * group + g
                 both = dot_nt(jnp.concatenate([xh, xl], axis=0), oh_ref[t, :, place])
-                total = total + (both[:cols] + both[cols:] + dot_nt(xh, ol_ref[t, :, place]))
+                total = total + (both[: 2 * cols] + both[2 * cols :] + dot_nt(xh, ol_ref[t, :, place]))
         return total
 
-    out_ref[...] = lax.fori_loop(0, chunks, body, total)
+    total = jnp.zeros(out_ref.shape, F32)
+    for first, own_chunks, held in sources:
+        total = lax.fori_loop(0, own_chunks, functools.partial(body, first, held), total)
+    out_ref[...] = total
 
 
 def whole(array):
@@ -346,14 +361,16 @@
     return [(k, k ^ mask) for k in range(size)]
 
 
-def reduce_quarters(keep, send, first, second, size):
-    near = keep + lax.ppermute(send, "sens", swap(size, first))
-    return near
-
-
-def reduce_rest(near, first, second, size):
+def reduce_near(keep, send, first, size):
+    return keep + lax.ppermute(send, "sens", swap(size, first))
+
+
+def reduce_here(near, second, size):
     per = near.shape[0] // 2
-    here = near[:per] + lax.ppermute(near[per:], "sens", swap(size, second))
+    return near[:per] + lax.ppermute(near[per:], "sens", swap(size, second))
+
+
+def spread_back(here, first, second, size):
     over = lax.ppermute(here, "sens", swap(size, second))
     back = lax.ppermute(here, "sens", swap(size, first))
     return [here, over, back, lax.ppermute(over, "sens", swap(size, first))]
@@ -365,7 +382,7 @@
     padded = round_up(bins, 8)
     sens, par = lax.axis_size("sens"), lax.axis_size("par")
     sens_index, par_index = lax.axis_index("sens"), lax.axis_index("par")
-    packing = Packing(cols, sens_dev)
+    packing = Packing(cols // 2, sens_dev)
     rows_dev, times, sensors = inverse_rows.shape
     quarters = sens == 4 and cols % 8 == 0
     limit = 58 * 2**20
@@ -424,47 +441,65 @@
     folded = jax.ShapeDtypeStruct((2 * padded, steps), BF16)
     turned = jax.ShapeDtypeStruct((steps, 2 * padded), BF16)
     map_column = sensor_map.reshape(sensors, 1)
-    oh, ol, th, tl, ih2, il2 = pl.pallas_call(
-        functools.partial(prepare_kernel, packing),
-        grid=(times // time_block,),
-        in_specs=[
-            smem,
-            whole(map_column),
-            whole(prior_cov),
-            whole(fh),
-            whole(fl),
-            whole(inv_blocks),
-            pl.BlockSpec((time_block, rows_dev, sensors), lambda i: (i, 0, 0)),
-        ],
-        out_specs=[pl.BlockSpec((time_block, rows_dev, width), lambda i: (i, 0, 0))] * 2
-        + [whole(folded)] * 2
-        + [whole(turned)] * 2,
-        out_shape=[moved, moved, folded, folded, turned, turned],
-        scratch_shapes=[pltpu.VMEM((sensors, width), BF16), pltpu.VMEM((steps, 2 * padded), F32)],
+    chosen = jax.ShapeDtypeStruct((sensors, width), BF16)
+    select, th, tl, ih2, il2 = pl.pallas_call(
+        functools.partial(tables_kernel, packing),
+        in_specs=[smem, whole(map_column), whole(prior_cov), whole(fh), whole(fl), whole(inv_blocks)],
+        out_shape=[chosen, folded, folded, turned, turned],
+        scratch_shapes=[pltpu.VMEM((steps, 2 * padded), F32)],
         compiler_params=pltpu.CompilerParams(vmem_limit_bytes=limit),
-        cost_estimate=pl.CostEstimate(
-            flops=4 * rows_dev * times * sensors * width, bytes_accessed=8 * rows_dev * times * sensors, transcendentals=0
-        ),
-        name="prepare",
-    )(index, map_column, prior_cov, fh, fl, inv_blocks, by_time)
-
-    if quarters:
-        near0 = reduce_quarters(parts[0], parts[1], 1, 2, sens)
-        near1 = reduce_quarters(parts[2], parts[3], 2, 1, sens)
-        near0, near1, th = lax.optimization_barrier((near0, near1, th))
-        pieces = reduce_rest(near0, 1, 2, sens) + reduce_rest(near1, 2, 1, sens)
+        name="tables",
+    )(index, map_column, prior_cov, fh, fl, inv_blocks)
+
+    blocks = times // time_block
+    third = max(blocks // 3, 1)
+    cuts = [0, third, 2 * third, blocks] if blocks >= 3 else [0, blocks]
+
+    def move_rows(number, chosen_rows):
+        start, stop = cuts[number], cuts[number + 1]
+        moved = jax.ShapeDtypeStruct(((stop - start) * time_block, rows_dev, width), BF16)
+        return pl.pallas_call(
+            rows_kernel,
+            grid=(stop - start,),
+            in_specs=[
+                whole(chosen),
+                pl.BlockSpec((time_block, rows_dev, sensors), lambda i: (i + start, 0, 0)),
+            ],
+            out_specs=[pl.BlockSpec((time_block, rows_dev, width), lambda i: (i, 0, 0))] * 2,
+            out_shape=[moved, moved],
+            compiler_params=pltpu.CompilerParams(vmem_limit_bytes=limit),
+            cost_estimate=pl.CostEstimate(
+                flops=4 * rows_dev * moved.shape[0] * sensors * width,
+                bytes_accessed=8 * rows_dev * moved.shape[0] * sensors,
+                transcendentals=0,
+            ),
+            name="rows",
+        )(chosen_rows, by_time)
+
+    ready = [move_rows(0, select)]
+    if quarters and len(cuts) == 4:
+        near0 = reduce_near(parts[0], parts[1], 1, sens)
+        near1 = reduce_near(parts[2], parts[3], 2, sens)
+        near0, near1, th, ready[0], select = lax.optimization_barrier((near0, near1, th, ready[0], select))
+        ready.append(move_rows(1, select))
+        here0, here1 = reduce_here(near0, 2, sens), reduce_here(near1, 1, sens)
+        here0, here1, ready[1], select = lax.optimization_barrier((here0, here1, ready[1], select))
+        ready.append(move_rows(2, select))
+        pieces = spread_back(here0, 1, 2, sens) + spread_back(here1, 2, 1, sens)
+        pieces[-1], ready[2] = lax.optimization_barrier((pieces[-1], ready[2]))
     else:
-        pieces = [lax.psum(parts[0], "sens")]
+        pieces = [lax.psum(jnp.concatenate(parts, axis=0), "sens")]
+        ready.extend(move_rows(number, select) for number in range(1, len(cuts) - 1))
 
     shard_rows = times * packing.rows
     half = jax.ShapeDtypeStruct((par // 2 * shard_rows, LANES), F32)
-    keep, send = pl.pallas_call(
+    keep0, keep1, send0, send1 = pl.pallas_call(
         functools.partial(forward_kernel, packing),
         in_specs=[smem, whole(th), whole(tl), whole(ih2), whole(il2)]
         + [whole(piece) for piece in pieces]
         + [outside, outside],
-        out_specs=[whole(half)] * 2,
-        out_shape=[half, half],
+        out_specs=[whole(half)] * 4,
+        out_shape=[half] * 4,
         scratch_shapes=spec_scratch
         + [
             pltpu.VMEM((cols, steps, par_dev), F32),
@@ -477,29 +512,37 @@
         name="forward",
     )(mask, th, tl, ih2, il2, *pieces, spec_real, spec_imag)
 
-    pair = keep + lax.ppermute(send, "par", swap(par, 1))
-    mine = pair[:shard_rows]
-    for d in range(1, par // 2):
+    def over_pairs(pair, d):
         there = pair[d * shard_rows : (d + 1) * shard_rows]
-        mine = mine + lax.ppermute(there, "par", [(k, (k + 2 * d) % par) for k in range(par)])
-    gathered = [mine] + [lax.ppermute(mine, "sens", swap(sens, m)) for m in range(1, sens)]
+        return lax.ppermute(there, "par", [(k, (k + 2 * d) % par) for k in range(par)])
+
+    def over_sens(mine):
+        return [mine] + [lax.ppermute(mine, "sens", swap(sens, m)) for m in range(1, sens)]
+
+    pair0 = keep0 + lax.ppermute(send0, "par", swap(par, 1))
+    pair1 = keep1 + lax.ppermute(send1, "par", swap(par, 1))
+    come = [over_pairs(pair0, d) for d in range(1, par // 2)]
+    come[0], come[-1], pair1 = lax.optimization_barrier((come[0], come[-1], pair1))
+    mine0 = pair0[:shard_rows] + sum(come[1:], come[0])
+    mine1 = pair1[:shard_rows] + sum(over_pairs(pair1, d) for d in range(1, par // 2))
+    gathered = over_sens(mine0) + over_sens(mine1)
 
     result = jax.ShapeDtypeStruct((cols, rows_dev), F32)
     partial = pl.pallas_call(
-        functools.partial(update_kernel, packing),
-        in_specs=[outside, outside] + [whole(part) for part in gathered],
+        functools.partial(update_kernel, packing, len(ready)),
+        in_specs=[outside] * (2 * len(ready)) + [whole(part) for part in gathered],
         out_shape=result,
         scratch_shapes=[
-            pltpu.VMEM(oh.shape, BF16),
-            pltpu.VMEM(ol.shape, BF16),
-            pltpu.SemaphoreType.DMA((2, times // block_of(times, 2))),
+            pltpu.VMEM(moved.shape, BF16),
+            pltpu.VMEM(moved.shape, BF16),
+            pltpu.SemaphoreType.DMA((2, blocks)),
         ],
         compiler_params=pltpu.CompilerParams(vmem_limit_bytes=limit),
         cost_estimate=pl.CostEstimate(
             flops=6 * rows_dev * times * cols * width, bytes_accessed=4 * rows_dev * times * width, transcendentals=0
         ),
         name="update",
-    )(oh, ol, *gathered)
+    )(*(pair[0] for pair in ready), *(pair[1] for pair in ready), *gathered)
     per_dev = cols // par
     spread = lax.all_to_all(partial.reshape(par, per_dev, rows_dev), "par", 0, 0)
     return jnp.sum(spread, axis=0)

time: 170 us -> 155 us (0.912)
  waiting for transfers between devices: 55.9 us -> 28.3 us
  starting transfers between devices: 19.7 us -> 31.3 us
    ppermute x17 -> x24, waiting for transfers between devices: 55.9 us -> 28.3 us  [the longest x6 13.8 us: over_pairs(): lax.ppermute(there, 'par', [(k, (k + 2 * d) % par) for k in range(par)])]
    ppermute x17 -> x24, starting transfers between devices: 19.7 us -> 31.3 us  [the longest x6 11.8 us: over_pairs(): lax.ppermute(there, 'par', [(k, (k + 2 * d) % par) for k in range(par)])]
    pallas_call x2 -> x5, Pallas kernels: 22.3 us -> 28.7 us  [the longest x3 18.1 us: move_rows(): pl.pallas_call(rows_kernel, grid=(stop - start,), in_specs=[whole(chosen)...]
    pallas_call x1, Pallas kernels: 29.4 us -> 24.2 us  [shards(): pl.pallas_call(adjoint_kernel, in_specs=[smem, whole(by_sensor), whole(fh...]
  transfers between devices with their start and end apart: 17 -> 24, of which waited for: 11 -> 10; matrix products, arithmetic and copies ran while one was open for 1% -> 1% of each run, Pallas kernels for 8% -> 14%
where the time goes in v3:
time: 155 us; the launch traced here: 154 us
  Pallas kernels  79.2 us (51%)
  starting transfers between devices  31.3 us (20%)
  waiting for transfers between devices  28.3 us (18%)
  blocking collectives  8.8 us (6%)
  other arithmetic  3.27 us (2%)
  local copies, waits for them, and re-layouts  3.16 us (2%)
    pallas_call x1, Pallas kernels, shards(): pl.pallas_call(functools.partial(forward_kernel, packing), in_specs=[smem...  26.3 us
    pallas_call x1, Pallas kernels, shards(): pl.pallas_call(adjoint_kernel, in_specs=[smem, whole(by_sensor), whole(fh...  24.2 us
    pallas_call x3, Pallas kernels, move_rows(): pl.pallas_call(rows_kernel, grid=(stop - start,), in_specs=[whole(chosen)...  18.1 us
    ppermute x6, waiting for transfers between devices, over_pairs(): lax.ppermute(there, 'par', [(k, (k + 2 * d) % par) for k in range(par)])  13.8 us
    ppermute x6, starting transfers between devices, over_pairs(): lax.ppermute(there, 'par', [(k, (k + 2 * d) % par) for k in range(par)])  11.8 us
    all_to_all x1, blocking collectives, shards(): lax.all_to_all(partial.reshape(par, per_dev, rows_dev), 'par', 0, 0)  8.8 us
    pallas_call x1, Pallas kernels, shards(): pl.pallas_call(functools.partial(update_kernel, packing, len(ready)), in_...  7.38 us
    ppermute x6, starting transfers between devices, over_sens(): lax.ppermute(mine, 'sens', swap(sens, m))  7.11 us
  transfers between devices with their start and end apart: 24, of which 10 were waited for; matrix products, arithmetic and copies ran while one was open for 1% of the time, Pallas kernels for 14%

profile of v3, /device:TPU:0, one launch (start us, length us, event | category | flops | bytes accessed | tf_op | source)
XLA Modules:
  0.0 154.3 jit_solution(11864394435269814976)
XLA Ops:
  0.0 0.7 pad_add_fusion.mask_ref
  0.7 0.6 pad_add_fusion.1.index_ref
  1.3 24.2 %adjoint.1 = (f32[4,224,128]{2,1,0:T(8,128)}, f32[4,224,128]{2,1,0:T(8,128)}, f32[4,224,128]{2,1,0:T(8,128)}, f32[4,224,128]{2,1,0:T(8,128)}) custom-call(s32[2]{0:T(128)} %pad_add_fusion.mask_ref, f32[150,16,224]{2,1,0:T(8,128)} %bitcast.10, bf16[464,224]{1,0:T(8,128)(2,1)} %constant.24.clone.fh_ref, bf16[464,224]{1,0:T(8,128)(2,1)} %constant.25.clone.fl_ref, ...), custom_call_target="tpu_custom_call" | custom-call | flops 1658880000 | bytes 34560000 | tf_op jit(solution)/shard_map/adjoint/pallas_call | solution.py:420
  25.4 3.0 %collective-permute-start = (f32[4,224,128]{2,1,0:T(8,128)}, f32[4,224,128]{2,1,0:T(8,128)S(1)}, u32[]{:S(2)}, u32[]{:S(2)}) collective-permute-start(f32[4,224,128]{2,1,0:T(8,128)} %get-tuple-element.51), channel_id=1, source_target_pairs={{0,8},{8,0},{16,24},{24,16},{1,9},{9,1},{17,25},{25,17},{2,10},{10... | collective-permute-start | bytes 1376264 | tf_op jit(solution)/shard_map/ppermute | solution.py:365
  28.5 1.5 collective-permute-start.1
  30.0 0.9 reshape.8.map_ref
  30.9 3.3 %tables.1 = (bf16[600,1024]{1,0:T(8,128)(2,1)}, bf16[464,224]{1,0:T(8,128)(2,1)}, bf16[464,224]{1,0:T(8,128)(2,1)}, bf16[224,464]{1,0:T(8,128)(2,1)}, bf16[224,464]{1,0:T(8,128)(2,1)}) custom-call(s32[2]{0:T(128)} %pad_add_fusion.1.index_ref, s32[600,1]{1,0:T(8,128)} %reshape.8.map_ref, f32[224,224]{1,0:T(8,128)} %prior_ref.1, ...), custom_call_target="tpu_custom_call" | custom-call | tf_op jit(solution)/shard_map/tables/pallas_call | solution.py:445
  34.1 5.5 %rows.3 = (bf16[8,96,1024]{2,1,0:T(8,128)(2,1)}, bf16[8,96,1024]{2,1,0:T(8,128)(2,1)}) custom-call(bf16[600,1024]{1,0:T(8,128)(2,1)} %get-tuple-element.67.select, f32[28,96,600]{2,1,0:T(8,128)} %bitcast.7), custom_call_target="tpu_custom_call" | custom-call | flops 1887436800 | bytes 3686400 | tf_op jit(solution)/shard_map/rows/pallas_call | solution.py:461
  39.7 0.0 collective-permute-done
  39.7 0.1 add.44
  39.7 0.9 collective-permute-done.1
  40.7 1.6 %collective-permute-start.2 = (f32[2,224,128]{2,1,0:T(8,128)S(1)}, f32[2,224,128]{2,1,0:T(8,128)S(1)}, u32[]{:S(2)}, u32[]{:S(2)}) collective-permute-start(f32[2,224,128]{2,1,0:T(8,128)S(1)} %slice.37), channel_id=1, source_target_pairs={{0,16},{8,24},{16,0},{24,8},{1,17},{9,25},{17,1},{25,9},{2,18},{10... | collective-permute-start | bytes 688136 | tf_op jit(solution)/shard_map/ppermute | solution.py:370
  42.3 0.6 collective-permute-start.3
  42.9 5.5 %rows.4 = (bf16[8,96,1024]{2,1,0:T(8,128)(2,1)}, bf16[8,96,1024]{2,1,0:T(8,128)(2,1)}) custom-call(bf16[600,1024]{1,0:T(8,128)(2,1)} %get-tuple-element.67.select, f32[28,96,600]{2,1,0:T(8,128)} %bitcast.8), custom_call_target="tpu_custom_call" | custom-call | flops 1887436800 | bytes 3686400 | tf_op jit(solution)/shard_map/rows/pallas_call | solution.py:461
  48.4 0.0 collective-permute-done.2
  48.5 1.5 %collective-permute-start.4 = (f32[2,224,128]{2,1,0:T(8,128)S(1)}, f32[2,224,128]{2,1,0:T(8,128)S(1)}, u32[]{:S(2)}, u32[]{:S(2)}) collective-permute-start(f32[2,224,128]{2,1,0:T(8,128)S(1)} %slice_add_fusion.rest_4_), channel_id=1, source_target_pairs={{0,8},{8,0},{16,24},{24,16},{1,9},{9,1},{17,25},{25,17},{2,10},{10... | collective-permute-start | bytes 688136 | tf_op jit(solution)/shard_map/ppermute | solution.py:374
  50.0 0.5 collective-permute-start.6
  50.5 0.5 collective-permute-start.7
  51.0 1.6 %collective-permute-start.9 = (f32[2,224,128]{2,1,0:T(8,128)S(1)}, f32[2,224,128]{2,1,0:T(8,128)S(1)}, u32[]{:S(2)}, u32[]{:S(2)}) collective-permute-start(f32[2,224,128]{2,1,0:T(8,128)S(1)} %slice_add_fusion.rest_4_), channel_id=1, source_target_pairs={{0,16},{8,24},{16,0},{24,8},{1,17},{9,25},{17,1},{25,9},{2,18},{10... | collective-permute-start | bytes 688136 | tf_op jit(solution)/shard_map/ppermute | solution.py:375
  52.6 4.5 %collective-permute-done.4.rest_5_ = f32[2,224,128]{2,1,0:T(8,128)S(1)} collective-permute-done((f32[2,224,128]{2,1,0:T(8,128)S(1)}, f32[2,224,128]{2,1,0:T(8,128)S(1)}, u32[]{:S(2)}, u32[]{:S(2)}) %collective-permute-start.4) | collective-permute-done | bytes 229408 | tf_op jit(solution)/shard_map/ppermute | solution.py:374
  57.1 0.5 collective-permute-start.5
  57.6 1.0 collective-permute-done.6.rest_1_
  58.6 0.5 collective-permute-start.8
  59.1 7.1 %rows.5 = (bf16[12,96,1024]{2,1,0:T(8,128)(2,1)}, bf16[12,96,1024]{2,1,0:T(8,128)(2,1)}) custom-call(bf16[600,1024]{1,0:T(8,128)(2,1)} %get-tuple-element.67.select, f32[28,96,600]{2,1,0:T(8,128)} %bitcast.9), custom_call_target="tpu_custom_call" | custom-call | flops 2831155200 | bytes 5529600 | tf_op jit(solution)/shard_map/rows/pallas_call | solution.py:461
  66.3 0.0 collective-permute-done.7.rest_2_
  66.3 0.0 collective-permute-done.9.rest_6_
  66.3 0.6 copy-done.11
  67.0 0.1 copy-done.9
  67.0 0.1 copy-done.10
  67.1 0.1 copy-done.12
  67.2 26.3 %forward.1 = (f32[1120,128]{1,0:T(8,128)}, f32[1120,128]{1,0:T(8,128)}, f32[1120,128]{1,0:T(8,128)}, f32[1120,128]{1,0:T(8,128)}) custom-call(s32[2]{0:T(128)} %pad_add_fusion.mask_ref, bf16[464,224]{1,0:T(8,128)(2,1)} %get-tuple-element.74.th_ref, bf16[464,224]{1,0:T(8,128)(2,1)} %get-tuple-element.75.tl_ref, bf16[224,464]{1,0:T(8,128)(2,1)} %get-tuple-element.76.ih_ref, ...), custom_call_target="tpu_custom_call" | custom-call | flops 1658880000 | bytes 34560000 | tf_op jit(solution)/shard_map/forward/pallas_call | solution.py:496
  93.5 0.1 collective-permute-start.10
  93.6 0.5 collective-permute-start.13
  94.1 1.7 %collective-permute-done.10 = f32[1120,128]{1,0:T(8,128)S(1)} collective-permute-done((f32[1120,128]{1,0:T(8,128)}, f32[1120,128]{1,0:T(8,128)S(1)}, u32[]{:S(2)}, u32[]{:S(2)}) %collective-permute-start.10) | collective-permute-done | bytes 573472 | tf_op jit(solution)/shard_map/ppermute | solution.py:522
  95.7 1.1 add.48
  96.9 1.6 %collective-permute-start.11 = (f32[280,128]{1,0:T(8,128)S(1)}, f32[280,128]{1,0:T(8,128)S(1)}, u32[]{:S(2)}, u32[]{:S(2)}) collective-permute-start(f32[280,128]{1,0:T(8,128)S(1)} %get-tuple-element.92), channel_id=1, source_target_pairs={{0,2},{1,3},{2,4},{3,5},{4,6},{5,7},{6,0},{7,1},{8,10},{9,11},{10,... | collective-permute-start | bytes 430088 | tf_op jit(solution)/shard_map/ppermute | solution.py:517
  98.5 2.2 %collective-permute-start.12 = (f32[280,128]{1,0:T(8,128)S(1)}, f32[280,128]{1,0:T(8,128)S(1)}, u32[]{:S(2)}, u32[]{:S(2)}) collective-permute-start(f32[280,128]{1,0:T(8,128)S(1)} %get-tuple-element.91), channel_id=1, source_target_pairs={{0,6},{1,7},{2,0},{3,1},{4,2},{5,3},{6,4},{7,5},{8,14},{9,15},{10,... | collective-permute-start | bytes 430088 | tf_op jit(solution)/shard_map/ppermute | solution.py:517
  100.8 0.8 collective-permute-start.14
  101.6 0.0 collective-permute-done.13
  101.6 0.1 add.49
  101.6 3.8 %collective-permute-done.11 = f32[280,128]{1,0:T(8,128)S(1)} collective-permute-done((f32[280,128]{1,0:T(8,128)S(1)}, f32[280,128]{1,0:T(8,128)S(1)}, u32[]{:S(2)}, u32[]{:S(2)}) %collective-permute-start.11) | collective-permute-done | bytes 143392 | tf_op jit(solution)/shard_map/ppermute | solution.py:517
  105.4 1.7 %collective-permute-done.12 = f32[280,128]{1,0:T(8,128)S(1)} collective-permute-done((f32[280,128]{1,0:T(8,128)S(1)}, f32[280,128]{1,0:T(8,128)S(1)}, u32[]{:S(2)}, u32[]{:S(2)}) %collective-permute-start.12) | collective-permute-done | bytes 143392 | tf_op jit(solution)/shard_map/ppermute | solution.py:517
  107.2 3.0 %collective-permute-start.20 = (f32[280,128]{1,0:T(8,128)S(1)}, f32[280,128]{1,0:T(8,128)S(1)}, u32[]{:S(2)}, u32[]{:S(2)}) collective-permute-start(f32[280,128]{1,0:T(8,128)S(1)} %get-tuple-element.88), channel_id=1, source_target_pairs={{0,6},{1,7},{2,0},{3,1},{4,2},{5,3},{6,4},{7,5},{8,14},{9,15},{10,... | collective-permute-start | bytes 430088 | tf_op jit(solution)/shard_map/ppermute | solution.py:517
  110.2 0.1 collective-permute-start.18
  110.3 4.0 %collective-permute-start.19 = (f32[280,128]{1,0:T(8,128)S(1)}, f32[280,128]{1,0:T(8,128)S(1)}, u32[]{:S(2)}, u32[]{:S(2)}) collective-permute-start(f32[280,128]{1,0:T(8,128)S(1)} %get-tuple-element.87), channel_id=1, source_target_pairs={{0,4},{1,5},{2,6},{3,7},{4,0},{5,1},{6,2},{7,3},{8,12},{9,13},{10,... | collective-permute-start | bytes 430088 | tf_op jit(solution)/shard_map/ppermute | solution.py:517
  114.3 2.8 %collective-permute-done.14 = f32[280,128]{1,0:T(8,128)S(1)} collective-permute-done((f32[280,128]{1,0:T(8,128)S(1)}, f32[280,128]{1,0:T(8,128)S(1)}, u32[]{:S(2)}, u32[]{:S(2)}) %collective-permute-start.14) | collective-permute-done | bytes 143392 | tf_op jit(solution)/shard_map/ppermute | solution.py:517
  117.1 1.5 collective-permute-start.15
  118.7 0.6 collective-permute-start.16
  119.2 0.0 collective-permute-done.20
  119.2 1.5 collective-permute-start.17
  120.7 0.0 collective-permute-done.18
  120.7 5.5 %collective-permute-done.19 = f32[280,128]{1,0:T(8,128)S(1)} collective-permute-done((f32[280,128]{1,0:T(8,128)S(1)}, f32[280,128]{1,0:T(8,128)S(1)}, u32[]{:S(2)}, u32[]{:S(2)}) %collective-permute-start.19) | collective-permute-done | bytes 143392 | tf_op jit(solution)/shard_map/ppermute | solution.py:517
  126.2 1.5 collective-permute-start.21
  127.8 0.6 collective-permute-start.22
  128.3 1.5 collective-permute-start.23
  129.8 0.0 collective-permute-done.17.rest_9_
  129.8 2.8 %collective-permute-done.21.rest_11_ = f32[280,128]{1,0:T(8,128)S(1)} collective-permute-done((f32[280,128]{1,0:T(8,128)S(1)}, f32[280,128]{1,0:T(8,128)S(1)}, u32[]{:S(2)}, u32[]{:S(2)}) %collective-permute-start.21) | collective-permute-done | bytes 143392 | tf_op jit(solution)/shard_map/ppermute | solution.py:520
  132.6 3.6 %collective-permute-done.22.rest_12_ = f32[280,128]{1,0:T(8,128)S(1)} collective-permute-done((f32[280,128]{1,0:T(8,128)S(1)}, f32[280,128]{1,0:T(8,128)S(1)}, u32[]{:S(2)}, u32[]{:S(2)}) %collective-permute-start.22) | collective-permute-done | bytes 143392 | tf_op jit(solution)/shard_map/ppermute | solution.py:520
  136.3 0.0 collective-permute-done.23.rest_13_
  136.3 0.6 copy-done.17
  136.9 0.7 copy-done.18
  137.6 7.4 %update.1 = f32[16,96]{1,0:T(8,128)} custom-call(bf16[8,96,1024]{2,1,0:T(8,128)(2,1)} %get-tuple-element.59.rest_0_, bf16[8,96,1024]{2,1,0:T(8,128)(2,1)} %get-tuple-element.65.rest_1_, bf16[12,96,1024]{2,1,0:T(8,128)(2,1)} %get-tuple-element.70.rest_2_, bf16[8,96,1024]{2,1,0:T(8,128)(2,1)} %get-tuple-element.71.rest_3_, ...), custom_call_target="tpu_custom_call" | custom-call | flops 264241152 | bytes 11010048 | tf_op jit(solution)/shard_map/update/pallas_call | solution.py:531
  144.9 8.8 %all_to_all.5 = f32[8,2,96]{2,1,0:T(2,128)S(1)} all-to-all(f32[8,2,96]{2,1,0:T(2,128)} %bitcast.11), channel_id=1, replica_groups=mesh['sens'=4,'par'=8] {'par'}, dimensions={0} | all-to-all | bytes 12288 | tf_op jit(solution)/shard_map/all_to_all | solution.py:547
  153.7 0.6 reduce_sum.9
  (48 shorter events, 0.4 us)
Async XLA Ops:
  1.3 28.7 %copy-start.19 = (s32[600]{0:T(1024)S(1)}, s32[600]{0:T(1024)}, u32[]{:S(2)}) copy-start(s32[600]{0:T(1024)} %param.15) | copy-start | bytes 7204
  25.4 14.2 %collective-permute-start = (f32[4,224,128]{2,1,0:T(8,128)}, f32[4,224,128]{2,1,0:T(8,128)S(1)}, u32[]{:S(2)}, u32[]{:S(2)}) collective-permute-start(f32[4,224,128]{2,1,0:T(8,128)} %get-tuple-element.51), channel_id=1, source_target_pairs={{0,8},{8,0},{16,24},{24,16},{1,9},{9,1},{17,25},{25,17},{2,10},{10... | collective-permute-start | bytes 1376264 | tf_op jit(solution)/shard_map/ppermute | solution.py:365
  28.5 12.2 %collective-permute-start.1 = (f32[4,224,128]{2,1,0:T(8,128)}, f32[4,224,128]{2,1,0:T(8,128)S(1)}, u32[]{:S(2)}, u32[]{:S(2)}) collective-permute-start(f32[4,224,128]{2,1,0:T(8,128)} %get-tuple-element.53), channel_id=1, source_target_pairs={{0,16},{8,24},{16,0},{24,8},{1,17},{9,25},{17,1},{25,9},{2,18},{10... | collective-permute-start | bytes 1376264 | tf_op jit(solution)/shard_map/ppermute | solution.py:365
  34.1 5.6 %copy-start.6 = (f32[4,224,128]{2,1,0:T(8,128)S(1)}, f32[4,224,128]{2,1,0:T(8,128)}, u32[]{:S(2)}) copy-start(f32[4,224,128]{2,1,0:T(8,128)} %get-tuple-element.50) | copy-start | bytes 1376260
  34.1 6.5 %copy-start.5 = (f32[4,224,128]{2,1,0:T(8,128)S(1)}, f32[4,224,128]{2,1,0:T(8,128)}, u32[]{:S(2)}) copy-start(f32[4,224,128]{2,1,0:T(8,128)} %get-tuple-element.52) | copy-start | bytes 1376260
  40.7 7.7 %collective-permute-start.2 = (f32[2,224,128]{2,1,0:T(8,128)S(1)}, f32[2,224,128]{2,1,0:T(8,128)S(1)}, u32[]{:S(2)}, u32[]{:S(2)}) collective-permute-start(f32[2,224,128]{2,1,0:T(8,128)S(1)} %slice.37), channel_id=1, source_target_pairs={{0,16},{8,24},{16,0},{24,8},{1,17},{9,25},{17,1},{25,9},{2,18},{10... | collective-permute-start | bytes 688136 | tf_op jit(solution)/shard_map/ppermute | solution.py:370
  42.3 6.1 %collective-permute-start.3 = (f32[2,224,128]{2,1,0:T(8,128)S(1)}, f32[2,224,128]{2,1,0:T(8,128)S(1)}, u32[]{:S(2)}, u32[]{:S(2)}) collective-permute-start(f32[2,224,128]{2,1,0:T(8,128)S(1)} %slice.39), channel_id=1, source_target_pairs={{0,8},{8,0},{16,24},{24,16},{1,9},{9,1},{17,25},{25,17},{2,10},{10... | collective-permute-start | bytes 688136 | tf_op jit(solution)/shard_map/ppermute | solution.py:370
  48.4 17.8 %copy-start = (f32[2,224,128]{2,1,0:T(8,128)}, f32[2,224,128]{2,1,0:T(8,128)S(1)}, u32[]{:S(2)}) copy-start(f32[2,224,128]{2,1,0:T(8,128)S(1)} %slice_add_fusion.1.rest_0_) | copy-start | bytes 688132
  48.5 17.8 %copy-start.1 = (f32[2,224,128]{2,1,0:T(8,128)}, f32[2,224,128]{2,1,0:T(8,128)S(1)}, u32[]{:S(2)}) copy-start(f32[2,224,128]{2,1,0:T(8,128)S(1)} %slice_add_fusion.rest_4_) | copy-start | bytes 688132
  48.5 8.6 %collective-permute-start.4 = (f32[2,224,128]{2,1,0:T(8,128)S(1)}, f32[2,224,128]{2,1,0:T(8,128)S(1)}, u32[]{:S(2)}, u32[]{:S(2)}) collective-permute-start(f32[2,224,128]{2,1,0:T(8,128)S(1)} %slice_add_fusion.rest_4_), channel_id=1, source_target_pairs={{0,8},{8,0},{16,24},{24,16},{1,9},{9,1},{17,25},{25,17},{2,10},{10... | collective-permute-start | bytes 688136 | tf_op jit(solution)/shard_map/ppermute | solution.py:374
  50.0 8.5 %collective-permute-start.6 = (f32[2,224,128]{2,1,0:T(8,128)S(1)}, f32[2,224,128]{2,1,0:T(8,128)S(1)}, u32[]{:S(2)}, u32[]{:S(2)}) collective-permute-start(f32[2,224,128]{2,1,0:T(8,128)S(1)} %slice_add_fusion.1.rest_0_), channel_id=1, source_target_pairs={{0,16},{8,24},{16,0},{24,8},{1,17},{9,25},{17,1},{25,9},{2,18},{10... | collective-permute-start | bytes 688136 | tf_op jit(solution)/shard_map/ppermute | solution.py:374
  50.5 15.8 %collective-permute-start.7 = (f32[2,224,128]{2,1,0:T(8,128)S(1)}, f32[2,224,128]{2,1,0:T(8,128)S(1)}, u32[]{:S(2)}, u32[]{:S(2)}) collective-permute-start(f32[2,224,128]{2,1,0:T(8,128)S(1)} %slice_add_fusion.1.rest_0_), channel_id=1, source_target_pairs={{0,8},{8,0},{16,24},{24,16},{1,9},{9,1},{17,25},{25,17},{2,10},{10... | collective-permute-start | bytes 688136 | tf_op jit(solution)/shard_map/ppermute | solution.py:375
  51.0 15.3 %collective-permute-start.9 = (f32[2,224,128]{2,1,0:T(8,128)S(1)}, f32[2,224,128]{2,1,0:T(8,128)S(1)}, u32[]{:S(2)}, u32[]{:S(2)}) collective-permute-start(f32[2,224,128]{2,1,0:T(8,128)S(1)} %slice_add_fusion.rest_4_), channel_id=1, source_target_pairs={{0,16},{8,24},{16,0},{24,8},{1,17},{9,25},{17,1},{25,9},{2,18},{10... | collective-permute-start | bytes 688136 | tf_op jit(solution)/shard_map/ppermute | solution.py:375
  57.1 9.1 %copy-start.7 = (f32[2,224,128]{2,1,0:T(8,128)}, f32[2,224,128]{2,1,0:T(8,128)S(1)}, u32[]{:S(2)}) copy-start(f32[2,224,128]{2,1,0:T(8,128)S(1)} %collective-permute-done.4.rest_5_) | copy-start | bytes 688132
  57.1 9.2 %collective-permute-start.5 = (f32[2,224,128]{2,1,0:T(8,128)S(1)}, f32[2,224,128]{2,1,0:T(8,128)S(1)}, u32[]{:S(2)}, u32[]{:S(2)}) collective-permute-start(f32[2,224,128]{2,1,0:T(8,128)S(1)} %collective-permute-done.4.rest_5_), channel_id=1, source_target_pairs={{0,16},{8,24},{16,0},{24,8},{1,17},{9,25},{17,1},{25,9},{2,18},{10... | collective-permute-start | bytes 688136 | tf_op jit(solution)/shard_map/ppermute | solution.py:376
  58.6 7.7 %copy-start.8 = (f32[2,224,128]{2,1,0:T(8,128)}, f32[2,224,128]{2,1,0:T(8,128)S(1)}, u32[]{:S(2)}) copy-start(f32[2,224,128]{2,1,0:T(8,128)S(1)} %collective-permute-done.6.rest_1_) | copy-start | bytes 688132
  58.6 7.7 %collective-permute-start.8 = (f32[2,224,128]{2,1,0:T(8,128)S(1)}, f32[2,224,128]{2,1,0:T(8,128)S(1)}, u32[]{:S(2)}, u32[]{:S(2)}) collective-permute-start(f32[2,224,128]{2,1,0:T(8,128)S(1)} %collective-permute-done.6.rest_1_), channel_id=1, source_target_pairs={{0,8},{8,0},{16,24},{24,16},{1,9},{9,1},{17,25},{25,17},{2,10},{10... | collective-permute-start | bytes 688136 | tf_op jit(solution)/shard_map/ppermute | solution.py:376
  66.3 0.7 copy-start.11
  66.3 0.7 copy-start.9
  66.3 0.8 copy-start.10
  66.3 0.9 copy-start.12
  93.5 8.1 %copy-start.2 = (f32[1120,128]{1,0:T(8,128)S(1)}, f32[1120,128]{1,0:T(8,128)}, u32[]{:S(2)}) copy-start(f32[1120,128]{1,0:T(8,128)} %get-tuple-element.82) | copy-start | bytes 1720324
  93.5 2.3 %collective-permute-start.10 = (f32[1120,128]{1,0:T(8,128)}, f32[1120,128]{1,0:T(8,128)S(1)}, u32[]{:S(2)}, u32[]{:S(2)}) collective-permute-start(f32[1120,128]{1,0:T(8,128)} %get-tuple-element.81), channel_id=1, source_target_pairs={{0,1},{1,0},{2,3},{3,2},{4,5},{5,4},{6,7},{7,6},{8,9},{9,8},{10,11... | collective-permute-start | bytes 1720328 | tf_op jit(solution)/shard_map/ppermute | solution.py:522
  93.6 8.0 %collective-permute-start.13 = (f32[1120,128]{1,0:T(8,128)}, f32[1120,128]{1,0:T(8,128)S(1)}, u32[]{:S(2)}, u32[]{:S(2)}) collective-permute-start(f32[1120,128]{1,0:T(8,128)} %get-tuple-element.83), channel_id=1, source_target_pairs={{0,1},{1,0},{2,3},{3,2},{4,5},{5,4},{6,7},{7,6},{8,9},{9,8},{10,11... | collective-permute-start | bytes 1720328 | tf_op jit(solution)/shard_map/ppermute | solution.py:523
  96.9 8.5 %collective-permute-start.11 = (f32[280,128]{1,0:T(8,128)S(1)}, f32[280,128]{1,0:T(8,128)S(1)}, u32[]{:S(2)}, u32[]{:S(2)}) collective-permute-start(f32[280,128]{1,0:T(8,128)S(1)} %get-tuple-element.92), channel_id=1, source_target_pairs={{0,2},{1,3},{2,4},{3,5},{4,6},{5,7},{6,0},{7,1},{8,10},{9,11},{10,... | collective-permute-start | bytes 430088 | tf_op jit(solution)/shard_map/ppermute | solution.py:517
  98.5 8.6 %collective-permute-start.12 = (f32[280,128]{1,0:T(8,128)S(1)}, f32[280,128]{1,0:T(8,128)S(1)}, u32[]{:S(2)}, u32[]{:S(2)}) collective-permute-start(f32[280,128]{1,0:T(8,128)S(1)} %get-tuple-element.91), channel_id=1, source_target_pairs={{0,6},{1,7},{2,0},{3,1},{4,2},{5,3},{6,4},{7,5},{8,14},{9,15},{10,... | collective-permute-start | bytes 430088 | tf_op jit(solution)/shard_map/ppermute | solution.py:517
  100.8 16.3 %collective-permute-start.14 = (f32[280,128]{1,0:T(8,128)S(1)}, f32[280,128]{1,0:T(8,128)S(1)}, u32[]{:S(2)}, u32[]{:S(2)}) collective-permute-start(f32[280,128]{1,0:T(8,128)S(1)} %get-tuple-element.90), channel_id=1, source_target_pairs={{0,4},{1,5},{2,6},{3,7},{4,0},{5,1},{6,2},{7,3},{8,12},{9,13},{10,... | collective-permute-start | bytes 430088 | tf_op jit(solution)/shard_map/ppermute | solution.py:517
  107.2 12.0 %collective-permute-start.20 = (f32[280,128]{1,0:T(8,128)S(1)}, f32[280,128]{1,0:T(8,128)S(1)}, u32[]{:S(2)}, u32[]{:S(2)}) collective-permute-start(f32[280,128]{1,0:T(8,128)S(1)} %get-tuple-element.88), channel_id=1, source_target_pairs={{0,6},{1,7},{2,0},{3,1},{4,2},{5,3},{6,4},{7,5},{8,14},{9,15},{10,... | collective-permute-start | bytes 430088 | tf_op jit(solution)/shard_map/ppermute | solution.py:517
  110.2 10.5 %collective-permute-start.18 = (f32[280,128]{1,0:T(8,128)S(1)}, f32[280,128]{1,0:T(8,128)S(1)}, u32[]{:S(2)}, u32[]{:S(2)}) collective-permute-start(f32[280,128]{1,0:T(8,128)S(1)} %get-tuple-element.89), channel_id=1, source_target_pairs={{0,2},{1,3},{2,4},{3,5},{4,6},{5,7},{6,0},{7,1},{8,10},{9,11},{10,... | collective-permute-start | bytes 430088 | tf_op jit(solution)/shard_map/ppermute | solution.py:517
  110.3 15.9 %collective-permute-start.19 = (f32[280,128]{1,0:T(8,128)S(1)}, f32[280,128]{1,0:T(8,128)S(1)}, u32[]{:S(2)}, u32[]{:S(2)}) collective-permute-start(f32[280,128]{1,0:T(8,128)S(1)} %get-tuple-element.87), channel_id=1, source_target_pairs={{0,4},{1,5},{2,6},{3,7},{4,0},{5,1},{6,2},{7,3},{8,12},{9,13},{10,... | collective-permute-start | bytes 430088 | tf_op jit(solution)/shard_map/ppermute | solution.py:517
  117.1 19.1 %copy-start.3 = (f32[280,128]{1,0:T(8,128)}, f32[280,128]{1,0:T(8,128)S(1)}, u32[]{:S(2)}) copy-start(f32[280,128]{1,0:T(8,128)S(1)} %slice_add_fusion.2.rest_6_) | copy-start | bytes 430084
  117.1 11.2 %collective-permute-start.15 = (f32[280,128]{1,0:T(8,128)S(1)}, f32[280,128]{1,0:T(8,128)S(1)}, u32[]{:S(2)}, u32[]{:S(2)}) collective-permute-start(f32[280,128]{1,0:T(8,128)S(1)} %slice_add_fusion.2.rest_6_), channel_id=1, source_target_pairs={{0,8},{8,0},{16,24},{24,16},{1,9},{9,1},{17,25},{25,17},{2,10},{10... | collective-permute-start | bytes 430088 | tf_op jit(solution)/shard_map/ppermute | solution.py:520
  118.7 11.1 %collective-permute-start.16 = (f32[280,128]{1,0:T(8,128)S(1)}, f32[280,128]{1,0:T(8,128)S(1)}, u32[]{:S(2)}, u32[]{:S(2)}) collective-permute-start(f32[280,128]{1,0:T(8,128)S(1)} %slice_add_fusion.2.rest_6_), channel_id=1, source_target_pairs={{0,16},{8,24},{16,0},{24,8},{1,17},{9,25},{17,1},{25,9},{2,18},{10... | collective-permute-start | bytes 430088 | tf_op jit(solution)/shard_map/ppermute | solution.py:520
  119.2 10.6 %collective-permute-start.17 = (f32[280,128]{1,0:T(8,128)S(1)}, f32[280,128]{1,0:T(8,128)S(1)}, u32[]{:S(2)}, u32[]{:S(2)}) collective-permute-start(f32[280,128]{1,0:T(8,128)S(1)} %slice_add_fusion.2.rest_6_), channel_id=1, source_target_pairs={{0,24},{8,16},{16,8},{24,0},{1,25},{9,17},{17,9},{25,1},{2,26},{10... | collective-permute-start | bytes 430088 | tf_op jit(solution)/shard_map/ppermute | solution.py:520
  126.2 10.0 %copy-start.4 = (f32[280,128]{1,0:T(8,128)}, f32[280,128]{1,0:T(8,128)S(1)}, u32[]{:S(2)}) copy-start(f32[280,128]{1,0:T(8,128)S(1)} %add_add_fusion.rest_10_) | copy-start | bytes 430084
  126.2 6.4 %collective-permute-start.21 = (f32[280,128]{1,0:T(8,128)S(1)}, f32[280,128]{1,0:T(8,128)S(1)}, u32[]{:S(2)}, u32[]{:S(2)}) collective-permute-start(f32[280,128]{1,0:T(8,128)S(1)} %add_add_fusion.rest_10_), channel_id=1, source_target_pairs={{0,8},{8,0},{16,24},{24,16},{1,9},{9,1},{17,25},{25,17},{2,10},{10... | collective-permute-start | bytes 430088 | tf_op jit(solution)/shard_map/ppermute | solution.py:520
  127.8 8.5 %collective-permute-start.22 = (f32[280,128]{1,0:T(8,128)S(1)}, f32[280,128]{1,0:T(8,128)S(1)}, u32[]{:S(2)}, u32[]{:S(2)}) collective-permute-start(f32[280,128]{1,0:T(8,128)S(1)} %add_add_fusion.rest_10_), channel_id=1, source_target_pairs={{0,16},{8,24},{16,0},{24,8},{1,17},{9,25},{17,1},{25,9},{2,18},{10... | collective-permute-start | bytes 430088 | tf_op jit(solution)/shard_map/ppermute | solution.py:520
  128.3 7.9 %copy-start.13 = (f32[280,128]{1,0:T(8,128)}, f32[280,128]{1,0:T(8,128)S(1)}, u32[]{:S(2)}) copy-start(f32[280,128]{1,0:T(8,128)S(1)} %collective-permute-done.15.rest_7_) | copy-start | bytes 430084
  128.3 7.9 %collective-permute-start.23 = (f32[280,128]{1,0:T(8,128)S(1)}, f32[280,128]{1,0:T(8,128)S(1)}, u32[]{:S(2)}, u32[]{:S(2)}) collective-permute-start(f32[280,128]{1,0:T(8,128)S(1)} %add_add_fusion.rest_10_), channel_id=1, source_target_pairs={{0,24},{8,16},{16,8},{24,0},{1,25},{9,17},{17,9},{25,1},{2,26},{10... | collective-permute-start | bytes 430088 | tf_op jit(solution)/shard_map/ppermute | solution.py:520
  129.8 6.5 %copy-start.14 = (f32[280,128]{1,0:T(8,128)}, f32[280,128]{1,0:T(8,128)S(1)}, u32[]{:S(2)}) copy-start(f32[280,128]{1,0:T(8,128)S(1)} %collective-permute-done.16.rest_8_) | copy-start | bytes 430084
  129.8 6.5 %copy-start.15 = (f32[280,128]{1,0:T(8,128)}, f32[280,128]{1,0:T(8,128)S(1)}, u32[]{:S(2)}) copy-start(f32[280,128]{1,0:T(8,128)S(1)} %collective-permute-done.17.rest_9_) | copy-start | bytes 430084
  132.6 3.7 %copy-start.16 = (f32[280,128]{1,0:T(8,128)}, f32[280,128]{1,0:T(8,128)S(1)}, u32[]{:S(2)}) copy-start(f32[280,128]{1,0:T(8,128)S(1)} %collective-permute-done.21.rest_11_) | copy-start | bytes 430084
  136.3 0.7 copy-start.17
  136.9 0.7 copy-start.18

commit v4 on v3

--- a/solution.py
+++ b/solution.py
@@ -101,7 +101,16 @@
             copy.start()
 
 
-def adjoint_kernel(mask_ref, rec_ref, fh_ref, fl_ref, ih_ref, il_ref, sr_hbm, si_hbm, *rest):
+def column_masks(quarters, cols):
+    if not quarters:
+        return (0, 0)
+    index = lax.axis_index("sens")
+    bit0, bit1 = index & 1, index >> 1
+    unit = cols // 8
+    return ((2 * bit0 + bit1) * unit, (2 * bit1 + bit0) * unit)
+
+
+def adjoint_kernel(quarters, rec_ref, fh_ref, fl_ref, ih_ref, il_ref, sr_hbm, si_hbm, *rest):
     outs, (sr_ref, si_ref, sems, spread, rec_spec, adj) = rest[:-6], rest[-6:]
     sens_dev, cols, steps = rec_ref.shape
     bins, _, par_dev = sr_ref.shape
@@ -110,6 +119,7 @@
     padded = adj.shape[0] // cols // 2
     tall = 2 * padded
     half = cols // 2
+    masks = column_masks(quarters, cols)
     start_all((sr_hbm, si_hbm), (sr_ref, si_ref), sems, chunks, block)
 
     every = rec_ref[...].reshape(sens_dev * cols, steps)
@@ -128,7 +138,7 @@
             rec_spec[f, pl.ds(cols + c, bins, stride=2 * cols), :] = tile[padded : padded + bins]
         return 0
 
-    lax.fori_loop(0, cols, column, 0, unroll=4)
+    lax.fori_loop(0, cols, column, 0, unroll=True)
 
     def chunk_body(chunk, _):
         for copy in spec_copies((sr_hbm, si_hbm), (sr_ref, si_ref), sems, chunk, block):
@@ -153,7 +163,7 @@
             wide = []
             for e in range(2):
                 k = o * per + 2 * j + e
-                c = jnp.bitwise_xor(k, mask_ref[o * per // half])
+                c = k ^ masks[o * per // half]
                 wide.append(adj[pl.ds(pl.multiple_of(c * tall, 8), tall), :])
             ah, al = split(jnp.concatenate(wide, axis=1))
             ih, il = ih_ref[...], il_ref[...]
@@ -165,7 +175,7 @@
         lax.fori_loop(0, per // 2, pair, 0, unroll=True)
 
 
-def forward_kernel(packing, mask_ref, th_ref, tl_ref, ih_ref, il_ref, *rest):
+def forward_kernel(packing, quarters, th_ref, tl_ref, ih_ref, il_ref, *rest):
     keep_refs, send_refs = rest[-11:-9], rest[-9:-7]
     (sr_ref, si_ref, sems, whole_ref, field, pred, left) = rest[-7:]
     sr_hbm, si_hbm = rest[-13:-11]
@@ -177,6 +187,7 @@
     padded = pred.shape[1] // cols // 2
     tall = 2 * padded
     half = cols // 2
+    masks = column_masks(quarters, cols)
     full, width = packing.full, packing.full * LANES
     start_all((sr_hbm, si_hbm), (sr_ref, si_ref), sems, chunks, block)
 
@@ -184,7 +195,7 @@
     for p, piece in enumerate(pieces):
         for e in range(per):
             k = p * per + e
-            whole_ref[jnp.bitwise_xor(k, mask_ref[k // half])] = piece[e]
+            whole_ref[k ^ masks[k // half]] = piece[e]
     for row in list(range(bins, padded)) + list(range(padded + bins, tall)):
         for f in range(pred.shape[0]):
             pred[f, pl.ds(row, cols, stride=tall), :] = jnp.zeros((cols, LANES), F32)
@@ -211,8 +222,15 @@
             turned = jnp.concatenate([-x[cols:], x[:cols]], axis=0)
             xh, xl = split(jnp.concatenate([x, turned], axis=1))
             sh, sl = split(jnp.concatenate([sr_ref[w], si_ref[w]], axis=1))
-            both = dot_nt(jnp.concatenate([xh, xl], axis=0), sh)
-            value = both[: 2 * cols] + both[2 * cols :] + dot_nt(xh, sl)
+            data = jnp.concatenate(
+                [
+                    jnp.concatenate([xh, xh], axis=1),
+                    jnp.concatenate([xl, jnp.zeros_like(xl)], axis=1),
+                ],
+                axis=0,
+            )
+            both = dot_nt(jnp.concatenate([sh, sl], axis=1), data).T
+            value = both[: 2 * cols] + both[2 * cols :]
             for f, tile in enumerate(lane_tiles(value)):
                 pred[f, pl.ds(w, cols, stride=tall), :] = tile[:cols]
                 pred[f, pl.ds(padded + w, cols, stride=tall), :] = tile[cols:]
@@ -247,7 +265,7 @@
                 send_ref[pl.ds(row, count, stride=rows), :] = left[count:]
 
 
-def tables_kernel(packing, index_ref, map_ref, prior_ref, fh_ref, fl_ref, inv_ref,
+def tables_kernel(packing, map_ref, prior_ref, fh_ref, fl_ref, inv_ref,
                   select, th_ref, tl_ref, ih_ref, il_ref, table):
     blocks = select.shape[1] // packing.width
     times = inv_ref.shape[1]
@@ -262,7 +280,7 @@
         local = lane
         valid = lane >= 0
     for m in range(blocks):
-        owner = jnp.bitwise_xor(index_ref[0], m)
+        owner = lax.axis_index("sens") ^ m
         wanted = jnp.where(valid, owner * packing.sens_dev + local, -1)
         hit = map_ref[...] == wanted
         select[:, m * packing.width : (m + 1) * packing.width] = jnp.where(hit, 1.0, 0.0).astype(BF16)
@@ -273,10 +291,11 @@
     tl_ref[...] = tl
     par = inv_ref.shape[0]
     pairs = par // 2
+    place = lax.axis_index("par")
     for r in range(2):
         for d in range(pairs):
-            z = lax.rem(index_ref[1] // 2 + d, pairs)
-            core = jnp.bitwise_xor(lax.rem(index_ref[1], 2), r)
+            z = lax.rem(place // 2 + d, pairs)
+            core = lax.rem(place, 2) ^ r
             j = r * pairs + d
             table[j * times : (j + 1) * times, :] = inv_ref[2 * z + core]
     ih, il = split(table[...])
@@ -381,7 +400,6 @@
     bins, _, par_dev = spec_real.shape
     padded = round_up(bins, 8)
     sens, par = lax.axis_size("sens"), lax.axis_size("par")
-    sens_index, par_index = lax.axis_index("sens"), lax.axis_index("par")
     packing = Packing(cols // 2, sens_dev)
     rows_dev, times, sensors = inverse_rows.shape
     quarters = sens == 4 and cols % 8 == 0
@@ -393,14 +411,7 @@
     ih, il = (jnp.asarray(part) for part in split_host(inv))
     inv_blocks = jnp.asarray(inv.reshape(par, times, 2 * padded).astype(np.float32))
 
-    if quarters:
-        bit0, bit1 = sens_index & 1, sens_index >> 1
-        unit = cols // 8
-        mask = jnp.stack([(2 * bit0 + bit1) * unit, (2 * bit1 + bit0) * unit]).astype(jnp.int32)
-        n_out = 4
-    else:
-        mask = jnp.zeros((2,), jnp.int32)
-        n_out = 1
+    n_out = 4 if quarters else 1
 
     by_sensor = jnp.transpose(records, (1, 0, 2))
     by_time = jnp.transpose(inverse_rows, (1, 0, 2))
@@ -412,14 +423,13 @@
         pltpu.SemaphoreType.DMA((2, bins // block)),
     ]
     sens_tiles = -(-sens_dev // LANES)
-    smem = pl.BlockSpec(memory_space=pltpu.SMEM)
     phase_cost = pl.CostEstimate(
         flops=24 * cols * bins * sens_dev * par_dev, bytes_accessed=8 * bins * sens_dev * par_dev, transcendentals=0
     )
     out_a = [jax.ShapeDtypeStruct((cols // n_out, steps, par_dev), F32)] * n_out
     parts = pl.pallas_call(
-        adjoint_kernel,
-        in_specs=[smem, whole(by_sensor), whole(fh), whole(fl), whole(ih), whole(il), outside, outside],
+        functools.partial(adjoint_kernel, quarters),
+        in_specs=[whole(by_sensor), whole(fh), whole(fl), whole(ih), whole(il), outside, outside],
         out_specs=[whole(shape) for shape in out_a],
         out_shape=out_a,
         scratch_shapes=spec_scratch
@@ -431,25 +441,24 @@
         compiler_params=pltpu.CompilerParams(vmem_limit_bytes=limit),
         cost_estimate=phase_cost,
         name="adjoint",
-    )(mask, by_sensor, fh, fl, ih, il, spec_real, spec_imag)
-
-    index = jnp.stack([sens_index, par_index]).astype(jnp.int32)
-    *parts, index = lax.optimization_barrier((*parts, index))
+    )(by_sensor, fh, fl, ih, il, spec_real, spec_imag)
+
     time_block = block_of(times, 4)
     width = sens * packing.width
     moved = jax.ShapeDtypeStruct((times, rows_dev, width), BF16)
     folded = jax.ShapeDtypeStruct((2 * padded, steps), BF16)
     turned = jax.ShapeDtypeStruct((steps, 2 * padded), BF16)
     map_column = sensor_map.reshape(sensors, 1)
+    *parts, map_column = lax.optimization_barrier((*parts, map_column))
     chosen = jax.ShapeDtypeStruct((sensors, width), BF16)
     select, th, tl, ih2, il2 = pl.pallas_call(
         functools.partial(tables_kernel, packing),
-        in_specs=[smem, whole(map_column), whole(prior_cov), whole(fh), whole(fl), whole(inv_blocks)],
+        in_specs=[whole(map_column), whole(prior_cov), whole(fh), whole(fl), whole(inv_blocks)],
         out_shape=[chosen, folded, folded, turned, turned],
         scratch_shapes=[pltpu.VMEM((steps, 2 * padded), F32)],
         compiler_params=pltpu.CompilerParams(vmem_limit_bytes=limit),
         name="tables",
-    )(index, map_column, prior_cov, fh, fl, inv_blocks)
+    )(map_column, prior_cov, fh, fl, inv_blocks)
 
     blocks = times // time_block
     third = max(blocks // 3, 1)
@@ -494,8 +503,8 @@
     shard_rows = times * packing.rows
     half = jax.ShapeDtypeStruct((par // 2 * shard_rows, LANES), F32)
     keep0, keep1, send0, send1 = pl.pallas_call(
-        functools.partial(forward_kernel, packing),
-        in_specs=[smem, whole(th), whole(tl), whole(ih2), whole(il2)]
+        functools.partial(forward_kernel, packing, quarters),
+        in_specs=[whole(th), whole(tl), whole(ih2), whole(il2)]
         + [whole(piece) for piece in pieces]
         + [outside, outside],
         out_specs=[whole(half)] * 4,
@@ -510,7 +519,7 @@
         compiler_params=pltpu.CompilerParams(vmem_limit_bytes=limit),
         cost_estimate=phase_cost,
         name="forward",
-    )(mask, th, tl, ih2, il2, *pieces, spec_real, spec_imag)
+    )(th, tl, ih2, il2, *pieces, spec_real, spec_imag)
 
     def over_pairs(pair, d):
         there = pair[d * shard_rows : (d + 1) * shard_rows]
@@ -543,8 +552,7 @@
         ),
         name="update",
     )(*(pair[0] for pair in ready), *(pair[1] for pair in ready), *gathered)
-    per_dev = cols // par
-    spread = lax.all_to_all(partial.reshape(par, per_dev, rows_dev), "par", 0, 0)
+    spread = lax.all_to_all(partial.reshape(par, cols // par, rows_dev), "par", 0, 0)
     return jnp.sum(spread, axis=0)
 
 

time: 155 us -> 152 us (0.981)
  Pallas kernels: 79.2 us -> 76.6 us
    pallas_call x3, Pallas kernels: 53.7 us -> 51.1 us  [the longest x1 24.6 us: shards(): pl.pallas_call(functools.partial(forward_kernel, packing, quarters), in_s...]
  transfers between devices with their start and end apart: 24 -> 24, of which waited for: 10 -> 10; matrix products, arithmetic and copies ran while one was open for 1% -> 2% of each run, Pallas kernels for 14% -> 14%
where the time goes in v4:
time: 152 us; the launch traced here: 151 us
  Pallas kernels  76.6 us (50%)
  starting transfers between devices  31.3 us (21%)
  waiting for transfers between devices  28.3 us (19%)
  blocking collectives  8.84 us (6%)
  local copies, waits for them, and re-layouts  3.87 us (3%)
  other arithmetic  2 us (1%)
    pallas_call x1, Pallas kernels, shards(): pl.pallas_call(functools.partial(forward_kernel, packing, quarters), in_s...  24.6 us
    pallas_call x1, Pallas kernels, shards(): pl.pallas_call(functools.partial(adjoint_kernel, quarters), in_specs=[who...  23.2 us
    pallas_call x3, Pallas kernels, move_rows(): pl.pallas_call(rows_kernel, grid=(stop - start,), in_specs=[whole(chosen)...  18.2 us
    ppermute x6, waiting for transfers between devices, over_pairs(): lax.ppermute(there, 'par', [(k, (k + 2 * d) % par) for k in range(par)])  13.8 us
    ppermute x6, starting transfers between devices, over_pairs(): lax.ppermute(there, 'par', [(k, (k + 2 * d) % par) for k in range(par)])  11.8 us
    all_to_all x1, blocking collectives, shards(): lax.all_to_all(partial.reshape(par, cols // par, rows_dev), 'par', 0, 0)  8.84 us
    pallas_call x1, Pallas kernels, shards(): pl.pallas_call(functools.partial(update_kernel, packing, len(ready)), in_...  7.37 us
    ppermute x6, starting transfers between devices, over_sens(): lax.ppermute(mine, 'sens', swap(sens, m))  7.11 us
  transfers between devices with their start and end apart: 24, of which 10 were waited for; matrix products, arithmetic and copies ran while one was open for 2% of the time, Pallas kernels for 14%

profile of v4, /device:TPU:0, one launch (start us, length us, event | category | flops | bytes accessed | tf_op | source)
XLA Modules:
  0.0 151.2 jit_solution(898372847002304512)
XLA Ops:
  0.0 0.7 reshape.6
  0.7 23.2 %adjoint.1 = (f32[4,224,128]{2,1,0:T(8,128)}, f32[4,224,128]{2,1,0:T(8,128)}, f32[4,224,128]{2,1,0:T(8,128)}, f32[4,224,128]{2,1,0:T(8,128)}) custom-call(f32[150,16,224]{2,1,0:T(8,128)} %bitcast.6, bf16[464,224]{1,0:T(8,128)(2,1)} %constant.12.clone.fh_ref, bf16[464,224]{1,0:T(8,128)(2,1)} %constant.13.clone.fl_ref, ...), custom_call_target="tpu_custom_call" | custom-call | flops 1658880000 | bytes 34560000 | tf_op jit(solution)/shard_map/adjoint/pallas_call | solution.py:430
  23.9 3.0 %collective-permute-start = (f32[4,224,128]{2,1,0:T(8,128)}, f32[4,224,128]{2,1,0:T(8,128)S(1)}, u32[]{:S(2)}, u32[]{:S(2)}) collective-permute-start(f32[4,224,128]{2,1,0:T(8,128)} %get-tuple-element.51), channel_id=1, source_target_pairs={{0,8},{8,0},{16,24},{24,16},{1,9},{9,1},{17,25},{25,17},{2,10},{10... | collective-permute-start | bytes 1376264 | tf_op jit(solution)/shard_map/ppermute | solution.py:384
  26.9 1.6 %collective-permute-start.1 = (f32[4,224,128]{2,1,0:T(8,128)}, f32[4,224,128]{2,1,0:T(8,128)S(1)}, u32[]{:S(2)}, u32[]{:S(2)}) collective-permute-start(f32[4,224,128]{2,1,0:T(8,128)} %get-tuple-element.53), channel_id=1, source_target_pairs={{0,16},{8,24},{16,0},{24,8},{1,17},{9,25},{17,1},{25,9},{2,18},{10... | collective-permute-start | bytes 1376264 | tf_op jit(solution)/shard_map/ppermute | solution.py:384
  28.4 0.9 copy.12.map_ref
  29.3 3.2 %tables.1 = (bf16[600,1024]{1,0:T(8,128)(2,1)}, bf16[464,224]{1,0:T(8,128)(2,1)}, bf16[464,224]{1,0:T(8,128)(2,1)}, bf16[224,464]{1,0:T(8,128)(2,1)}, bf16[224,464]{1,0:T(8,128)(2,1)}) custom-call(s32[600,1]{1,0:T(8,128)} %copy.12.map_ref, f32[224,224]{1,0:T(8,128)} %prior_ref.1, bf16[464,224]{1,0:T(8,128)(2,1)} %constant.12.clone.fh_ref, ...), custom_call_target="tpu_custom_call" | custom-call | tf_op jit(solution)/shard_map/tables/pallas_call | solution.py:454
  32.6 5.6 %rows.3 = (bf16[8,96,1024]{2,1,0:T(8,128)(2,1)}, bf16[8,96,1024]{2,1,0:T(8,128)(2,1)}) custom-call(bf16[600,1024]{1,0:T(8,128)(2,1)} %get-tuple-element.67.select, f32[28,96,600]{2,1,0:T(8,128)} %bitcast.3), custom_call_target="tpu_custom_call" | custom-call | flops 1887436800 | bytes 3686400 | tf_op jit(solution)/shard_map/rows/pallas_call | solution.py:470
  38.2 0.0 collective-permute-done
  38.2 0.1 add.36
  38.2 0.8 collective-permute-done.1
  39.2 1.6 %collective-permute-start.2 = (f32[2,224,128]{2,1,0:T(8,128)S(1)}, f32[2,224,128]{2,1,0:T(8,128)S(1)}, u32[]{:S(2)}, u32[]{:S(2)}) collective-permute-start(f32[2,224,128]{2,1,0:T(8,128)S(1)} %slice.37), channel_id=1, source_target_pairs={{0,16},{8,24},{16,0},{24,8},{1,17},{9,25},{17,1},{25,9},{2,18},{10... | collective-permute-start | bytes 688136 | tf_op jit(solution)/shard_map/ppermute | solution.py:389
  40.8 0.6 collective-permute-start.3
  41.4 5.5 %rows.4 = (bf16[8,96,1024]{2,1,0:T(8,128)(2,1)}, bf16[8,96,1024]{2,1,0:T(8,128)(2,1)}) custom-call(bf16[600,1024]{1,0:T(8,128)(2,1)} %get-tuple-element.67.select, f32[28,96,600]{2,1,0:T(8,128)} %bitcast.4), custom_call_target="tpu_custom_call" | custom-call | flops 1887436800 | bytes 3686400 | tf_op jit(solution)/shard_map/rows/pallas_call | solution.py:470
  46.8 0.0 collective-permute-done.2
  46.9 0.0 collective-permute-done.3
  46.9 1.6 %collective-permute-start.4 = (f32[2,224,128]{2,1,0:T(8,128)S(1)}, f32[2,224,128]{2,1,0:T(8,128)S(1)}, u32[]{:S(2)}, u32[]{:S(2)}) collective-permute-start(f32[2,224,128]{2,1,0:T(8,128)S(1)} %slice_add_fusion.rest_4_), channel_id=1, source_target_pairs={{0,8},{8,0},{16,24},{24,16},{1,9},{9,1},{17,25},{25,17},{2,10},{10... | collective-permute-start | bytes 688136 | tf_op jit(solution)/shard_map/ppermute | solution.py:393
  48.5 0.5 collective-permute-start.6
  49.0 0.5 collective-permute-start.7
  49.5 1.6 %collective-permute-start.9 = (f32[2,224,128]{2,1,0:T(8,128)S(1)}, f32[2,224,128]{2,1,0:T(8,128)S(1)}, u32[]{:S(2)}, u32[]{:S(2)}) collective-permute-start(f32[2,224,128]{2,1,0:T(8,128)S(1)} %slice_add_fusion.rest_4_), channel_id=1, source_target_pairs={{0,16},{8,24},{16,0},{24,8},{1,17},{9,25},{17,1},{25,9},{2,18},{10... | collective-permute-start | bytes 688136 | tf_op jit(solution)/shard_map/ppermute | solution.py:394
  51.0 4.5 %collective-permute-done.4.rest_5_ = f32[2,224,128]{2,1,0:T(8,128)S(1)} collective-permute-done((f32[2,224,128]{2,1,0:T(8,128)S(1)}, f32[2,224,128]{2,1,0:T(8,128)S(1)}, u32[]{:S(2)}, u32[]{:S(2)}) %collective-permute-start.4) | collective-permute-done | bytes 229408 | tf_op jit(solution)/shard_map/ppermute | solution.py:393
  55.5 0.5 collective-permute-start.5
  56.0 1.0 collective-permute-done.6.rest_1_
  57.0 0.5 collective-permute-start.8
  57.6 7.1 %rows.5 = (bf16[12,96,1024]{2,1,0:T(8,128)(2,1)}, bf16[12,96,1024]{2,1,0:T(8,128)(2,1)}) custom-call(bf16[600,1024]{1,0:T(8,128)(2,1)} %get-tuple-element.67.select, f32[28,96,600]{2,1,0:T(8,128)} %bitcast.5), custom_call_target="tpu_custom_call" | custom-call | flops 2831155200 | bytes 5529600 | tf_op jit(solution)/shard_map/rows/pallas_call | solution.py:470
  64.7 0.0 collective-permute-done.5.rest_7_
  64.7 0.0 collective-permute-done.7.rest_2_
  64.8 0.0 collective-permute-done.9.rest_6_
  64.8 0.0 collective-permute-done.8.rest_3_
  64.8 0.6 copy-done.11
  65.4 0.1 copy-done.9
  65.5 0.1 copy-done.10
  65.6 0.1 copy-done.12
  65.7 24.6 %forward.1 = (f32[1120,128]{1,0:T(8,128)}, f32[1120,128]{1,0:T(8,128)}, f32[1120,128]{1,0:T(8,128)}, f32[1120,128]{1,0:T(8,128)}) custom-call(bf16[464,224]{1,0:T(8,128)(2,1)} %get-tuple-element.74.th_ref, bf16[464,224]{1,0:T(8,128)(2,1)} %get-tuple-element.75.tl_ref, bf16[224,464]{1,0:T(8,128)(2,1)} %get-tuple-element.76.ih_ref, ...), custom_call_target="tpu_custom_call" | custom-call | flops 1658880000 | bytes 34560000 | tf_op jit(solution)/shard_map/forward/pallas_call | solution.py:505
  90.3 0.1 collective-permute-start.10
  90.4 0.5 collective-permute-start.13
  90.9 1.7 %collective-permute-done.10 = f32[1120,128]{1,0:T(8,128)S(1)} collective-permute-done((f32[1120,128]{1,0:T(8,128)}, f32[1120,128]{1,0:T(8,128)S(1)}, u32[]{:S(2)}, u32[]{:S(2)}) %collective-permute-start.10) | collective-permute-done | bytes 573472 | tf_op jit(solution)/shard_map/ppermute | solution.py:531
  92.6 1.1 add.40
  93.7 1.6 %collective-permute-start.11 = (f32[280,128]{1,0:T(8,128)S(1)}, f32[280,128]{1,0:T(8,128)S(1)}, u32[]{:S(2)}, u32[]{:S(2)}) collective-permute-start(f32[280,128]{1,0:T(8,128)S(1)} %get-tuple-element.92), channel_id=1, source_target_pairs={{0,2},{1,3},{2,4},{3,5},{4,6},{5,7},{6,0},{7,1},{8,10},{9,11},{10,... | collective-permute-start | bytes 430088 | tf_op jit(solution)/shard_map/ppermute | solution.py:526
  95.4 2.3 %collective-permute-start.12 = (f32[280,128]{1,0:T(8,128)S(1)}, f32[280,128]{1,0:T(8,128)S(1)}, u32[]{:S(2)}, u32[]{:S(2)}) collective-permute-start(f32[280,128]{1,0:T(8,128)S(1)} %get-tuple-element.91), channel_id=1, source_target_pairs={{0,6},{1,7},{2,0},{3,1},{4,2},{5,3},{6,4},{7,5},{8,14},{9,15},{10,... | collective-permute-start | bytes 430088 | tf_op jit(solution)/shard_map/ppermute | solution.py:526
  97.6 0.8 collective-permute-start.14
  98.4 0.0 collective-permute-done.13
  98.4 0.1 add.41
  98.5 3.8 %collective-permute-done.11 = f32[280,128]{1,0:T(8,128)S(1)} collective-permute-done((f32[280,128]{1,0:T(8,128)S(1)}, f32[280,128]{1,0:T(8,128)S(1)}, u32[]{:S(2)}, u32[]{:S(2)}) %collective-permute-start.11) | collective-permute-done | bytes 143392 | tf_op jit(solution)/shard_map/ppermute | solution.py:526
  102.2 1.7 %collective-permute-done.12 = f32[280,128]{1,0:T(8,128)S(1)} collective-permute-done((f32[280,128]{1,0:T(8,128)S(1)}, f32[280,128]{1,0:T(8,128)S(1)}, u32[]{:S(2)}, u32[]{:S(2)}) %collective-permute-start.12) | collective-permute-done | bytes 143392 | tf_op jit(solution)/shard_map/ppermute | solution.py:526
  104.0 3.0 %collective-permute-start.20 = (f32[280,128]{1,0:T(8,128)S(1)}, f32[280,128]{1,0:T(8,128)S(1)}, u32[]{:S(2)}, u32[]{:S(2)}) collective-permute-start(f32[280,128]{1,0:T(8,128)S(1)} %get-tuple-element.88), channel_id=1, source_target_pairs={{0,6},{1,7},{2,0},{3,1},{4,2},{5,3},{6,4},{7,5},{8,14},{9,15},{10,... | collective-permute-start | bytes 430088 | tf_op jit(solution)/shard_map/ppermute | solution.py:526
  107.0 0.1 collective-permute-start.18
  107.1 4.0 %collective-permute-start.19 = (f32[280,128]{1,0:T(8,128)S(1)}, f32[280,128]{1,0:T(8,128)S(1)}, u32[]{:S(2)}, u32[]{:S(2)}) collective-permute-start(f32[280,128]{1,0:T(8,128)S(1)} %get-tuple-element.87), channel_id=1, source_target_pairs={{0,4},{1,5},{2,6},{3,7},{4,0},{5,1},{6,2},{7,3},{8,12},{9,13},{10,... | collective-permute-start | bytes 430088 | tf_op jit(solution)/shard_map/ppermute | solution.py:526
  111.1 2.8 %collective-permute-done.14 = f32[280,128]{1,0:T(8,128)S(1)} collective-permute-done((f32[280,128]{1,0:T(8,128)S(1)}, f32[280,128]{1,0:T(8,128)S(1)}, u32[]{:S(2)}, u32[]{:S(2)}) %collective-permute-start.14) | collective-permute-done | bytes 143392 | tf_op jit(solution)/shard_map/ppermute | solution.py:526
  114.0 1.5 %collective-permute-start.15 = (f32[280,128]{1,0:T(8,128)S(1)}, f32[280,128]{1,0:T(8,128)S(1)}, u32[]{:S(2)}, u32[]{:S(2)}) collective-permute-start(f32[280,128]{1,0:T(8,128)S(1)} %slice_add_fusion.2.rest_6_), channel_id=1, source_target_pairs={{0,8},{8,0},{16,24},{24,16},{1,9},{9,1},{17,25},{25,17},{2,10},{10... | collective-permute-start | bytes 430088 | tf_op jit(solution)/shard_map/ppermute | solution.py:529
  115.5 0.6 collective-permute-start.16
  116.1 0.0 collective-permute-done.20
  116.1 1.5 collective-permute-start.17
  117.6 0.0 collective-permute-done.18
  117.6 5.5 %collective-permute-done.19 = f32[280,128]{1,0:T(8,128)S(1)} collective-permute-done((f32[280,128]{1,0:T(8,128)S(1)}, f32[280,128]{1,0:T(8,128)S(1)}, u32[]{:S(2)}, u32[]{:S(2)}) %collective-permute-start.19) | collective-permute-done | bytes 143392 | tf_op jit(solution)/shard_map/ppermute | solution.py:526
  123.1 1.5 %collective-permute-start.21 = (f32[280,128]{1,0:T(8,128)S(1)}, f32[280,128]{1,0:T(8,128)S(1)}, u32[]{:S(2)}, u32[]{:S(2)}) collective-permute-start(f32[280,128]{1,0:T(8,128)S(1)} %add_add_fusion.rest_10_), channel_id=1, source_target_pairs={{0,8},{8,0},{16,24},{24,16},{1,9},{9,1},{17,25},{25,17},{2,10},{10... | collective-permute-start | bytes 430088 | tf_op jit(solution)/shard_map/ppermute | solution.py:529
  124.6 0.6 collective-permute-start.22
  125.2 1.5 collective-permute-start.23
  126.7 2.8 %collective-permute-done.21.rest_11_ = f32[280,128]{1,0:T(8,128)S(1)} collective-permute-done((f32[280,128]{1,0:T(8,128)S(1)}, f32[280,128]{1,0:T(8,128)S(1)}, u32[]{:S(2)}, u32[]{:S(2)}) %collective-permute-start.21) | collective-permute-done | bytes 143392 | tf_op jit(solution)/shard_map/ppermute | solution.py:529
  129.5 3.6 %collective-permute-done.22.rest_12_ = f32[280,128]{1,0:T(8,128)S(1)} collective-permute-done((f32[280,128]{1,0:T(8,128)S(1)}, f32[280,128]{1,0:T(8,128)S(1)}, u32[]{:S(2)}, u32[]{:S(2)}) %collective-permute-start.22) | collective-permute-done | bytes 143392 | tf_op jit(solution)/shard_map/ppermute | solution.py:529
  133.2 0.6 copy-done.17
  133.8 0.7 copy-done.18
  134.4 7.4 %update.1 = f32[16,96]{1,0:T(8,128)} custom-call(bf16[8,96,1024]{2,1,0:T(8,128)(2,1)} %get-tuple-element.59.rest_0_, bf16[8,96,1024]{2,1,0:T(8,128)(2,1)} %get-tuple-element.65.rest_1_, bf16[12,96,1024]{2,1,0:T(8,128)(2,1)} %get-tuple-element.70.rest_2_, bf16[8,96,1024]{2,1,0:T(8,128)(2,1)} %get-tuple-element.71.rest_3_, ...), custom_call_target="tpu_custom_call" | custom-call | flops 264241152 | bytes 11010048 | tf_op jit(solution)/shard_map/update/pallas_call | solution.py:540
  141.8 8.8 %all_to_all.5 = f32[8,2,96]{2,1,0:T(2,128)S(1)} all-to-all(f32[8,2,96]{2,1,0:T(2,128)} %bitcast.7), channel_id=1, replica_groups=mesh['sens'=4,'par'=8] {'par'}, dimensions={0} | all-to-all | bytes 12288 | tf_op jit(solution)/shard_map/all_to_all | solution.py:555
  150.6 0.6 reduce_sum.9
  (45 shorter events, 0.4 us)
Async XLA Ops:
  23.9 14.3 %collective-permute-start = (f32[4,224,128]{2,1,0:T(8,128)}, f32[4,224,128]{2,1,0:T(8,128)S(1)}, u32[]{:S(2)}, u32[]{:S(2)}) collective-permute-start(f32[4,224,128]{2,1,0:T(8,128)} %get-tuple-element.51), channel_id=1, source_target_pairs={{0,8},{8,0},{16,24},{24,16},{1,9},{9,1},{17,25},{25,17},{2,10},{10... | collective-permute-start | bytes 1376264 | tf_op jit(solution)/shard_map/ppermute | solution.py:384
  26.9 12.2 %collective-permute-start.1 = (f32[4,224,128]{2,1,0:T(8,128)}, f32[4,224,128]{2,1,0:T(8,128)S(1)}, u32[]{:S(2)}, u32[]{:S(2)}) collective-permute-start(f32[4,224,128]{2,1,0:T(8,128)} %get-tuple-element.53), channel_id=1, source_target_pairs={{0,16},{8,24},{16,0},{24,8},{1,17},{9,25},{17,1},{25,9},{2,18},{10... | collective-permute-start | bytes 1376264 | tf_op jit(solution)/shard_map/ppermute | solution.py:384
  32.6 5.6 %copy-start.6 = (f32[4,224,128]{2,1,0:T(8,128)S(1)}, f32[4,224,128]{2,1,0:T(8,128)}, u32[]{:S(2)}) copy-start(f32[4,224,128]{2,1,0:T(8,128)} %get-tuple-element.50) | copy-start | bytes 1376260
  32.6 6.5 %copy-start.5 = (f32[4,224,128]{2,1,0:T(8,128)S(1)}, f32[4,224,128]{2,1,0:T(8,128)}, u32[]{:S(2)}) copy-start(f32[4,224,128]{2,1,0:T(8,128)} %get-tuple-element.52) | copy-start | bytes 1376260
  39.2 7.7 %collective-permute-start.2 = (f32[2,224,128]{2,1,0:T(8,128)S(1)}, f32[2,224,128]{2,1,0:T(8,128)S(1)}, u32[]{:S(2)}, u32[]{:S(2)}) collective-permute-start(f32[2,224,128]{2,1,0:T(8,128)S(1)} %slice.37), channel_id=1, source_target_pairs={{0,16},{8,24},{16,0},{24,8},{1,17},{9,25},{17,1},{25,9},{2,18},{10... | collective-permute-start | bytes 688136 | tf_op jit(solution)/shard_map/ppermute | solution.py:389
  40.8 6.1 %collective-permute-start.3 = (f32[2,224,128]{2,1,0:T(8,128)S(1)}, f32[2,224,128]{2,1,0:T(8,128)S(1)}, u32[]{:S(2)}, u32[]{:S(2)}) collective-permute-start(f32[2,224,128]{2,1,0:T(8,128)S(1)} %slice.39), channel_id=1, source_target_pairs={{0,8},{8,0},{16,24},{24,16},{1,9},{9,1},{17,25},{25,17},{2,10},{10... | collective-permute-start | bytes 688136 | tf_op jit(solution)/shard_map/ppermute | solution.py:389
  46.9 17.8 %copy-start = (f32[2,224,128]{2,1,0:T(8,128)}, f32[2,224,128]{2,1,0:T(8,128)S(1)}, u32[]{:S(2)}) copy-start(f32[2,224,128]{2,1,0:T(8,128)S(1)} %slice_add_fusion.1.rest_0_) | copy-start | bytes 688132
  46.9 17.8 %copy-start.1 = (f32[2,224,128]{2,1,0:T(8,128)}, f32[2,224,128]{2,1,0:T(8,128)S(1)}, u32[]{:S(2)}) copy-start(f32[2,224,128]{2,1,0:T(8,128)S(1)} %slice_add_fusion.rest_4_) | copy-start | bytes 688132
  46.9 8.6 %collective-permute-start.4 = (f32[2,224,128]{2,1,0:T(8,128)S(1)}, f32[2,224,128]{2,1,0:T(8,128)S(1)}, u32[]{:S(2)}, u32[]{:S(2)}) collective-permute-start(f32[2,224,128]{2,1,0:T(8,128)S(1)} %slice_add_fusion.rest_4_), channel_id=1, source_target_pairs={{0,8},{8,0},{16,24},{24,16},{1,9},{9,1},{17,25},{25,17},{2,10},{10... | collective-permute-start | bytes 688136 | tf_op jit(solution)/shard_map/ppermute | solution.py:393
  48.5 8.5 %collective-permute-start.6 = (f32[2,224,128]{2,1,0:T(8,128)S(1)}, f32[2,224,128]{2,1,0:T(8,128)S(1)}, u32[]{:S(2)}, u32[]{:S(2)}) collective-permute-start(f32[2,224,128]{2,1,0:T(8,128)S(1)} %slice_add_fusion.1.rest_0_), channel_id=1, source_target_pairs={{0,16},{8,24},{16,0},{24,8},{1,17},{9,25},{17,1},{25,9},{2,18},{10... | collective-permute-start | bytes 688136 | tf_op jit(solution)/shard_map/ppermute | solution.py:393
  49.0 15.7 %collective-permute-start.7 = (f32[2,224,128]{2,1,0:T(8,128)S(1)}, f32[2,224,128]{2,1,0:T(8,128)S(1)}, u32[]{:S(2)}, u32[]{:S(2)}) collective-permute-start(f32[2,224,128]{2,1,0:T(8,128)S(1)} %slice_add_fusion.1.rest_0_), channel_id=1, source_target_pairs={{0,8},{8,0},{16,24},{24,16},{1,9},{9,1},{17,25},{25,17},{2,10},{10... | collective-permute-start | bytes 688136 | tf_op jit(solution)/shard_map/ppermute | solution.py:394
  49.5 15.3 %collective-permute-start.9 = (f32[2,224,128]{2,1,0:T(8,128)S(1)}, f32[2,224,128]{2,1,0:T(8,128)S(1)}, u32[]{:S(2)}, u32[]{:S(2)}) collective-permute-start(f32[2,224,128]{2,1,0:T(8,128)S(1)} %slice_add_fusion.rest_4_), channel_id=1, source_target_pairs={{0,16},{8,24},{16,0},{24,8},{1,17},{9,25},{17,1},{25,9},{2,18},{10... | collective-permute-start | bytes 688136 | tf_op jit(solution)/shard_map/ppermute | solution.py:394
  55.5 9.2 %copy-start.7 = (f32[2,224,128]{2,1,0:T(8,128)}, f32[2,224,128]{2,1,0:T(8,128)S(1)}, u32[]{:S(2)}) copy-start(f32[2,224,128]{2,1,0:T(8,128)S(1)} %collective-permute-done.4.rest_5_) | copy-start | bytes 688132
  55.5 9.2 %collective-permute-start.5 = (f32[2,224,128]{2,1,0:T(8,128)S(1)}, f32[2,224,128]{2,1,0:T(8,128)S(1)}, u32[]{:S(2)}, u32[]{:S(2)}) collective-permute-start(f32[2,224,128]{2,1,0:T(8,128)S(1)} %collective-permute-done.4.rest_5_), channel_id=1, source_target_pairs={{0,16},{8,24},{16,0},{24,8},{1,17},{9,25},{17,1},{25,9},{2,18},{10... | collective-permute-start | bytes 688136 | tf_op jit(solution)/shard_map/ppermute | solution.py:395
  57.0 7.7 %copy-start.8 = (f32[2,224,128]{2,1,0:T(8,128)}, f32[2,224,128]{2,1,0:T(8,128)S(1)}, u32[]{:S(2)}) copy-start(f32[2,224,128]{2,1,0:T(8,128)S(1)} %collective-permute-done.6.rest_1_) | copy-start | bytes 688132
  57.0 7.8 %collective-permute-start.8 = (f32[2,224,128]{2,1,0:T(8,128)S(1)}, f32[2,224,128]{2,1,0:T(8,128)S(1)}, u32[]{:S(2)}, u32[]{:S(2)}) collective-permute-start(f32[2,224,128]{2,1,0:T(8,128)S(1)} %collective-permute-done.6.rest_1_), channel_id=1, source_target_pairs={{0,8},{8,0},{16,24},{24,16},{1,9},{9,1},{17,25},{25,17},{2,10},{10... | collective-permute-start | bytes 688136 | tf_op jit(solution)/shard_map/ppermute | solution.py:395
  64.7 0.7 copy-start.11
  64.7 0.8 copy-start.9
  64.8 0.8 copy-start.10
  64.8 0.9 copy-start.12
  90.3 8.1 %copy-start.2 = (f32[1120,128]{1,0:T(8,128)S(1)}, f32[1120,128]{1,0:T(8,128)}, u32[]{:S(2)}) copy-start(f32[1120,128]{1,0:T(8,128)} %get-tuple-element.82) | copy-start | bytes 1720324
  90.3 2.3 %collective-permute-start.10 = (f32[1120,128]{1,0:T(8,128)}, f32[1120,128]{1,0:T(8,128)S(1)}, u32[]{:S(2)}, u32[]{:S(2)}) collective-permute-start(f32[1120,128]{1,0:T(8,128)} %get-tuple-element.81), channel_id=1, source_target_pairs={{0,1},{1,0},{2,3},{3,2},{4,5},{5,4},{6,7},{7,6},{8,9},{9,8},{10,11... | collective-permute-start | bytes 1720328 | tf_op jit(solution)/shard_map/ppermute | solution.py:531
  90.4 8.0 %collective-permute-start.13 = (f32[1120,128]{1,0:T(8,128)}, f32[1120,128]{1,0:T(8,128)S(1)}, u32[]{:S(2)}, u32[]{:S(2)}) collective-permute-start(f32[1120,128]{1,0:T(8,128)} %get-tuple-element.83), channel_id=1, source_target_pairs={{0,1},{1,0},{2,3},{3,2},{4,5},{5,4},{6,7},{7,6},{8,9},{9,8},{10,11... | collective-permute-start | bytes 1720328 | tf_op jit(solution)/shard_map/ppermute | solution.py:532
  93.7 8.5 %collective-permute-start.11 = (f32[280,128]{1,0:T(8,128)S(1)}, f32[280,128]{1,0:T(8,128)S(1)}, u32[]{:S(2)}, u32[]{:S(2)}) collective-permute-start(f32[280,128]{1,0:T(8,128)S(1)} %get-tuple-element.92), channel_id=1, source_target_pairs={{0,2},{1,3},{2,4},{3,5},{4,6},{5,7},{6,0},{7,1},{8,10},{9,11},{10,... | collective-permute-start | bytes 430088 | tf_op jit(solution)/shard_map/ppermute | solution.py:526
  95.4 8.6 %collective-permute-start.12 = (f32[280,128]{1,0:T(8,128)S(1)}, f32[280,128]{1,0:T(8,128)S(1)}, u32[]{:S(2)}, u32[]{:S(2)}) collective-permute-start(f32[280,128]{1,0:T(8,128)S(1)} %get-tuple-element.91), channel_id=1, source_target_pairs={{0,6},{1,7},{2,0},{3,1},{4,2},{5,3},{6,4},{7,5},{8,14},{9,15},{10,... | collective-permute-start | bytes 430088 | tf_op jit(solution)/shard_map/ppermute | solution.py:526
  97.6 16.3 %collective-permute-start.14 = (f32[280,128]{1,0:T(8,128)S(1)}, f32[280,128]{1,0:T(8,128)S(1)}, u32[]{:S(2)}, u32[]{:S(2)}) collective-permute-start(f32[280,128]{1,0:T(8,128)S(1)} %get-tuple-element.90), channel_id=1, source_target_pairs={{0,4},{1,5},{2,6},{3,7},{4,0},{5,1},{6,2},{7,3},{8,12},{9,13},{10,... | collective-permute-start | bytes 430088 | tf_op jit(solution)/shard_map/ppermute | solution.py:526
  104.0 12.1 %collective-permute-start.20 = (f32[280,128]{1,0:T(8,128)S(1)}, f32[280,128]{1,0:T(8,128)S(1)}, u32[]{:S(2)}, u32[]{:S(2)}) collective-permute-start(f32[280,128]{1,0:T(8,128)S(1)} %get-tuple-element.88), channel_id=1, source_target_pairs={{0,6},{1,7},{2,0},{3,1},{4,2},{5,3},{6,4},{7,5},{8,14},{9,15},{10,... | collective-permute-start | bytes 430088 | tf_op jit(solution)/shard_map/ppermute | solution.py:526
  107.0 10.5 %collective-permute-start.18 = (f32[280,128]{1,0:T(8,128)S(1)}, f32[280,128]{1,0:T(8,128)S(1)}, u32[]{:S(2)}, u32[]{:S(2)}) collective-permute-start(f32[280,128]{1,0:T(8,128)S(1)} %get-tuple-element.89), channel_id=1, source_target_pairs={{0,2},{1,3},{2,4},{3,5},{4,6},{5,7},{6,0},{7,1},{8,10},{9,11},{10,... | collective-permute-start | bytes 430088 | tf_op jit(solution)/shard_map/ppermute | solution.py:526
  107.1 16.0 %collective-permute-start.19 = (f32[280,128]{1,0:T(8,128)S(1)}, f32[280,128]{1,0:T(8,128)S(1)}, u32[]{:S(2)}, u32[]{:S(2)}) collective-permute-start(f32[280,128]{1,0:T(8,128)S(1)} %get-tuple-element.87), channel_id=1, source_target_pairs={{0,4},{1,5},{2,6},{3,7},{4,0},{5,1},{6,2},{7,3},{8,12},{9,13},{10,... | collective-permute-start | bytes 430088 | tf_op jit(solution)/shard_map/ppermute | solution.py:526
  114.0 19.1 %copy-start.3 = (f32[280,128]{1,0:T(8,128)}, f32[280,128]{1,0:T(8,128)S(1)}, u32[]{:S(2)}) copy-start(f32[280,128]{1,0:T(8,128)S(1)} %slice_add_fusion.2.rest_6_) | copy-start | bytes 430084
  114.0 11.2 %collective-permute-start.15 = (f32[280,128]{1,0:T(8,128)S(1)}, f32[280,128]{1,0:T(8,128)S(1)}, u32[]{:S(2)}, u32[]{:S(2)}) collective-permute-start(f32[280,128]{1,0:T(8,128)S(1)} %slice_add_fusion.2.rest_6_), channel_id=1, source_target_pairs={{0,8},{8,0},{16,24},{24,16},{1,9},{9,1},{17,25},{25,17},{2,10},{10... | collective-permute-start | bytes 430088 | tf_op jit(solution)/shard_map/ppermute | solution.py:529
  115.5 11.2 %collective-permute-start.16 = (f32[280,128]{1,0:T(8,128)S(1)}, f32[280,128]{1,0:T(8,128)S(1)}, u32[]{:S(2)}, u32[]{:S(2)}) collective-permute-start(f32[280,128]{1,0:T(8,128)S(1)} %slice_add_fusion.2.rest_6_), channel_id=1, source_target_pairs={{0,16},{8,24},{16,0},{24,8},{1,17},{9,25},{17,1},{25,9},{2,18},{10... | collective-permute-start | bytes 430088 | tf_op jit(solution)/shard_map/ppermute | solution.py:529
  116.1 10.6 %collective-permute-start.17 = (f32[280,128]{1,0:T(8,128)S(1)}, f32[280,128]{1,0:T(8,128)S(1)}, u32[]{:S(2)}, u32[]{:S(2)}) collective-permute-start(f32[280,128]{1,0:T(8,128)S(1)} %slice_add_fusion.2.rest_6_), channel_id=1, source_target_pairs={{0,24},{8,16},{16,8},{24,0},{1,25},{9,17},{17,9},{25,1},{2,26},{10... | collective-permute-start | bytes 430088 | tf_op jit(solution)/shard_map/ppermute | solution.py:529
  123.1 10.0 %copy-start.4 = (f32[280,128]{1,0:T(8,128)}, f32[280,128]{1,0:T(8,128)S(1)}, u32[]{:S(2)}) copy-start(f32[280,128]{1,0:T(8,128)S(1)} %add_add_fusion.rest_10_) | copy-start | bytes 430084
  123.1 6.4 %collective-permute-start.21 = (f32[280,128]{1,0:T(8,128)S(1)}, f32[280,128]{1,0:T(8,128)S(1)}, u32[]{:S(2)}, u32[]{:S(2)}) collective-permute-start(f32[280,128]{1,0:T(8,128)S(1)} %add_add_fusion.rest_10_), channel_id=1, source_target_pairs={{0,8},{8,0},{16,24},{24,16},{1,9},{9,1},{17,25},{25,17},{2,10},{10... | collective-permute-start | bytes 430088 | tf_op jit(solution)/shard_map/ppermute | solution.py:529
  124.6 8.5 %collective-permute-start.22 = (f32[280,128]{1,0:T(8,128)S(1)}, f32[280,128]{1,0:T(8,128)S(1)}, u32[]{:S(2)}, u32[]{:S(2)}) collective-permute-start(f32[280,128]{1,0:T(8,128)S(1)} %add_add_fusion.rest_10_), channel_id=1, source_target_pairs={{0,16},{8,24},{16,0},{24,8},{1,17},{9,25},{17,1},{25,9},{2,18},{10... | collective-permute-start | bytes 430088 | tf_op jit(solution)/shard_map/ppermute | solution.py:529
  125.2 7.9 %copy-start.13 = (f32[280,128]{1,0:T(8,128)}, f32[280,128]{1,0:T(8,128)S(1)}, u32[]{:S(2)}) copy-start(f32[280,128]{1,0:T(8,128)S(1)} %collective-permute-done.15.rest_7_) | copy-start | bytes 430084
  125.2 7.9 %collective-permute-start.23 = (f32[280,128]{1,0:T(8,128)S(1)}, f32[280,128]{1,0:T(8,128)S(1)}, u32[]{:S(2)}, u32[]{:S(2)}) collective-permute-start(f32[280,128]{1,0:T(8,128)S(1)} %add_add_fusion.rest_10_), channel_id=1, source_target_pairs={{0,24},{8,16},{16,8},{24,0},{1,25},{9,17},{17,9},{25,1},{2,26},{10... | collective-permute-start | bytes 430088 | tf_op jit(solution)/shard_map/ppermute | solution.py:529
  126.7 6.5 %copy-start.14 = (f32[280,128]{1,0:T(8,128)}, f32[280,128]{1,0:T(8,128)S(1)}, u32[]{:S(2)}) copy-start(f32[280,128]{1,0:T(8,128)S(1)} %collective-permute-done.16.rest_8_) | copy-start | bytes 430084
  126.7 6.5 %copy-start.15 = (f32[280,128]{1,0:T(8,128)}, f32[280,128]{1,0:T(8,128)S(1)}, u32[]{:S(2)}) copy-start(f32[280,128]{1,0:T(8,128)S(1)} %collective-permute-done.17.rest_9_) | copy-start | bytes 430084
  129.5 3.6 %copy-start.16 = (f32[280,128]{1,0:T(8,128)}, f32[280,128]{1,0:T(8,128)S(1)}, u32[]{:S(2)}) copy-start(f32[280,128]{1,0:T(8,128)S(1)} %collective-permute-done.21.rest_11_) | copy-start | bytes 430084
  133.1 0.6 copy-start.17
  133.8 0.7 copy-start.18

commit v5 on v4

--- a/solution.py
+++ b/solution.py
@@ -531,7 +531,6 @@
     pair0 = keep0 + lax.ppermute(send0, "par", swap(par, 1))
     pair1 = keep1 + lax.ppermute(send1, "par", swap(par, 1))
     come = [over_pairs(pair0, d) for d in range(1, par // 2)]
-    come[0], come[-1], pair1 = lax.optimization_barrier((come[0], come[-1], pair1))
     mine0 = pair0[:shard_rows] + sum(come[1:], come[0])
     mine1 = pair1[:shard_rows] + sum(over_pairs(pair1, d) for d in range(1, par // 2))
     gathered = over_sens(mine0) + over_sens(mine1)

time: 152 us -> 150 us (0.987)
  starting transfers between devices: 31.3 us -> 29.1 us
    ppermute x6, starting transfers between devices: 11.8 us -> 9.61 us  [over_pairs(): lax.ppermute(there, 'par', [(k, (k + 2 * d) % par) for k in range(par)])]
  transfers between devices with their start and end apart: 24 -> 24, of which waited for: 10 -> 9; matrix products, arithmetic and copies ran while one was open for 2% -> 2% of each run, Pallas kernels for 14% -> 14%
where the time goes in v5:
time: 150 us
  Pallas kernels  76.6 us (51%)
  starting transfers between devices  29.1 us (19%)
  waiting for transfers between devices  28.8 us (19%)
  blocking collectives  9.28 us (6%)
  local copies, waits for them, and re-layouts  3.87 us (3%)
  other arithmetic  2.01 us (1%)
    pallas_call x1, Pallas kernels, shards(): pl.pallas_call(functools.partial(forward_kernel, packing, quarters), in_s...  24.6 us
    pallas_call x1, Pallas kernels, shards(): pl.pallas_call(functools.partial(adjoint_kernel, quarters), in_specs=[who...  23.2 us
    pallas_call x3, Pallas kernels, move_rows(): pl.pallas_call(rows_kernel, grid=(stop - start,), in_specs=[whole(chosen)...  18.2 us
    ppermute x6, waiting for transfers between devices, over_pairs(): lax.ppermute(there, 'par', [(k, (k + 2 * d) % par) for k in range(par)])  15.2 us
    ppermute x6, starting transfers between devices, over_pairs(): lax.ppermute(there, 'par', [(k, (k + 2 * d) % par) for k in range(par)])  9.61 us
    all_to_all x1, blocking collectives, shards(): lax.all_to_all(partial.reshape(par, cols // par, rows_dev), 'par', 0, 0)  9.28 us
    pallas_call x1, Pallas kernels, shards(): pl.pallas_call(functools.partial(update_kernel, packing, len(ready)), in_...  7.38 us
    ppermute x6, starting transfers between devices, over_sens(): lax.ppermute(mine, 'sens', swap(sens, m))  7.11 us
  transfers between devices with their start and end apart: 24, of which 9 were waited for; matrix products, arithmetic and copies ran while one was open for 2% of the time, Pallas kernels for 14%

profile of v5, /device:TPU:0, one launch (start us, length us, event | category | flops | bytes accessed | tf_op | source)
XLA Modules:
  0.0 150.0 jit_solution(4314880698696941652)
XLA Ops:
  0.0 0.7 reshape.6
  0.7 23.2 %adjoint.1 = (f32[4,224,128]{2,1,0:T(8,128)}, f32[4,224,128]{2,1,0:T(8,128)}, f32[4,224,128]{2,1,0:T(8,128)}, f32[4,224,128]{2,1,0:T(8,128)}) custom-call(f32[150,16,224]{2,1,0:T(8,128)} %bitcast.6, bf16[464,224]{1,0:T(8,128)(2,1)} %constant.12.clone.fh_ref, bf16[464,224]{1,0:T(8,128)(2,1)} %constant.13.clone.fl_ref, ...), custom_call_target="tpu_custom_call" | custom-call | flops 1658880000 | bytes 34560000 | tf_op jit(solution)/shard_map/adjoint/pallas_call | solution.py:430
  23.9 3.0 %collective-permute-start = (f32[4,224,128]{2,1,0:T(8,128)}, f32[4,224,128]{2,1,0:T(8,128)S(1)}, u32[]{:S(2)}, u32[]{:S(2)}) collective-permute-start(f32[4,224,128]{2,1,0:T(8,128)} %get-tuple-element.48), channel_id=1, source_target_pairs={{0,8},{8,0},{16,24},{24,16},{1,9},{9,1},{17,25},{25,17},{2,10},{10... | collective-permute-start | bytes 1376264 | tf_op jit(solution)/shard_map/ppermute | solution.py:384
  26.9 1.6 %collective-permute-start.1 = (f32[4,224,128]{2,1,0:T(8,128)}, f32[4,224,128]{2,1,0:T(8,128)S(1)}, u32[]{:S(2)}, u32[]{:S(2)}) collective-permute-start(f32[4,224,128]{2,1,0:T(8,128)} %get-tuple-element.50), channel_id=1, source_target_pairs={{0,16},{8,24},{16,0},{24,8},{1,17},{9,25},{17,1},{25,9},{2,18},{10... | collective-permute-start | bytes 1376264 | tf_op jit(solution)/shard_map/ppermute | solution.py:384
  28.4 0.9 copy.12.map_ref
  29.3 3.2 %tables.1 = (bf16[600,1024]{1,0:T(8,128)(2,1)}, bf16[464,224]{1,0:T(8,128)(2,1)}, bf16[464,224]{1,0:T(8,128)(2,1)}, bf16[224,464]{1,0:T(8,128)(2,1)}, bf16[224,464]{1,0:T(8,128)(2,1)}) custom-call(s32[600,1]{1,0:T(8,128)} %copy.12.map_ref, f32[224,224]{1,0:T(8,128)} %prior_ref.1, bf16[464,224]{1,0:T(8,128)(2,1)} %constant.12.clone.fh_ref, ...), custom_call_target="tpu_custom_call" | custom-call | tf_op jit(solution)/shard_map/tables/pallas_call | solution.py:454
  32.6 5.6 %rows.3 = (bf16[8,96,1024]{2,1,0:T(8,128)(2,1)}, bf16[8,96,1024]{2,1,0:T(8,128)(2,1)}) custom-call(bf16[600,1024]{1,0:T(8,128)(2,1)} %get-tuple-element.64.select, f32[28,96,600]{2,1,0:T(8,128)} %bitcast.3), custom_call_target="tpu_custom_call" | custom-call | flops 1887436800 | bytes 3686400 | tf_op jit(solution)/shard_map/rows/pallas_call | solution.py:470
  38.2 0.0 collective-permute-done
  38.2 0.1 add.36
  38.2 0.8 collective-permute-done.1
  39.2 1.6 %collective-permute-start.2 = (f32[2,224,128]{2,1,0:T(8,128)S(1)}, f32[2,224,128]{2,1,0:T(8,128)S(1)}, u32[]{:S(2)}, u32[]{:S(2)}) collective-permute-start(f32[2,224,128]{2,1,0:T(8,128)S(1)} %slice.37), channel_id=1, source_target_pairs={{0,16},{8,24},{16,0},{24,8},{1,17},{9,25},{17,1},{25,9},{2,18},{10... | collective-permute-start | bytes 688136 | tf_op jit(solution)/shard_map/ppermute | solution.py:389
  40.8 0.6 collective-permute-start.3
  41.4 5.5 %rows.4 = (bf16[8,96,1024]{2,1,0:T(8,128)(2,1)}, bf16[8,96,1024]{2,1,0:T(8,128)(2,1)}) custom-call(bf16[600,1024]{1,0:T(8,128)(2,1)} %get-tuple-element.64.select, f32[28,96,600]{2,1,0:T(8,128)} %bitcast.4), custom_call_target="tpu_custom_call" | custom-call | flops 1887436800 | bytes 3686400 | tf_op jit(solution)/shard_map/rows/pallas_call | solution.py:470
  46.8 0.0 collective-permute-done.2
  46.9 0.0 collective-permute-done.3
  46.9 1.6 %collective-permute-start.4 = (f32[2,224,128]{2,1,0:T(8,128)S(1)}, f32[2,224,128]{2,1,0:T(8,128)S(1)}, u32[]{:S(2)}, u32[]{:S(2)}) collective-permute-start(f32[2,224,128]{2,1,0:T(8,128)S(1)} %slice_add_fusion.rest_4_), channel_id=1, source_target_pairs={{0,8},{8,0},{16,24},{24,16},{1,9},{9,1},{17,25},{25,17},{2,10},{10... | collective-permute-start | bytes 688136 | tf_op jit(solution)/shard_map/ppermute | solution.py:393
  48.5 0.5 collective-permute-start.6
  49.0 0.5 collective-permute-start.7
  49.5 1.6 %collective-permute-start.9 = (f32[2,224,128]{2,1,0:T(8,128)S(1)}, f32[2,224,128]{2,1,0:T(8,128)S(1)}, u32[]{:S(2)}, u32[]{:S(2)}) collective-permute-start(f32[2,224,128]{2,1,0:T(8,128)S(1)} %slice_add_fusion.rest_4_), channel_id=1, source_target_pairs={{0,16},{8,24},{16,0},{24,8},{1,17},{9,25},{17,1},{25,9},{2,18},{10... | collective-permute-start | bytes 688136 | tf_op jit(solution)/shard_map/ppermute | solution.py:394
  51.0 4.5 %collective-permute-done.4.rest_5_ = f32[2,224,128]{2,1,0:T(8,128)S(1)} collective-permute-done((f32[2,224,128]{2,1,0:T(8,128)S(1)}, f32[2,224,128]{2,1,0:T(8,128)S(1)}, u32[]{:S(2)}, u32[]{:S(2)}) %collective-permute-start.4) | collective-permute-done | bytes 229408 | tf_op jit(solution)/shard_map/ppermute | solution.py:393
  55.5 0.5 collective-permute-start.5
  56.0 1.0 collective-permute-done.6.rest_1_
  57.0 0.5 collective-permute-start.8
  57.6 7.1 %rows.5 = (bf16[12,96,1024]{2,1,0:T(8,128)(2,1)}, bf16[12,96,1024]{2,1,0:T(8,128)(2,1)}) custom-call(bf16[600,1024]{1,0:T(8,128)(2,1)} %get-tuple-element.64.select, f32[28,96,600]{2,1,0:T(8,128)} %bitcast.5), custom_call_target="tpu_custom_call" | custom-call | flops 2831155200 | bytes 5529600 | tf_op jit(solution)/shard_map/rows/pallas_call | solution.py:470
  64.7 0.0 collective-permute-done.5.rest_7_
  64.7 0.0 collective-permute-done.7.rest_2_
  64.8 0.0 collective-permute-done.9.rest_6_
  64.8 0.0 collective-permute-done.8.rest_3_
  64.8 0.6 copy-done.11
  65.4 0.1 copy-done.9
  65.5 0.1 copy-done.10
  65.6 0.1 copy-done.12
  65.7 24.6 %forward.1 = (f32[1120,128]{1,0:T(8,128)}, f32[1120,128]{1,0:T(8,128)}, f32[1120,128]{1,0:T(8,128)}, f32[1120,128]{1,0:T(8,128)}) custom-call(bf16[464,224]{1,0:T(8,128)(2,1)} %get-tuple-element.71.th_ref, bf16[464,224]{1,0:T(8,128)(2,1)} %get-tuple-element.72.tl_ref, bf16[224,464]{1,0:T(8,128)(2,1)} %get-tuple-element.73.ih_ref, ...), custom_call_target="tpu_custom_call" | custom-call | flops 1658880000 | bytes 34560000 | tf_op jit(solution)/shard_map/forward/pallas_call | solution.py:505
  90.3 0.1 collective-permute-start.10
  90.4 0.5 collective-permute-start.17
  90.9 1.7 %collective-permute-done.10 = f32[1120,128]{1,0:T(8,128)S(1)} collective-permute-done((f32[1120,128]{1,0:T(8,128)}, f32[1120,128]{1,0:T(8,128)S(1)}, u32[]{:S(2)}, u32[]{:S(2)}) %collective-permute-start.10) | collective-permute-done | bytes 573472 | tf_op jit(solution)/shard_map/ppermute | solution.py:531
  92.6 1.1 add.40
  93.7 3.7 %collective-permute-start.13 = (f32[280,128]{1,0:T(8,128)S(1)}, f32[280,128]{1,0:T(8,128)S(1)}, u32[]{:S(2)}, u32[]{:S(2)}) collective-permute-start(f32[280,128]{1,0:T(8,128)S(1)} %get-tuple-element.85), channel_id=1, source_target_pairs={{0,6},{1,7},{2,0},{3,1},{4,2},{5,3},{6,4},{7,5},{8,14},{9,15},{10,... | collective-permute-start | bytes 430088 | tf_op jit(solution)/shard_map/ppermute | solution.py:526
  97.4 1.0 collective-permute-start.12
  98.4 0.0 collective-permute-done.17
  98.4 0.1 add.44
  98.5 2.9 %collective-permute-start.20 = (f32[280,128]{1,0:T(8,128)S(1)}, f32[280,128]{1,0:T(8,128)S(1)}, u32[]{:S(2)}, u32[]{:S(2)}) collective-permute-start(f32[280,128]{1,0:T(8,128)S(1)} %get-tuple-element.82), channel_id=1, source_target_pairs={{0,6},{1,7},{2,0},{3,1},{4,2},{5,3},{6,4},{7,5},{8,14},{9,15},{10,... | collective-permute-start | bytes 430088 | tf_op jit(solution)/shard_map/ppermute | solution.py:526
  101.4 0.6 collective-permute-start.18
  102.1 0.0 collective-permute-done.13
  102.1 1.4 collective-permute-start.19
  103.5 2.5 %collective-permute-done.11 = f32[280,128]{1,0:T(8,128)S(1)} collective-permute-done((f32[280,128]{1,0:T(8,128)S(1)}, f32[280,128]{1,0:T(8,128)S(1)}, u32[]{:S(2)}, u32[]{:S(2)}) %collective-permute-start.11) | collective-permute-done | bytes 143392 | tf_op jit(solution)/shard_map/ppermute | solution.py:526
  106.0 6.2 %collective-permute-done.12 = f32[280,128]{1,0:T(8,128)S(1)} collective-permute-done((f32[280,128]{1,0:T(8,128)S(1)}, f32[280,128]{1,0:T(8,128)S(1)}, u32[]{:S(2)}, u32[]{:S(2)}) %collective-permute-start.12) | collective-permute-done | bytes 143392 | tf_op jit(solution)/shard_map/ppermute | solution.py:526
  112.2 1.5 %collective-permute-start.14 = (f32[280,128]{1,0:T(8,128)S(1)}, f32[280,128]{1,0:T(8,128)S(1)}, u32[]{:S(2)}, u32[]{:S(2)}) collective-permute-start(f32[280,128]{1,0:T(8,128)S(1)} %slice_add_fusion.3.rest_6_), channel_id=1, source_target_pairs={{0,8},{8,0},{16,24},{24,16},{1,9},{9,1},{17,25},{25,17},{2,10},{10... | collective-permute-start | bytes 430088 | tf_op jit(solution)/shard_map/ppermute | solution.py:529
  113.7 0.6 collective-permute-start.15
  114.3 1.5 collective-permute-start.16
  115.7 6.6 %collective-permute-done.19 = f32[280,128]{1,0:T(8,128)S(1)} collective-permute-done((f32[280,128]{1,0:T(8,128)S(1)}, f32[280,128]{1,0:T(8,128)S(1)}, u32[]{:S(2)}, u32[]{:S(2)}) %collective-permute-start.19) | collective-permute-done | bytes 143392 | tf_op jit(solution)/shard_map/ppermute | solution.py:526
  122.3 0.1 slice_add_fusion.2.rest_10_
  122.4 1.5 %collective-permute-start.21 = (f32[280,128]{1,0:T(8,128)S(1)}, f32[280,128]{1,0:T(8,128)S(1)}, u32[]{:S(2)}, u32[]{:S(2)}) collective-permute-start(f32[280,128]{1,0:T(8,128)S(1)} %slice_add_fusion.2.rest_10_), channel_id=1, source_target_pairs={{0,8},{8,0},{16,24},{24,16},{1,9},{9,1},{17,25},{25,17},{2,10},{10... | collective-permute-start | bytes 430088 | tf_op jit(solution)/shard_map/ppermute | solution.py:529
  123.9 0.6 collective-permute-start.22
  124.5 1.5 collective-permute-start.23
  125.9 0.0 collective-permute-done.15.rest_8_
  125.9 0.0 collective-permute-done.16.rest_9_
  126.0 2.7 %collective-permute-done.21.rest_11_ = f32[280,128]{1,0:T(8,128)S(1)} collective-permute-done((f32[280,128]{1,0:T(8,128)S(1)}, f32[280,128]{1,0:T(8,128)S(1)}, u32[]{:S(2)}, u32[]{:S(2)}) %collective-permute-start.21) | collective-permute-done | bytes 143392 | tf_op jit(solution)/shard_map/ppermute | solution.py:529
  128.7 2.8 %collective-permute-done.22.rest_12_ = f32[280,128]{1,0:T(8,128)S(1)} collective-permute-done((f32[280,128]{1,0:T(8,128)S(1)}, f32[280,128]{1,0:T(8,128)S(1)}, u32[]{:S(2)}, u32[]{:S(2)}) %collective-permute-start.22) | collective-permute-done | bytes 143392 | tf_op jit(solution)/shard_map/ppermute | solution.py:529
  131.5 0.6 copy-done.17
  132.1 0.7 copy-done.18
  132.8 7.4 %update.1 = f32[16,96]{1,0:T(8,128)} custom-call(bf16[8,96,1024]{2,1,0:T(8,128)(2,1)} %get-tuple-element.56.rest_0_, bf16[8,96,1024]{2,1,0:T(8,128)(2,1)} %get-tuple-element.62.rest_1_, bf16[12,96,1024]{2,1,0:T(8,128)(2,1)} %get-tuple-element.67.rest_2_, bf16[8,96,1024]{2,1,0:T(8,128)(2,1)} %get-tuple-element.68.rest_3_, ...), custom_call_target="tpu_custom_call" | custom-call | flops 264241152 | bytes 11010048 | tf_op jit(solution)/shard_map/update/pallas_call | solution.py:539
  140.2 9.3 %all_to_all.5 = f32[8,2,96]{2,1,0:T(2,128)S(1)} all-to-all(f32[8,2,96]{2,1,0:T(2,128)} %bitcast.7), channel_id=1, replica_groups=mesh['sens'=4,'par'=8] {'par'}, dimensions={0} | all-to-all | bytes 12288 | tf_op jit(solution)/shard_map/all_to_all | solution.py:554
  149.4 0.6 reduce_sum.9
  (45 shorter events, 0.3 us)
Async XLA Ops:
  23.9 14.3 %collective-permute-start = (f32[4,224,128]{2,1,0:T(8,128)}, f32[4,224,128]{2,1,0:T(8,128)S(1)}, u32[]{:S(2)}, u32[]{:S(2)}) collective-permute-start(f32[4,224,128]{2,1,0:T(8,128)} %get-tuple-element.48), channel_id=1, source_target_pairs={{0,8},{8,0},{16,24},{24,16},{1,9},{9,1},{17,25},{25,17},{2,10},{10... | collective-permute-start | bytes 1376264 | tf_op jit(solution)/shard_map/ppermute | solution.py:384
  26.9 12.2 %collective-permute-start.1 = (f32[4,224,128]{2,1,0:T(8,128)}, f32[4,224,128]{2,1,0:T(8,128)S(1)}, u32[]{:S(2)}, u32[]{:S(2)}) collective-permute-start(f32[4,224,128]{2,1,0:T(8,128)} %get-tuple-element.50), channel_id=1, source_target_pairs={{0,16},{8,24},{16,0},{24,8},{1,17},{9,25},{17,1},{25,9},{2,18},{10... | collective-permute-start | bytes 1376264 | tf_op jit(solution)/shard_map/ppermute | solution.py:384
  32.6 5.6 %copy-start.6 = (f32[4,224,128]{2,1,0:T(8,128)S(1)}, f32[4,224,128]{2,1,0:T(8,128)}, u32[]{:S(2)}) copy-start(f32[4,224,128]{2,1,0:T(8,128)} %get-tuple-element.47) | copy-start | bytes 1376260
  32.6 6.5 %copy-start.5 = (f32[4,224,128]{2,1,0:T(8,128)S(1)}, f32[4,224,128]{2,1,0:T(8,128)}, u32[]{:S(2)}) copy-start(f32[4,224,128]{2,1,0:T(8,128)} %get-tuple-element.49) | copy-start | bytes 1376260
  39.2 7.7 %collective-permute-start.2 = (f32[2,224,128]{2,1,0:T(8,128)S(1)}, f32[2,224,128]{2,1,0:T(8,128)S(1)}, u32[]{:S(2)}, u32[]{:S(2)}) collective-permute-start(f32[2,224,128]{2,1,0:T(8,128)S(1)} %slice.37), channel_id=1, source_target_pairs={{0,16},{8,24},{16,0},{24,8},{1,17},{9,25},{17,1},{25,9},{2,18},{10... | collective-permute-start | bytes 688136 | tf_op jit(solution)/shard_map/ppermute | solution.py:389
  40.8 6.1 %collective-permute-start.3 = (f32[2,224,128]{2,1,0:T(8,128)S(1)}, f32[2,224,128]{2,1,0:T(8,128)S(1)}, u32[]{:S(2)}, u32[]{:S(2)}) collective-permute-start(f32[2,224,128]{2,1,0:T(8,128)S(1)} %slice.39), channel_id=1, source_target_pairs={{0,8},{8,0},{16,24},{24,16},{1,9},{9,1},{17,25},{25,17},{2,10},{10... | collective-permute-start | bytes 688136 | tf_op jit(solution)/shard_map/ppermute | solution.py:389
  46.9 17.8 %copy-start = (f32[2,224,128]{2,1,0:T(8,128)}, f32[2,224,128]{2,1,0:T(8,128)S(1)}, u32[]{:S(2)}) copy-start(f32[2,224,128]{2,1,0:T(8,128)S(1)} %slice_add_fusion.1.rest_0_) | copy-start | bytes 688132
  46.9 17.8 %copy-start.1 = (f32[2,224,128]{2,1,0:T(8,128)}, f32[2,224,128]{2,1,0:T(8,128)S(1)}, u32[]{:S(2)}) copy-start(f32[2,224,128]{2,1,0:T(8,128)S(1)} %slice_add_fusion.rest_4_) | copy-start | bytes 688132
  46.9 8.6 %collective-permute-start.4 = (f32[2,224,128]{2,1,0:T(8,128)S(1)}, f32[2,224,128]{2,1,0:T(8,128)S(1)}, u32[]{:S(2)}, u32[]{:S(2)}) collective-permute-start(f32[2,224,128]{2,1,0:T(8,128)S(1)} %slice_add_fusion.rest_4_), channel_id=1, source_target_pairs={{0,8},{8,0},{16,24},{24,16},{1,9},{9,1},{17,25},{25,17},{2,10},{10... | collective-permute-start | bytes 688136 | tf_op jit(solution)/shard_map/ppermute | solution.py:393
  48.5 8.5 %collective-permute-start.6 = (f32[2,224,128]{2,1,0:T(8,128)S(1)}, f32[2,224,128]{2,1,0:T(8,128)S(1)}, u32[]{:S(2)}, u32[]{:S(2)}) collective-permute-start(f32[2,224,128]{2,1,0:T(8,128)S(1)} %slice_add_fusion.1.rest_0_), channel_id=1, source_target_pairs={{0,16},{8,24},{16,0},{24,8},{1,17},{9,25},{17,1},{25,9},{2,18},{10... | collective-permute-start | bytes 688136 | tf_op jit(solution)/shard_map/ppermute | solution.py:393
  49.0 15.7 %collective-permute-start.7 = (f32[2,224,128]{2,1,0:T(8,128)S(1)}, f32[2,224,128]{2,1,0:T(8,128)S(1)}, u32[]{:S(2)}, u32[]{:S(2)}) collective-permute-start(f32[2,224,128]{2,1,0:T(8,128)S(1)} %slice_add_fusion.1.rest_0_), channel_id=1, source_target_pairs={{0,8},{8,0},{16,24},{24,16},{1,9},{9,1},{17,25},{25,17},{2,10},{10... | collective-permute-start | bytes 688136 | tf_op jit(solution)/shard_map/ppermute | solution.py:394
  49.5 15.3 %collective-permute-start.9 = (f32[2,224,128]{2,1,0:T(8,128)S(1)}, f32[2,224,128]{2,1,0:T(8,128)S(1)}, u32[]{:S(2)}, u32[]{:S(2)}) collective-permute-start(f32[2,224,128]{2,1,0:T(8,128)S(1)} %slice_add_fusion.rest_4_), channel_id=1, source_target_pairs={{0,16},{8,24},{16,0},{24,8},{1,17},{9,25},{17,1},{25,9},{2,18},{10... | collective-permute-start | bytes 688136 | tf_op jit(solution)/shard_map/ppermute | solution.py:394
  55.5 9.2 %copy-start.7 = (f32[2,224,128]{2,1,0:T(8,128)}, f32[2,224,128]{2,1,0:T(8,128)S(1)}, u32[]{:S(2)}) copy-start(f32[2,224,128]{2,1,0:T(8,128)S(1)} %collective-permute-done.4.rest_5_) | copy-start | bytes 688132
  55.5 9.2 %collective-permute-start.5 = (f32[2,224,128]{2,1,0:T(8,128)S(1)}, f32[2,224,128]{2,1,0:T(8,128)S(1)}, u32[]{:S(2)}, u32[]{:S(2)}) collective-permute-start(f32[2,224,128]{2,1,0:T(8,128)S(1)} %collective-permute-done.4.rest_5_), channel_id=1, source_target_pairs={{0,16},{8,24},{16,0},{24,8},{1,17},{9,25},{17,1},{25,9},{2,18},{10... | collective-permute-start | bytes 688136 | tf_op jit(solution)/shard_map/ppermute | solution.py:395
  57.0 7.7 %copy-start.8 = (f32[2,224,128]{2,1,0:T(8,128)}, f32[2,224,128]{2,1,0:T(8,128)S(1)}, u32[]{:S(2)}) copy-start(f32[2,224,128]{2,1,0:T(8,128)S(1)} %collective-permute-done.6.rest_1_) | copy-start | bytes 688132
  57.0 7.8 %collective-permute-start.8 = (f32[2,224,128]{2,1,0:T(8,128)S(1)}, f32[2,224,128]{2,1,0:T(8,128)S(1)}, u32[]{:S(2)}, u32[]{:S(2)}) collective-permute-start(f32[2,224,128]{2,1,0:T(8,128)S(1)} %collective-permute-done.6.rest_1_), channel_id=1, source_target_pairs={{0,8},{8,0},{16,24},{24,16},{1,9},{9,1},{17,25},{25,17},{2,10},{10... | collective-permute-start | bytes 688136 | tf_op jit(solution)/shard_map/ppermute | solution.py:395
  64.7 0.7 copy-start.11
  64.7 0.8 copy-start.9
  64.8 0.8 copy-start.10
  64.8 0.9 copy-start.12
  90.3 8.1 %copy-start.2 = (f32[1120,128]{1,0:T(8,128)S(1)}, f32[1120,128]{1,0:T(8,128)}, u32[]{:S(2)}) copy-start(f32[1120,128]{1,0:T(8,128)} %get-tuple-element.79) | copy-start | bytes 1720324
  90.3 2.3 %collective-permute-start.10 = (f32[1120,128]{1,0:T(8,128)}, f32[1120,128]{1,0:T(8,128)S(1)}, u32[]{:S(2)}, u32[]{:S(2)}) collective-permute-start(f32[1120,128]{1,0:T(8,128)} %get-tuple-element.78), channel_id=1, source_target_pairs={{0,1},{1,0},{2,3},{3,2},{4,5},{5,4},{6,7},{7,6},{8,9},{9,8},{10,11... | collective-permute-start | bytes 1720328 | tf_op jit(solution)/shard_map/ppermute | solution.py:531
  90.4 8.0 %collective-permute-start.17 = (f32[1120,128]{1,0:T(8,128)}, f32[1120,128]{1,0:T(8,128)S(1)}, u32[]{:S(2)}, u32[]{:S(2)}) collective-permute-start(f32[1120,128]{1,0:T(8,128)} %get-tuple-element.80), channel_id=1, source_target_pairs={{0,1},{1,0},{2,3},{3,2},{4,5},{5,4},{6,7},{7,6},{8,9},{9,8},{10,11... | collective-permute-start | bytes 1720328 | tf_op jit(solution)/shard_map/ppermute | solution.py:532
  93.7 8.3 %collective-permute-start.13 = (f32[280,128]{1,0:T(8,128)S(1)}, f32[280,128]{1,0:T(8,128)S(1)}, u32[]{:S(2)}, u32[]{:S(2)}) collective-permute-start(f32[280,128]{1,0:T(8,128)S(1)} %get-tuple-element.85), channel_id=1, source_target_pairs={{0,6},{1,7},{2,0},{3,1},{4,2},{5,3},{6,4},{7,5},{8,14},{9,15},{10,... | collective-permute-start | bytes 430088 | tf_op jit(solution)/shard_map/ppermute | solution.py:526
  97.4 8.5 %collective-permute-start.11 = (f32[280,128]{1,0:T(8,128)S(1)}, f32[280,128]{1,0:T(8,128)S(1)}, u32[]{:S(2)}, u32[]{:S(2)}) collective-permute-start(f32[280,128]{1,0:T(8,128)S(1)} %get-tuple-element.86), channel_id=1, source_target_pairs={{0,2},{1,3},{2,4},{3,5},{4,6},{5,7},{6,0},{7,1},{8,10},{9,11},{10,... | collective-permute-start | bytes 430088 | tf_op jit(solution)/shard_map/ppermute | solution.py:526
  97.4 14.7 %collective-permute-start.12 = (f32[280,128]{1,0:T(8,128)S(1)}, f32[280,128]{1,0:T(8,128)S(1)}, u32[]{:S(2)}, u32[]{:S(2)}) collective-permute-start(f32[280,128]{1,0:T(8,128)S(1)} %get-tuple-element.84), channel_id=1, source_target_pairs={{0,4},{1,5},{2,6},{3,7},{4,0},{5,1},{6,2},{7,3},{8,12},{9,13},{10,... | collective-permute-start | bytes 430088 | tf_op jit(solution)/shard_map/ppermute | solution.py:526
  98.5 15.7 %collective-permute-start.20 = (f32[280,128]{1,0:T(8,128)S(1)}, f32[280,128]{1,0:T(8,128)S(1)}, u32[]{:S(2)}, u32[]{:S(2)}) collective-permute-start(f32[280,128]{1,0:T(8,128)S(1)} %get-tuple-element.82), channel_id=1, source_target_pairs={{0,6},{1,7},{2,0},{3,1},{4,2},{5,3},{6,4},{7,5},{8,14},{9,15},{10,... | collective-permute-start | bytes 430088 | tf_op jit(solution)/shard_map/ppermute | solution.py:526
  101.4 14.3 %collective-permute-start.18 = (f32[280,128]{1,0:T(8,128)S(1)}, f32[280,128]{1,0:T(8,128)S(1)}, u32[]{:S(2)}, u32[]{:S(2)}) collective-permute-start(f32[280,128]{1,0:T(8,128)S(1)} %get-tuple-element.83), channel_id=1, source_target_pairs={{0,2},{1,3},{2,4},{3,5},{4,6},{5,7},{6,0},{7,1},{8,10},{9,11},{10,... | collective-permute-start | bytes 430088 | tf_op jit(solution)/shard_map/ppermute | solution.py:526
  102.1 20.3 %collective-permute-start.19 = (f32[280,128]{1,0:T(8,128)S(1)}, f32[280,128]{1,0:T(8,128)S(1)}, u32[]{:S(2)}, u32[]{:S(2)}) collective-permute-start(f32[280,128]{1,0:T(8,128)S(1)} %get-tuple-element.81), channel_id=1, source_target_pairs={{0,4},{1,5},{2,6},{3,7},{4,0},{5,1},{6,2},{7,3},{8,12},{9,13},{10,... | collective-permute-start | bytes 430088 | tf_op jit(solution)/shard_map/ppermute | solution.py:526
  112.2 19.3 %copy-start.3 = (f32[280,128]{1,0:T(8,128)}, f32[280,128]{1,0:T(8,128)S(1)}, u32[]{:S(2)}) copy-start(f32[280,128]{1,0:T(8,128)S(1)} %slice_add_fusion.3.rest_6_) | copy-start | bytes 430084
  112.2 12.3 %collective-permute-start.14 = (f32[280,128]{1,0:T(8,128)S(1)}, f32[280,128]{1,0:T(8,128)S(1)}, u32[]{:S(2)}, u32[]{:S(2)}) collective-permute-start(f32[280,128]{1,0:T(8,128)S(1)} %slice_add_fusion.3.rest_6_), channel_id=1, source_target_pairs={{0,8},{8,0},{16,24},{24,16},{1,9},{9,1},{17,25},{25,17},{2,10},{10... | collective-permute-start | bytes 430088 | tf_op jit(solution)/shard_map/ppermute | solution.py:529
  113.7 12.3 %collective-permute-start.15 = (f32[280,128]{1,0:T(8,128)S(1)}, f32[280,128]{1,0:T(8,128)S(1)}, u32[]{:S(2)}, u32[]{:S(2)}) collective-permute-start(f32[280,128]{1,0:T(8,128)S(1)} %slice_add_fusion.3.rest_6_), channel_id=1, source_target_pairs={{0,16},{8,24},{16,0},{24,8},{1,17},{9,25},{17,1},{25,9},{2,18},{10... | collective-permute-start | bytes 430088 | tf_op jit(solution)/shard_map/ppermute | solution.py:529
  114.3 11.7 %collective-permute-start.16 = (f32[280,128]{1,0:T(8,128)S(1)}, f32[280,128]{1,0:T(8,128)S(1)}, u32[]{:S(2)}, u32[]{:S(2)}) collective-permute-start(f32[280,128]{1,0:T(8,128)S(1)} %slice_add_fusion.3.rest_6_), channel_id=1, source_target_pairs={{0,24},{8,16},{16,8},{24,0},{1,25},{9,17},{17,9},{25,1},{2,26},{10... | collective-permute-start | bytes 430088 | tf_op jit(solution)/shard_map/ppermute | solution.py:529
  122.4 9.1 %copy-start.4 = (f32[280,128]{1,0:T(8,128)}, f32[280,128]{1,0:T(8,128)S(1)}, u32[]{:S(2)}) copy-start(f32[280,128]{1,0:T(8,128)S(1)} %slice_add_fusion.2.rest_10_) | copy-start | bytes 430084
  122.4 6.3 %collective-permute-start.21 = (f32[280,128]{1,0:T(8,128)S(1)}, f32[280,128]{1,0:T(8,128)S(1)}, u32[]{:S(2)}, u32[]{:S(2)}) collective-permute-start(f32[280,128]{1,0:T(8,128)S(1)} %slice_add_fusion.2.rest_10_), channel_id=1, source_target_pairs={{0,8},{8,0},{16,24},{24,16},{1,9},{9,1},{17,25},{25,17},{2,10},{10... | collective-permute-start | bytes 430088 | tf_op jit(solution)/shard_map/ppermute | solution.py:529
  123.9 7.6 %collective-permute-start.22 = (f32[280,128]{1,0:T(8,128)S(1)}, f32[280,128]{1,0:T(8,128)S(1)}, u32[]{:S(2)}, u32[]{:S(2)}) collective-permute-start(f32[280,128]{1,0:T(8,128)S(1)} %slice_add_fusion.2.rest_10_), channel_id=1, source_target_pairs={{0,16},{8,24},{16,0},{24,8},{1,17},{9,25},{17,1},{25,9},{2,18},{10... | collective-permute-start | bytes 430088 | tf_op jit(solution)/shard_map/ppermute | solution.py:529
  124.5 7.0 %copy-start.13 = (f32[280,128]{1,0:T(8,128)}, f32[280,128]{1,0:T(8,128)S(1)}, u32[]{:S(2)}) copy-start(f32[280,128]{1,0:T(8,128)S(1)} %collective-permute-done.14.rest_7_) | copy-start | bytes 430084
  124.5 7.0 %collective-permute-start.23 = (f32[280,128]{1,0:T(8,128)S(1)}, f32[280,128]{1,0:T(8,128)S(1)}, u32[]{:S(2)}, u32[]{:S(2)}) collective-permute-start(f32[280,128]{1,0:T(8,128)S(1)} %slice_add_fusion.2.rest_10_), channel_id=1, source_target_pairs={{0,24},{8,16},{16,8},{24,0},{1,25},{9,17},{17,9},{25,1},{2,26},{10... | collective-permute-start | bytes 430088 | tf_op jit(solution)/shard_map/ppermute | solution.py:529
  125.9 5.6 %copy-start.14 = (f32[280,128]{1,0:T(8,128)}, f32[280,128]{1,0:T(8,128)S(1)}, u32[]{:S(2)}) copy-start(f32[280,128]{1,0:T(8,128)S(1)} %collective-permute-done.15.rest_8_) | copy-start | bytes 430084
  126.0 5.6 %copy-start.15 = (f32[280,128]{1,0:T(8,128)}, f32[280,128]{1,0:T(8,128)S(1)}, u32[]{:S(2)}) copy-start(f32[280,128]{1,0:T(8,128)S(1)} %collective-permute-done.16.rest_9_) | copy-start | bytes 430084
  128.6 2.9 %copy-start.16 = (f32[280,128]{1,0:T(8,128)}, f32[280,128]{1,0:T(8,128)S(1)}, u32[]{:S(2)}) copy-start(f32[280,128]{1,0:T(8,128)S(1)} %collective-permute-done.21.rest_11_) | copy-start | bytes 430084
  131.5 0.6 copy-start.17
  132.1 0.7 copy-start.18

commit v6 on v5

--- a/solution.py
+++ b/solution.py
@@ -415,7 +415,7 @@
 
     by_sensor = jnp.transpose(records, (1, 0, 2))
     by_time = jnp.transpose(inverse_rows, (1, 0, 2))
-    block = block_of(bins, 15)
+    block = block_of(bins, 25)
     outside = pl.BlockSpec(memory_space=pltpu.HBM)
     spec_scratch = [
         pltpu.VMEM(spec_real.shape, F32),

time: 150 us -> 148 us (0.987)
  Pallas kernels: 76.6 us -> 74.5 us
where the time goes in v6:
time: 148 us
  Pallas kernels  74.5 us (50%)
  starting transfers between devices  29.1 us (20%)
  waiting for transfers between devices  28.8 us (19%)
  blocking collectives  9.28 us (6%)
  local copies, waits for them, and re-layouts  3.87 us (3%)
  other arithmetic  2.01 us (1%)
    pallas_call x1, Pallas kernels, shards(): pl.pallas_call(functools.partial(forward_kernel, packing, quarters), in_s...  23.3 us
    pallas_call x1, Pallas kernels, shards(): pl.pallas_call(functools.partial(adjoint_kernel, quarters), in_specs=[who...  22.4 us
    pallas_call x3, Pallas kernels, move_rows(): pl.pallas_call(rows_kernel, grid=(stop - start,), in_specs=[whole(chosen)...  18.2 us
    ppermute x6, waiting for transfers between devices, over_pairs(): lax.ppermute(there, 'par', [(k, (k + 2 * d) % par) for k in range(par)])  15.2 us
    ppermute x6, starting transfers between devices, over_pairs(): lax.ppermute(there, 'par', [(k, (k + 2 * d) % par) for k in range(par)])  9.59 us
    all_to_all x1, blocking collectives, shards(): lax.all_to_all(partial.reshape(par, cols // par, rows_dev), 'par', 0, 0)  9.28 us
    pallas_call x1, Pallas kernels, shards(): pl.pallas_call(functools.partial(update_kernel, packing, len(ready)), in_...  7.38 us
    ppermute x6, starting transfers between devices, over_sens(): lax.ppermute(mine, 'sens', swap(sens, m))  7.11 us
  transfers between devices with their start and end apart: 24, of which 9 were waited for; matrix products, arithmetic and copies ran while one was open for 2% of the time, Pallas kernels for 14%

profile of v6, /device:TPU:0, one launch (start us, length us, event | category | flops | bytes accessed | tf_op | source)
XLA Modules:
  0.0 147.9 jit_solution(1170151103217861636)
XLA Ops:
  0.0 0.7 reshape.6
  0.7 22.4 %adjoint.1 = (f32[4,224,128]{2,1,0:T(8,128)}, f32[4,224,128]{2,1,0:T(8,128)}, f32[4,224,128]{2,1,0:T(8,128)}, f32[4,224,128]{2,1,0:T(8,128)}) custom-call(f32[150,16,224]{2,1,0:T(8,128)} %bitcast.6, bf16[464,224]{1,0:T(8,128)(2,1)} %constant.12.clone.fh_ref, bf16[464,224]{1,0:T(8,128)(2,1)} %constant.13.clone.fl_ref, ...), custom_call_target="tpu_custom_call" | custom-call | flops 1658880000 | bytes 34560000 | tf_op jit(solution)/shard_map/adjoint/pallas_call | solution.py:430
  23.1 3.0 %collective-permute-start = (f32[4,224,128]{2,1,0:T(8,128)}, f32[4,224,128]{2,1,0:T(8,128)S(1)}, u32[]{:S(2)}, u32[]{:S(2)}) collective-permute-start(f32[4,224,128]{2,1,0:T(8,128)} %get-tuple-element.48), channel_id=1, source_target_pairs={{0,8},{8,0},{16,24},{24,16},{1,9},{9,1},{17,25},{25,17},{2,10},{10... | collective-permute-start | bytes 1376264 | tf_op jit(solution)/shard_map/ppermute | solution.py:384
  26.1 1.6 %collective-permute-start.1 = (f32[4,224,128]{2,1,0:T(8,128)}, f32[4,224,128]{2,1,0:T(8,128)S(1)}, u32[]{:S(2)}, u32[]{:S(2)}) collective-permute-start(f32[4,224,128]{2,1,0:T(8,128)} %get-tuple-element.50), channel_id=1, source_target_pairs={{0,16},{8,24},{16,0},{24,8},{1,17},{9,25},{17,1},{25,9},{2,18},{10... | collective-permute-start | bytes 1376264 | tf_op jit(solution)/shard_map/ppermute | solution.py:384
  27.6 0.9 copy.12.map_ref
  28.5 3.2 %tables.1 = (bf16[600,1024]{1,0:T(8,128)(2,1)}, bf16[464,224]{1,0:T(8,128)(2,1)}, bf16[464,224]{1,0:T(8,128)(2,1)}, bf16[224,464]{1,0:T(8,128)(2,1)}, bf16[224,464]{1,0:T(8,128)(2,1)}) custom-call(s32[600,1]{1,0:T(8,128)} %copy.12.map_ref, f32[224,224]{1,0:T(8,128)} %prior_ref.1, bf16[464,224]{1,0:T(8,128)(2,1)} %constant.12.clone.fh_ref, ...), custom_call_target="tpu_custom_call" | custom-call | tf_op jit(solution)/shard_map/tables/pallas_call | solution.py:454
  31.8 5.6 %rows.3 = (bf16[8,96,1024]{2,1,0:T(8,128)(2,1)}, bf16[8,96,1024]{2,1,0:T(8,128)(2,1)}) custom-call(bf16[600,1024]{1,0:T(8,128)(2,1)} %get-tuple-element.64.select, f32[28,96,600]{2,1,0:T(8,128)} %bitcast.3), custom_call_target="tpu_custom_call" | custom-call | flops 1887436800 | bytes 3686400 | tf_op jit(solution)/shard_map/rows/pallas_call | solution.py:470
  37.4 0.0 collective-permute-done
  37.4 0.1 add.36
  37.4 0.8 collective-permute-done.1
  38.4 1.6 %collective-permute-start.2 = (f32[2,224,128]{2,1,0:T(8,128)S(1)}, f32[2,224,128]{2,1,0:T(8,128)S(1)}, u32[]{:S(2)}, u32[]{:S(2)}) collective-permute-start(f32[2,224,128]{2,1,0:T(8,128)S(1)} %slice.37), channel_id=1, source_target_pairs={{0,16},{8,24},{16,0},{24,8},{1,17},{9,25},{17,1},{25,9},{2,18},{10... | collective-permute-start | bytes 688136 | tf_op jit(solution)/shard_map/ppermute | solution.py:389
  40.0 0.6 collective-permute-start.3
  40.6 5.4 %rows.4 = (bf16[8,96,1024]{2,1,0:T(8,128)(2,1)}, bf16[8,96,1024]{2,1,0:T(8,128)(2,1)}) custom-call(bf16[600,1024]{1,0:T(8,128)(2,1)} %get-tuple-element.64.select, f32[28,96,600]{2,1,0:T(8,128)} %bitcast.4), custom_call_target="tpu_custom_call" | custom-call | flops 1887436800 | bytes 3686400 | tf_op jit(solution)/shard_map/rows/pallas_call | solution.py:470
  46.0 0.0 collective-permute-done.2
  46.1 0.0 collective-permute-done.3
  46.1 1.6 %collective-permute-start.4 = (f32[2,224,128]{2,1,0:T(8,128)S(1)}, f32[2,224,128]{2,1,0:T(8,128)S(1)}, u32[]{:S(2)}, u32[]{:S(2)}) collective-permute-start(f32[2,224,128]{2,1,0:T(8,128)S(1)} %slice_add_fusion.rest_4_), channel_id=1, source_target_pairs={{0,8},{8,0},{16,24},{24,16},{1,9},{9,1},{17,25},{25,17},{2,10},{10... | collective-permute-start | bytes 688136 | tf_op jit(solution)/shard_map/ppermute | solution.py:393
  47.7 0.5 collective-permute-start.6
  48.2 0.5 collective-permute-start.7
  48.7 1.5 %collective-permute-start.9 = (f32[2,224,128]{2,1,0:T(8,128)S(1)}, f32[2,224,128]{2,1,0:T(8,128)S(1)}, u32[]{:S(2)}, u32[]{:S(2)}) collective-permute-start(f32[2,224,128]{2,1,0:T(8,128)S(1)} %slice_add_fusion.rest_4_), channel_id=1, source_target_pairs={{0,16},{8,24},{16,0},{24,8},{1,17},{9,25},{17,1},{25,9},{2,18},{10... | collective-permute-start | bytes 688136 | tf_op jit(solution)/shard_map/ppermute | solution.py:394
  50.2 4.5 %collective-permute-done.4.rest_5_ = f32[2,224,128]{2,1,0:T(8,128)S(1)} collective-permute-done((f32[2,224,128]{2,1,0:T(8,128)S(1)}, f32[2,224,128]{2,1,0:T(8,128)S(1)}, u32[]{:S(2)}, u32[]{:S(2)}) %collective-permute-start.4) | collective-permute-done | bytes 229408 | tf_op jit(solution)/shard_map/ppermute | solution.py:393
  54.7 0.5 collective-permute-start.5
  55.2 1.0 collective-permute-done.6.rest_1_
  56.2 0.5 collective-permute-start.8
  56.8 7.1 %rows.5 = (bf16[12,96,1024]{2,1,0:T(8,128)(2,1)}, bf16[12,96,1024]{2,1,0:T(8,128)(2,1)}) custom-call(bf16[600,1024]{1,0:T(8,128)(2,1)} %get-tuple-element.64.select, f32[28,96,600]{2,1,0:T(8,128)} %bitcast.5), custom_call_target="tpu_custom_call" | custom-call | flops 2831155200 | bytes 5529600 | tf_op jit(solution)/shard_map/rows/pallas_call | solution.py:470
  63.9 0.0 collective-permute-done.5.rest_7_
  63.9 0.0 collective-permute-done.7.rest_2_
  64.0 0.6 copy-done.11
  64.6 0.1 copy-done.9
  64.7 0.1 copy-done.10
  64.8 0.1 copy-done.12
  64.9 23.3 %forward.1 = (f32[1120,128]{1,0:T(8,128)}, f32[1120,128]{1,0:T(8,128)}, f32[1120,128]{1,0:T(8,128)}, f32[1120,128]{1,0:T(8,128)}) custom-call(bf16[464,224]{1,0:T(8,128)(2,1)} %get-tuple-element.71.th_ref, bf16[464,224]{1,0:T(8,128)(2,1)} %get-tuple-element.72.tl_ref, bf16[224,464]{1,0:T(8,128)(2,1)} %get-tuple-element.73.ih_ref, ...), custom_call_target="tpu_custom_call" | custom-call | flops 1658880000 | bytes 34560000 | tf_op jit(solution)/shard_map/forward/pallas_call | solution.py:505
  88.2 0.1 collective-permute-start.10
  88.3 0.5 collective-permute-start.17
  88.8 1.7 %collective-permute-done.10 = f32[1120,128]{1,0:T(8,128)S(1)} collective-permute-done((f32[1120,128]{1,0:T(8,128)}, f32[1120,128]{1,0:T(8,128)S(1)}, u32[]{:S(2)}, u32[]{:S(2)}) %collective-permute-start.10) | collective-permute-done | bytes 573472 | tf_op jit(solution)/shard_map/ppermute | solution.py:531
  90.4 1.1 add.40
  91.6 3.7 %collective-permute-start.13 = (f32[280,128]{1,0:T(8,128)S(1)}, f32[280,128]{1,0:T(8,128)S(1)}, u32[]{:S(2)}, u32[]{:S(2)}) collective-permute-start(f32[280,128]{1,0:T(8,128)S(1)} %get-tuple-element.85), channel_id=1, source_target_pairs={{0,6},{1,7},{2,0},{3,1},{4,2},{5,3},{6,4},{7,5},{8,14},{9,15},{10,... | collective-permute-start | bytes 430088 | tf_op jit(solution)/shard_map/ppermute | solution.py:526
  95.3 1.0 collective-permute-start.12
  96.3 0.0 collective-permute-done.17
  96.3 0.1 add.44
  96.4 2.9 %collective-permute-start.20 = (f32[280,128]{1,0:T(8,128)S(1)}, f32[280,128]{1,0:T(8,128)S(1)}, u32[]{:S(2)}, u32[]{:S(2)}) collective-permute-start(f32[280,128]{1,0:T(8,128)S(1)} %get-tuple-element.82), channel_id=1, source_target_pairs={{0,6},{1,7},{2,0},{3,1},{4,2},{5,3},{6,4},{7,5},{8,14},{9,15},{10,... | collective-permute-start | bytes 430088 | tf_op jit(solution)/shard_map/ppermute | solution.py:526
  99.3 0.6 collective-permute-start.18
  99.9 0.0 collective-permute-done.13
  99.9 1.4 collective-permute-start.19
  101.3 2.5 %collective-permute-done.11 = f32[280,128]{1,0:T(8,128)S(1)} collective-permute-done((f32[280,128]{1,0:T(8,128)S(1)}, f32[280,128]{1,0:T(8,128)S(1)}, u32[]{:S(2)}, u32[]{:S(2)}) %collective-permute-start.11) | collective-permute-done | bytes 143392 | tf_op jit(solution)/shard_map/ppermute | solution.py:526
  103.8 6.2 %collective-permute-done.12 = f32[280,128]{1,0:T(8,128)S(1)} collective-permute-done((f32[280,128]{1,0:T(8,128)S(1)}, f32[280,128]{1,0:T(8,128)S(1)}, u32[]{:S(2)}, u32[]{:S(2)}) %collective-permute-start.12) | collective-permute-done | bytes 143392 | tf_op jit(solution)/shard_map/ppermute | solution.py:526
  110.0 1.5 %collective-permute-start.14 = (f32[280,128]{1,0:T(8,128)S(1)}, f32[280,128]{1,0:T(8,128)S(1)}, u32[]{:S(2)}, u32[]{:S(2)}) collective-permute-start(f32[280,128]{1,0:T(8,128)S(1)} %slice_add_fusion.3.rest_6_), channel_id=1, source_target_pairs={{0,8},{8,0},{16,24},{24,16},{1,9},{9,1},{17,25},{25,17},{2,10},{10... | collective-permute-start | bytes 430088 | tf_op jit(solution)/shard_map/ppermute | solution.py:529
  111.5 0.6 collective-permute-start.15
  112.1 1.5 collective-permute-start.16
  113.6 0.0 collective-permute-done.18
  113.6 6.6 %collective-permute-done.19 = f32[280,128]{1,0:T(8,128)S(1)} collective-permute-done((f32[280,128]{1,0:T(8,128)S(1)}, f32[280,128]{1,0:T(8,128)S(1)}, u32[]{:S(2)}, u32[]{:S(2)}) %collective-permute-start.19) | collective-permute-done | bytes 143392 | tf_op jit(solution)/shard_map/ppermute | solution.py:526
  120.2 0.1 slice_add_fusion.2.rest_10_
  120.2 1.5 %collective-permute-start.21 = (f32[280,128]{1,0:T(8,128)S(1)}, f32[280,128]{1,0:T(8,128)S(1)}, u32[]{:S(2)}, u32[]{:S(2)}) collective-permute-start(f32[280,128]{1,0:T(8,128)S(1)} %slice_add_fusion.2.rest_10_), channel_id=1, source_target_pairs={{0,8},{8,0},{16,24},{24,16},{1,9},{9,1},{17,25},{25,17},{2,10},{10... | collective-permute-start | bytes 430088 | tf_op jit(solution)/shard_map/ppermute | solution.py:529
  121.7 0.6 collective-permute-start.22
  122.3 1.5 collective-permute-start.23
  123.8 0.0 collective-permute-done.15.rest_8_
  123.8 0.0 collective-permute-done.16.rest_9_
  123.8 2.7 %collective-permute-done.21.rest_11_ = f32[280,128]{1,0:T(8,128)S(1)} collective-permute-done((f32[280,128]{1,0:T(8,128)S(1)}, f32[280,128]{1,0:T(8,128)S(1)}, u32[]{:S(2)}, u32[]{:S(2)}) %collective-permute-start.21) | collective-permute-done | bytes 143392 | tf_op jit(solution)/shard_map/ppermute | solution.py:529
  126.5 2.8 %collective-permute-done.22.rest_12_ = f32[280,128]{1,0:T(8,128)S(1)} collective-permute-done((f32[280,128]{1,0:T(8,128)S(1)}, f32[280,128]{1,0:T(8,128)S(1)}, u32[]{:S(2)}, u32[]{:S(2)}) %collective-permute-start.22) | collective-permute-done | bytes 143392 | tf_op jit(solution)/shard_map/ppermute | solution.py:529
  129.3 0.0 collective-permute-done.23.rest_13_
  129.4 0.6 copy-done.17
  130.0 0.7 copy-done.18
  130.6 7.4 %update.1 = f32[16,96]{1,0:T(8,128)} custom-call(bf16[8,96,1024]{2,1,0:T(8,128)(2,1)} %get-tuple-element.56.rest_0_, bf16[8,96,1024]{2,1,0:T(8,128)(2,1)} %get-tuple-element.62.rest_1_, bf16[12,96,1024]{2,1,0:T(8,128)(2,1)} %get-tuple-element.67.rest_2_, bf16[8,96,1024]{2,1,0:T(8,128)(2,1)} %get-tuple-element.68.rest_3_, ...), custom_call_target="tpu_custom_call" | custom-call | flops 264241152 | bytes 11010048 | tf_op jit(solution)/shard_map/update/pallas_call | solution.py:539
  138.0 9.3 %all_to_all.5 = f32[8,2,96]{2,1,0:T(2,128)S(1)} all-to-all(f32[8,2,96]{2,1,0:T(2,128)} %bitcast.7), channel_id=1, replica_groups=mesh['sens'=4,'par'=8] {'par'}, dimensions={0} | all-to-all | bytes 12288 | tf_op jit(solution)/shard_map/all_to_all | solution.py:554
  147.3 0.6 reduce_sum.9
  (45 shorter events, 0.3 us)
Async XLA Ops:
  23.1 14.3 %collective-permute-start = (f32[4,224,128]{2,1,0:T(8,128)}, f32[4,224,128]{2,1,0:T(8,128)S(1)}, u32[]{:S(2)}, u32[]{:S(2)}) collective-permute-start(f32[4,224,128]{2,1,0:T(8,128)} %get-tuple-element.48), channel_id=1, source_target_pairs={{0,8},{8,0},{16,24},{24,16},{1,9},{9,1},{17,25},{25,17},{2,10},{10... | collective-permute-start | bytes 1376264 | tf_op jit(solution)/shard_map/ppermute | solution.py:384
  26.1 12.2 %collective-permute-start.1 = (f32[4,224,128]{2,1,0:T(8,128)}, f32[4,224,128]{2,1,0:T(8,128)S(1)}, u32[]{:S(2)}, u32[]{:S(2)}) collective-permute-start(f32[4,224,128]{2,1,0:T(8,128)} %get-tuple-element.50), channel_id=1, source_target_pairs={{0,16},{8,24},{16,0},{24,8},{1,17},{9,25},{17,1},{25,9},{2,18},{10... | collective-permute-start | bytes 1376264 | tf_op jit(solution)/shard_map/ppermute | solution.py:384
  31.8 5.6 %copy-start.6 = (f32[4,224,128]{2,1,0:T(8,128)S(1)}, f32[4,224,128]{2,1,0:T(8,128)}, u32[]{:S(2)}) copy-start(f32[4,224,128]{2,1,0:T(8,128)} %get-tuple-element.47) | copy-start | bytes 1376260
  31.8 6.5 %copy-start.5 = (f32[4,224,128]{2,1,0:T(8,128)S(1)}, f32[4,224,128]{2,1,0:T(8,128)}, u32[]{:S(2)}) copy-start(f32[4,224,128]{2,1,0:T(8,128)} %get-tuple-element.49) | copy-start | bytes 1376260
  38.4 7.7 %collective-permute-start.2 = (f32[2,224,128]{2,1,0:T(8,128)S(1)}, f32[2,224,128]{2,1,0:T(8,128)S(1)}, u32[]{:S(2)}, u32[]{:S(2)}) collective-permute-start(f32[2,224,128]{2,1,0:T(8,128)S(1)} %slice.37), channel_id=1, source_target_pairs={{0,16},{8,24},{16,0},{24,8},{1,17},{9,25},{17,1},{25,9},{2,18},{10... | collective-permute-start | bytes 688136 | tf_op jit(solution)/shard_map/ppermute | solution.py:389
  40.0 6.1 %collective-permute-start.3 = (f32[2,224,128]{2,1,0:T(8,128)S(1)}, f32[2,224,128]{2,1,0:T(8,128)S(1)}, u32[]{:S(2)}, u32[]{:S(2)}) collective-permute-start(f32[2,224,128]{2,1,0:T(8,128)S(1)} %slice.39), channel_id=1, source_target_pairs={{0,8},{8,0},{16,24},{24,16},{1,9},{9,1},{17,25},{25,17},{2,10},{10... | collective-permute-start | bytes 688136 | tf_op jit(solution)/shard_map/ppermute | solution.py:389
  46.1 17.8 %copy-start = (f32[2,224,128]{2,1,0:T(8,128)}, f32[2,224,128]{2,1,0:T(8,128)S(1)}, u32[]{:S(2)}) copy-start(f32[2,224,128]{2,1,0:T(8,128)S(1)} %slice_add_fusion.1.rest_0_) | copy-start | bytes 688132
  46.1 17.8 %copy-start.1 = (f32[2,224,128]{2,1,0:T(8,128)}, f32[2,224,128]{2,1,0:T(8,128)S(1)}, u32[]{:S(2)}) copy-start(f32[2,224,128]{2,1,0:T(8,128)S(1)} %slice_add_fusion.rest_4_) | copy-start | bytes 688132
  46.1 8.6 %collective-permute-start.4 = (f32[2,224,128]{2,1,0:T(8,128)S(1)}, f32[2,224,128]{2,1,0:T(8,128)S(1)}, u32[]{:S(2)}, u32[]{:S(2)}) collective-permute-start(f32[2,224,128]{2,1,0:T(8,128)S(1)} %slice_add_fusion.rest_4_), channel_id=1, source_target_pairs={{0,8},{8,0},{16,24},{24,16},{1,9},{9,1},{17,25},{25,17},{2,10},{10... | collective-permute-start | bytes 688136 | tf_op jit(solution)/shard_map/ppermute | solution.py:393
  47.7 8.5 %collective-permute-start.6 = (f32[2,224,128]{2,1,0:T(8,128)S(1)}, f32[2,224,128]{2,1,0:T(8,128)S(1)}, u32[]{:S(2)}, u32[]{:S(2)}) collective-permute-start(f32[2,224,128]{2,1,0:T(8,128)S(1)} %slice_add_fusion.1.rest_0_), channel_id=1, source_target_pairs={{0,16},{8,24},{16,0},{24,8},{1,17},{9,25},{17,1},{25,9},{2,18},{10... | collective-permute-start | bytes 688136 | tf_op jit(solution)/shard_map/ppermute | solution.py:393
  48.2 15.7 %collective-permute-start.7 = (f32[2,224,128]{2,1,0:T(8,128)S(1)}, f32[2,224,128]{2,1,0:T(8,128)S(1)}, u32[]{:S(2)}, u32[]{:S(2)}) collective-permute-start(f32[2,224,128]{2,1,0:T(8,128)S(1)} %slice_add_fusion.1.rest_0_), channel_id=1, source_target_pairs={{0,8},{8,0},{16,24},{24,16},{1,9},{9,1},{17,25},{25,17},{2,10},{10... | collective-permute-start | bytes 688136 | tf_op jit(solution)/shard_map/ppermute | solution.py:394
  48.7 15.3 %collective-permute-start.9 = (f32[2,224,128]{2,1,0:T(8,128)S(1)}, f32[2,224,128]{2,1,0:T(8,128)S(1)}, u32[]{:S(2)}, u32[]{:S(2)}) collective-permute-start(f32[2,224,128]{2,1,0:T(8,128)S(1)} %slice_add_fusion.rest_4_), channel_id=1, source_target_pairs={{0,16},{8,24},{16,0},{24,8},{1,17},{9,25},{17,1},{25,9},{2,18},{10... | collective-permute-start | bytes 688136 | tf_op jit(solution)/shard_map/ppermute | solution.py:394
  54.7 9.2 %copy-start.7 = (f32[2,224,128]{2,1,0:T(8,128)}, f32[2,224,128]{2,1,0:T(8,128)S(1)}, u32[]{:S(2)}) copy-start(f32[2,224,128]{2,1,0:T(8,128)S(1)} %collective-permute-done.4.rest_5_) | copy-start | bytes 688132
  54.7 9.2 %collective-permute-start.5 = (f32[2,224,128]{2,1,0:T(8,128)S(1)}, f32[2,224,128]{2,1,0:T(8,128)S(1)}, u32[]{:S(2)}, u32[]{:S(2)}) collective-permute-start(f32[2,224,128]{2,1,0:T(8,128)S(1)} %collective-permute-done.4.rest_5_), channel_id=1, source_target_pairs={{0,16},{8,24},{16,0},{24,8},{1,17},{9,25},{17,1},{25,9},{2,18},{10... | collective-permute-start | bytes 688136 | tf_op jit(solution)/shard_map/ppermute | solution.py:395
  56.2 7.7 %copy-start.8 = (f32[2,224,128]{2,1,0:T(8,128)}, f32[2,224,128]{2,1,0:T(8,128)S(1)}, u32[]{:S(2)}) copy-start(f32[2,224,128]{2,1,0:T(8,128)S(1)} %collective-permute-done.6.rest_1_) | copy-start | bytes 688132
  56.2 7.8 %collective-permute-start.8 = (f32[2,224,128]{2,1,0:T(8,128)S(1)}, f32[2,224,128]{2,1,0:T(8,128)S(1)}, u32[]{:S(2)}, u32[]{:S(2)}) collective-permute-start(f32[2,224,128]{2,1,0:T(8,128)S(1)} %collective-permute-done.6.rest_1_), channel_id=1, source_target_pairs={{0,8},{8,0},{16,24},{24,16},{1,9},{9,1},{17,25},{25,17},{2,10},{10... | collective-permute-start | bytes 688136 | tf_op jit(solution)/shard_map/ppermute | solution.py:395
  63.9 0.7 copy-start.11
  64.0 0.8 copy-start.9
  64.0 0.8 copy-start.10
  64.0 0.9 copy-start.12
  88.2 8.1 %copy-start.2 = (f32[1120,128]{1,0:T(8,128)S(1)}, f32[1120,128]{1,0:T(8,128)}, u32[]{:S(2)}) copy-start(f32[1120,128]{1,0:T(8,128)} %get-tuple-element.79) | copy-start | bytes 1720324
  88.2 2.3 %collective-permute-start.10 = (f32[1120,128]{1,0:T(8,128)}, f32[1120,128]{1,0:T(8,128)S(1)}, u32[]{:S(2)}, u32[]{:S(2)}) collective-permute-start(f32[1120,128]{1,0:T(8,128)} %get-tuple-element.78), channel_id=1, source_target_pairs={{0,1},{1,0},{2,3},{3,2},{4,5},{5,4},{6,7},{7,6},{8,9},{9,8},{10,11... | collective-permute-start | bytes 1720328 | tf_op jit(solution)/shard_map/ppermute | solution.py:531
  88.3 8.0 %collective-permute-start.17 = (f32[1120,128]{1,0:T(8,128)}, f32[1120,128]{1,0:T(8,128)S(1)}, u32[]{:S(2)}, u32[]{:S(2)}) collective-permute-start(f32[1120,128]{1,0:T(8,128)} %get-tuple-element.80), channel_id=1, source_target_pairs={{0,1},{1,0},{2,3},{3,2},{4,5},{5,4},{6,7},{7,6},{8,9},{9,8},{10,11... | collective-permute-start | bytes 1720328 | tf_op jit(solution)/shard_map/ppermute | solution.py:532
  91.6 8.3 %collective-permute-start.13 = (f32[280,128]{1,0:T(8,128)S(1)}, f32[280,128]{1,0:T(8,128)S(1)}, u32[]{:S(2)}, u32[]{:S(2)}) collective-permute-start(f32[280,128]{1,0:T(8,128)S(1)} %get-tuple-element.85), channel_id=1, source_target_pairs={{0,6},{1,7},{2,0},{3,1},{4,2},{5,3},{6,4},{7,5},{8,14},{9,15},{10,... | collective-permute-start | bytes 430088 | tf_op jit(solution)/shard_map/ppermute | solution.py:526
  95.3 8.5 %collective-permute-start.11 = (f32[280,128]{1,0:T(8,128)S(1)}, f32[280,128]{1,0:T(8,128)S(1)}, u32[]{:S(2)}, u32[]{:S(2)}) collective-permute-start(f32[280,128]{1,0:T(8,128)S(1)} %get-tuple-element.86), channel_id=1, source_target_pairs={{0,2},{1,3},{2,4},{3,5},{4,6},{5,7},{6,0},{7,1},{8,10},{9,11},{10,... | collective-permute-start | bytes 430088 | tf_op jit(solution)/shard_map/ppermute | solution.py:526
  95.3 14.7 %collective-permute-start.12 = (f32[280,128]{1,0:T(8,128)S(1)}, f32[280,128]{1,0:T(8,128)S(1)}, u32[]{:S(2)}, u32[]{:S(2)}) collective-permute-start(f32[280,128]{1,0:T(8,128)S(1)} %get-tuple-element.84), channel_id=1, source_target_pairs={{0,4},{1,5},{2,6},{3,7},{4,0},{5,1},{6,2},{7,3},{8,12},{9,13},{10,... | collective-permute-start | bytes 430088 | tf_op jit(solution)/shard_map/ppermute | solution.py:526
  96.4 15.7 %collective-permute-start.20 = (f32[280,128]{1,0:T(8,128)S(1)}, f32[280,128]{1,0:T(8,128)S(1)}, u32[]{:S(2)}, u32[]{:S(2)}) collective-permute-start(f32[280,128]{1,0:T(8,128)S(1)} %get-tuple-element.82), channel_id=1, source_target_pairs={{0,6},{1,7},{2,0},{3,1},{4,2},{5,3},{6,4},{7,5},{8,14},{9,15},{10,... | collective-permute-start | bytes 430088 | tf_op jit(solution)/shard_map/ppermute | solution.py:526
  99.3 14.3 %collective-permute-start.18 = (f32[280,128]{1,0:T(8,128)S(1)}, f32[280,128]{1,0:T(8,128)S(1)}, u32[]{:S(2)}, u32[]{:S(2)}) collective-permute-start(f32[280,128]{1,0:T(8,128)S(1)} %get-tuple-element.83), channel_id=1, source_target_pairs={{0,2},{1,3},{2,4},{3,5},{4,6},{5,7},{6,0},{7,1},{8,10},{9,11},{10,... | collective-permute-start | bytes 430088 | tf_op jit(solution)/shard_map/ppermute | solution.py:526
  99.9 20.3 %collective-permute-start.19 = (f32[280,128]{1,0:T(8,128)S(1)}, f32[280,128]{1,0:T(8,128)S(1)}, u32[]{:S(2)}, u32[]{:S(2)}) collective-permute-start(f32[280,128]{1,0:T(8,128)S(1)} %get-tuple-element.81), channel_id=1, source_target_pairs={{0,4},{1,5},{2,6},{3,7},{4,0},{5,1},{6,2},{7,3},{8,12},{9,13},{10,... | collective-permute-start | bytes 430088 | tf_op jit(solution)/shard_map/ppermute | solution.py:526
  110.0 19.3 %copy-start.3 = (f32[280,128]{1,0:T(8,128)}, f32[280,128]{1,0:T(8,128)S(1)}, u32[]{:S(2)}) copy-start(f32[280,128]{1,0:T(8,128)S(1)} %slice_add_fusion.3.rest_6_) | copy-start | bytes 430084
  110.0 12.3 %collective-permute-start.14 = (f32[280,128]{1,0:T(8,128)S(1)}, f32[280,128]{1,0:T(8,128)S(1)}, u32[]{:S(2)}, u32[]{:S(2)}) collective-permute-start(f32[280,128]{1,0:T(8,128)S(1)} %slice_add_fusion.3.rest_6_), channel_id=1, source_target_pairs={{0,8},{8,0},{16,24},{24,16},{1,9},{9,1},{17,25},{25,17},{2,10},{10... | collective-permute-start | bytes 430088 | tf_op jit(solution)/shard_map/ppermute | solution.py:529
  111.5 12.3 %collective-permute-start.15 = (f32[280,128]{1,0:T(8,128)S(1)}, f32[280,128]{1,0:T(8,128)S(1)}, u32[]{:S(2)}, u32[]{:S(2)}) collective-permute-start(f32[280,128]{1,0:T(8,128)S(1)} %slice_add_fusion.3.rest_6_), channel_id=1, source_target_pairs={{0,16},{8,24},{16,0},{24,8},{1,17},{9,25},{17,1},{25,9},{2,18},{10... | collective-permute-start | bytes 430088 | tf_op jit(solution)/shard_map/ppermute | solution.py:529
  112.1 11.7 %collective-permute-start.16 = (f32[280,128]{1,0:T(8,128)S(1)}, f32[280,128]{1,0:T(8,128)S(1)}, u32[]{:S(2)}, u32[]{:S(2)}) collective-permute-start(f32[280,128]{1,0:T(8,128)S(1)} %slice_add_fusion.3.rest_6_), channel_id=1, source_target_pairs={{0,24},{8,16},{16,8},{24,0},{1,25},{9,17},{17,9},{25,1},{2,26},{10... | collective-permute-start | bytes 430088 | tf_op jit(solution)/shard_map/ppermute | solution.py:529
  120.2 9.1 %copy-start.4 = (f32[280,128]{1,0:T(8,128)}, f32[280,128]{1,0:T(8,128)S(1)}, u32[]{:S(2)}) copy-start(f32[280,128]{1,0:T(8,128)S(1)} %slice_add_fusion.2.rest_10_) | copy-start | bytes 430084
  120.2 6.3 %collective-permute-start.21 = (f32[280,128]{1,0:T(8,128)S(1)}, f32[280,128]{1,0:T(8,128)S(1)}, u32[]{:S(2)}, u32[]{:S(2)}) collective-permute-start(f32[280,128]{1,0:T(8,128)S(1)} %slice_add_fusion.2.rest_10_), channel_id=1, source_target_pairs={{0,8},{8,0},{16,24},{24,16},{1,9},{9,1},{17,25},{25,17},{2,10},{10... | collective-permute-start | bytes 430088 | tf_op jit(solution)/shard_map/ppermute | solution.py:529
  121.7 7.6 %collective-permute-start.22 = (f32[280,128]{1,0:T(8,128)S(1)}, f32[280,128]{1,0:T(8,128)S(1)}, u32[]{:S(2)}, u32[]{:S(2)}) collective-permute-start(f32[280,128]{1,0:T(8,128)S(1)} %slice_add_fusion.2.rest_10_), channel_id=1, source_target_pairs={{0,16},{8,24},{16,0},{24,8},{1,17},{9,25},{17,1},{25,9},{2,18},{10... | collective-permute-start | bytes 430088 | tf_op jit(solution)/shard_map/ppermute | solution.py:529
  122.3 7.0 %copy-start.13 = (f32[280,128]{1,0:T(8,128)}, f32[280,128]{1,0:T(8,128)S(1)}, u32[]{:S(2)}) copy-start(f32[280,128]{1,0:T(8,128)S(1)} %collective-permute-done.14.rest_7_) | copy-start | bytes 430084
  122.3 7.0 %collective-permute-start.23 = (f32[280,128]{1,0:T(8,128)S(1)}, f32[280,128]{1,0:T(8,128)S(1)}, u32[]{:S(2)}, u32[]{:S(2)}) collective-permute-start(f32[280,128]{1,0:T(8,128)S(1)} %slice_add_fusion.2.rest_10_), channel_id=1, source_target_pairs={{0,24},{8,16},{16,8},{24,0},{1,25},{9,17},{17,9},{25,1},{2,26},{10... | collective-permute-start | bytes 430088 | tf_op jit(solution)/shard_map/ppermute | solution.py:529
  123.8 5.6 %copy-start.14 = (f32[280,128]{1,0:T(8,128)}, f32[280,128]{1,0:T(8,128)S(1)}, u32[]{:S(2)}) copy-start(f32[280,128]{1,0:T(8,128)S(1)} %collective-permute-done.15.rest_8_) | copy-start | bytes 430084
  123.8 5.6 %copy-start.15 = (f32[280,128]{1,0:T(8,128)}, f32[280,128]{1,0:T(8,128)S(1)}, u32[]{:S(2)}) copy-start(f32[280,128]{1,0:T(8,128)S(1)} %collective-permute-done.16.rest_9_) | copy-start | bytes 430084
  126.5 2.9 %copy-start.16 = (f32[280,128]{1,0:T(8,128)}, f32[280,128]{1,0:T(8,128)S(1)}, u32[]{:S(2)}) copy-start(f32[280,128]{1,0:T(8,128)S(1)} %collective-permute-done.21.rest_11_) | copy-start | bytes 430084
  129.3 0.6 copy-start.17
  129.9 0.7 copy-start.18
